TPU v7x, 32 devices: a whole 2x2x4 slice. The times are simulated.
32 devices in a mesh: dp: 16 (over z, y, core), mp: 2 (over x).
Axes of the slice: x: 2, y: 2, z: 4, core: 2. Of those that a mesh axis runs over, the one named last changes fastest.
Arguments:
- hidden_state_rows: bfloat16 [8192, 8192], P('dp', 'mp'), may hold values from -6 to 6
- request_adapter_index: int32 [8192], P('dp'), may hold values from 0 to 15, as said below
- adapter_store_slot: int32 [16], replicated, may hold values from 0 to 15, as said below
- down_weight_store: bfloat16 [16, 4, 8192, 64], P('dp', None, 'mp'), may hold values from -0.0625 to 0.0625
- up_weight_store: bfloat16 [16, 4, 64, 8192], P('dp', None, None, 'mp'), may hold values from -0.75 to 0.75
Outputs:
- adapted_rows: bfloat16 [8192, 8192], P('dp', 'mp')
Inputs may be any that keep to these rules, and one draw needn't show every extreme that they name: `request_adapter_index`: among the 512 requests of one index of dp no adapter is named more than 64 times; in every draw one adapter is named exactly 64 times by every index of dp. `adapter_store_slot`: each slot is used by exactly one adapter; slot s lies in store shard s.
All inputs are finite; a program needn't handle non-finite values.
Results may differ from a plain program's by a relative error of at most 0.0075.
Values may be sent and summed in bfloat16 or wider, within the bound.
No kernel may reach another device: no remote copies, remote signals or barrier semaphores. Data moves between devices by JAX's collectives and lax.ppermute only.
A program may use at most 64 MiB of HBM per device.

v0:
```python
import jax
import jax.numpy as jnp
from jax import lax
from jax.sharding import PartitionSpec as P

MODEL_WIDTH = 8192


epsilon = 1e-05


def split_layer(current, down_a, up_b):
    widened = current.astype(jnp.float32)
    partial_value = jnp.einsum(
        "sjmd,jdr->sjmr", current, down_a, preferred_element_type=jnp.float32
    )
    squares = jnp.sum(widened * widened, axis=-1, keepdims=True)
    summed, sq_total = lax.psum((partial_value, squares), "mp")
    reduced = (summed * lax.rsqrt(sq_total / MODEL_WIDTH + epsilon)).astype(jnp.bfloat16)
    update = jnp.einsum("sjmr,jrd->sjmd", reduced, up_b, preferred_element_type=jnp.float32)
    return (widened + update).astype(jnp.bfloat16)


def local(
    hidden_state_rows, request_adapter_index, adapter_store_slot, down_weight_store, up_weight_store
):
    tok_count = hidden_state_rows.shape[0]
    width_dev = hidden_state_rows.shape[1]
    owners = lax.axis_size("dp")
    adapters_per_replica = down_weight_store.shape[0]
    layer_stack = down_weight_store.shape[1]
    adapters = adapter_store_slot.shape[0]
    tile_rows = 2 * tok_count // (owners * adapters_per_replica)
    adapter_ids = jnp.arange(adapters, dtype=jnp.int32)
    matches = request_adapter_index[:, None] == adapter_ids[None, :]
    slot_tok = jnp.sum(jnp.where(matches, adapter_store_slot[None, :], 0), axis=1)
    request_ids = jnp.arange(tok_count, dtype=jnp.int32)
    earlier = (request_adapter_index[:, None] == request_adapter_index[None, :]) & (
        request_ids[:, None] > request_ids[None, :]
    )
    position = jnp.sum(earlier.astype(jnp.int32), axis=1)
    target = slot_tok * tile_rows + position
    outgoing = (
        jnp.zeros((adapters * tile_rows, width_dev), hidden_state_rows.dtype)
        .at[target]
        .set(hidden_state_rows)
    )
    arrived = lax.all_to_all(
        outgoing.reshape(owners, adapters_per_replica * tile_rows, width_dev),
        "dp",
        split_axis=0,
        concat_axis=0,
        tiled=True,
    )
    current = arrived.reshape(owners, adapters_per_replica, tile_rows, width_dev)
    for layer_index in range(layer_stack):
        current = split_layer(
            current, down_weight_store[:, layer_index], up_weight_store[:, layer_index]
        )
    returned = lax.all_to_all(
        current.reshape(owners, adapters_per_replica * tile_rows, width_dev),
        "dp",
        split_axis=0,
        concat_axis=0,
        tiled=True,
    )
    return returned.reshape(adapters * tile_rows, width_dev)[target]


def solution(mesh):
    return jax.shard_map(
        local,
        mesh=mesh,
        in_specs=(
            P("dp", "mp"),
            P("dp"),
            P(),
            P("dp", None, "mp", None),
            P("dp", None, None, "mp"),
        ),
        out_specs=P("dp", "mp"),
        check_vma=False,
    )
```

profile of v0, /device:TPU:16, one launch (start us, length us, event | category | flops | bytes accessed | tf_op | source)
XLA Modules:
  0.0 586.0 jit_solution(87176154849966605)
XLA Ops:
  6.5 0.0 all-reduce.5.cloned.1.call-start
  6.5 1.0 convert_reduce_fusion
  7.5 0.8 select_reduce_fusion
  8.3 12.4 %scatter_custom_fusion = bf16[1024,4096]{1,0:T(8,128)(2,1)} fusion(s32[512]{0:T(512)S(1)} %bitcast.156, bf16[512,4096]{1,0:T(8,128)(2,1)} %param.5, bf16[]{:T(256)} %constant.7.clone.1), kind=kCustom, calls=%fused_computation.26 | custom fusion | bytes 8389120 | tf_op jit(solution)/shard_map/scatter | solution.py:46
  20.8 188.9 %all_to_all.10 = bf16[16,64,4096]{2,1,0:T(8,128)(2,1)S(1)} all-to-all(bf16[16,64,4096]{2,1,0:T(8,128)(2,1)} %bitcast.154), channel_id=1, replica_groups=mesh['dp'=16,'mp'=2] {'dp'}, dimensions={0} | all-to-all | bytes 16777216 | tf_op jit(solution)/shard_map/all_to_all | solution.py:48
  209.7 0.0 copy-start
  209.7 3.2 copy-done
  212.9 0.0 copy-start.2
  212.9 4.3 convolution_bitcast_fusion
  217.2 0.0 all-reduce.5.cloned.1.call-update
  217.3 0.0 all-reduce.7.cloned.1.call-start
  217.3 5.1 fusion.2
  222.4 5.1 psum.57
  227.5 18.6 %all-reduce.5.cloned.1.call-done = f32[16,1,64,64]{3,2,0,1:T(8,128)} async-done(((f32[16,1,64,64]{3,2,0,1:T(8,128)}), f32[16,1,64,64]{3,2,0,1:T(8,128)}) %all-reduce.5.cloned.1.call-update) | async-done | bytes 262160 | tf_op jit(solution)/shard_map/psum | solution.py:18
  246.1 0.0 copy-done.2
  246.1 5.4 fusion.3
  251.6 0.0 copy-start.3
  251.6 3.2 copy-done.3
  254.8 4.2 fusion.18
  259.0 0.0 all-reduce.7.cloned.1.call-update
  259.0 0.0 all-reduce.9.cloned.1.call-start
  259.0 5.0 psum.59
  264.1 23.7 %all-reduce.7.cloned.1.call-done = f32[16,1,64,64]{3,2,0,1:T(8,128)} async-done(((f32[16,1,64,64]{3,2,0,1:T(8,128)}), f32[16,1,64,64]{3,2,0,1:T(8,128)}) %all-reduce.7.cloned.1.call-update) | async-done | bytes 262160 | tf_op jit(solution)/shard_map/psum | solution.py:18
  287.7 5.4 fusion.5
  293.2 0.0 copy-start.4
  293.2 3.2 copy-done.4
  296.4 4.1 fusion.21
  300.5 0.0 all-reduce.9.cloned.1.call-update
  300.6 0.0 all-reduce.11.cloned.1.call-start
  300.6 5.2 psum.61
  305.9 23.5 %all-reduce.9.cloned.1.call-done = f32[16,1,64,64]{3,2,0,1:T(8,128)} async-done(((f32[16,1,64,64]{3,2,0,1:T(8,128)}), f32[16,1,64,64]{3,2,0,1:T(8,128)}) %all-reduce.9.cloned.1.call-update) | async-done | bytes 262160 | tf_op jit(solution)/shard_map/psum | solution.py:18
  329.3 5.4 fusion.7
  334.8 0.0 copy-start.1
  334.8 3.2 copy-done.1
  338.0 4.2 fusion.24
  342.1 0.0 all-reduce.11.cloned.1.call-update
  342.1 5.0 psum.63
  347.2 23.7 %all-reduce.11.cloned.1.call-done = f32[16,1,64,64]{3,2,0,1:T(8,128)} async-done(((f32[16,1,64,64]{3,2,0,1:T(8,128)}), f32[16,1,64,64]{3,2,0,1:T(8,128)}) %all-reduce.11.cloned.1.call-update) | async-done | bytes 262160 | tf_op jit(solution)/shard_map/psum | solution.py:18
  370.9 6.9 %fusion.15 = bf16[16,64,4096]{2,1,0:T(8,128)(2,1)} fusion(bf16[16,1,64,4096]{3,2,0,1:T(8,128)(2,1)} %copy-done.1, bf16[1,4,64,4096]{3,2,1,0:T(8,128)(2,1)S(1)} %copy-done.2, f32[16,1,64,64]{3,2,0,1:T(8,128)} %all-reduce.11.cloned.1.call-done, f32[16,64]{1,0:T(8,128)S(1)} %rsqrt_bitcast_fusion), kind=kOutput, calls=%fused_computation.25 | convolution fusion | flops 549584896 | bytes 17571840 | tf_op jit(solution)/shard_map/sjmr,jrd->sjmd/dot_general | solution.py:20
  377.8 6.0 %all-to-all-start.1 = ((bf16[16,64,4096]{2,1,0:T(8,128)(2,1)}), bf16[16,64,4096]{2,1,0:T(8,128)(2,1)}, u32[]{:S(2)}, u32[]{:S(2)}) async-start(bf16[16,64,4096]{2,1,0:T(8,128)(2,1)} %fusion.15), calls=%async_computation.1 | async-start | bytes 16777216 | tf_op jit(solution)/shard_map/all_to_all | solution.py:60
  383.8 182.6 %all-to-all-done.1 = bf16[16,64,4096]{2,1,0:T(8,128)(2,1)} async-done(((bf16[16,64,4096]{2,1,0:T(8,128)(2,1)}), bf16[16,64,4096]{2,1,0:T(8,128)(2,1)}, u32[]{:S(2)}, u32[]{:S(2)}) %all-to-all-start.1) | async-done | bytes 8388640 | tf_op jit(solution)/shard_map/all_to_all | solution.py:60
  566.4 13.0 %gather_fusion = bf16[512,4096]{1,0:T(8,128)(2,1)} fusion(bf16[1024,4096]{1,0:T(8,128)(2,1)} %bitcast.60, s32[1024]{0:T(1024)S(1)} %pad_clamp_fusion), kind=kCustom, calls=%fused_computation | custom fusion | bytes 8390656 | tf_op jit(solution)/shard_map/gather | solution.py:67
  (7 shorter events, 0.1 us)
Async XLA Ops:
  6.5 239.6 %all-reduce.5.cloned.1.call-start = ((), (), s32[]{:S(2)}) async-start(), calls=%async_computation.2 | async-start | bytes 1048576 | tf_op jit(solution)/shard_map/psum | solution.py:18
  209.7 3.2 copy-start
  212.9 33.2 %copy-start.2 = (bf16[1,4,64,4096]{3,2,1,0:T(8,128)(2,1)S(1)}, bf16[1,4,64,4096]{3,2,1,0:T(8,128)(2,1)}, u32[]{:S(2)}) copy-start(bf16[1,4,64,4096]{3,2,1,0:T(8,128)(2,1)} %param.9) | copy-start | bytes 6291460
  217.3 70.5 %all-reduce.7.cloned.1.call-start = ((), (), s32[]{:S(2)}) async-start(), calls=%async_computation.3 | async-start | bytes 1048576 | tf_op jit(solution)/shard_map/psum | solution.py:18
  251.6 3.2 copy-start.3
  259.0 70.3 %all-reduce.9.cloned.1.call-start = ((), (), s32[]{:S(2)}) async-start(), calls=%async_computation.4 | async-start | bytes 1048576 | tf_op jit(solution)/shard_map/psum | solution.py:18
  293.2 3.2 copy-start.4
  300.6 70.3 %all-reduce.11.cloned.1.call-start = ((), (), s32[]{:S(2)}) async-start(), calls=%async_computation.5 | async-start | bytes 1048576 | tf_op jit(solution)/shard_map/psum | solution.py:18
  334.8 3.2 copy-start.1
  377.8 188.6 %all-to-all-start.1 = ((bf16[16,64,4096]{2,1,0:T(8,128)(2,1)}), bf16[16,64,4096]{2,1,0:T(8,128)(2,1)}, u32[]{:S(2)}, u32[]{:S(2)}) async-start(bf16[16,64,4096]{2,1,0:T(8,128)(2,1)} %fusion.15), calls=%async_computation.1 | async-start | bytes 16777216 | tf_op jit(solution)/shard_map/all_to_all | solution.py:60
Sparse Core Ops, SparseCore 0:
  217.4 28.7 all-reduce.4
  259.1 28.5 all-reduce.6
  300.7 28.5 all-reduce.8
  342.3 28.5 all-reduce.10
where the time goes:
time: 587 us; the launch traced here: 586 us
  waiting for transfers between devices  272 us (46%)
  blocking collectives  209 us (36%)
  matrix products  39.9 us (7%)
  local copies, waits for them, and re-layouts  38.3 us (7%)
  between operations  13.2 us (2%)
  other arithmetic  6.93 us (1%)
  starting transfers between devices  6.17 us (1%)
    all_to_all x1, blocking collectives, local(): lax.all_to_all(outgoing.reshape(owners, adapters_per_replica * tile_rows,...  189 us
    all_to_all x1, waiting for transfers between devices, local(): lax.all_to_all(current.reshape(owners, adapters_per_replica * tile_rows,...  183 us
    psum x4, waiting for transfers between devices, split_layer(): summed, sq_total = lax.psum((partial_value, squares), 'mp')  89.5 us
    dot_general x4, matrix products, split_layer(): jnp.einsum('sjmr,jrd->sjmd', reduced, up_b, preferred_element_type=jnp.fl...  23.2 us
    psum x4, blocking collectives, split_layer(): summed, sq_total = lax.psum((partial_value, squares), 'mp')  20.4 us
    dot_general x4, matrix products, split_layer(): jnp.einsum('sjmd,jdr->sjmr', current, down_a, preferred_element_type=jnp....  16.8 us
    gather x1, local copies, waits for them, and re-layouts, local(): return returned.reshape(adapters * tile_rows, width_dev)[target]  13 us
    unnamed x10, local copies, waits for them, and re-layouts  12.9 us
  transfers between devices with their start and end apart: 5, of which 5 were waited for; matrix products, arithmetic and copies ran while one was open for 1% of the time, Pallas kernels for 0%

commit v1 on v0

v1 whole, which is shorter than its diff:
```python
import jax
import jax.numpy as jnp
from jax import lax
from jax.sharding import PartitionSpec as P

epsilon = 1e-05
F32 = jnp.float32
BF16 = jnp.bfloat16


def sum_mp(value):
    size = lax.axis_size("mp")
    if size == 2:
        return value + lax.ppermute(value, "mp", [(0, 1), (1, 0)])
    return lax.psum(value, "mp")


def one_hot(rows, columns):
    return (rows[:, None] == columns[None, :]).astype(BF16)


def place(hot, values):
    return jnp.dot(hot, values, preferred_element_type=F32).astype(BF16)


def sketch_weights(down, up):
    layers, width, rank = down.shape
    flat_down = jnp.swapaxes(down, 1, 2).reshape(layers * rank, width)
    return jnp.concatenate([flat_down, up.reshape(layers * rank, width)], axis=0)


def against(left, right):
    return lax.dot_general(left, right, (((1,), (1,)), ((), ())), preferred_element_type=F32)


def gram(weights):
    half = weights.shape[0] // 2
    return sum_mp(against(weights[half:], weights))


def exact_dot(low, table):
    high = table.astype(BF16)
    rest = (table - high.astype(F32)).astype(BF16)
    return jnp.dot(low, high, preferred_element_type=F32) + jnp.dot(
        low, rest, preferred_element_type=F32
    )


def low_rank(sketch, squares, table, layers, model_width):
    total = sketch.shape[1] // 2
    rank = total // layers
    lows = []
    for layer in range(layers):
        here = slice(layer * rank, (layer + 1) * rank)
        there = slice(total + layer * rank, total + (layer + 1) * rank)
        projected, overlap = sketch[:, here], sketch[:, there]
        if lows:
            before = jnp.concatenate(lows, axis=1)
            rows = slice(0, layer * rank)
            projected = projected + exact_dot(before, table[rows, here])
            overlap = overlap + exact_dot(before, table[rows, there])
        low = (projected * lax.rsqrt(squares / model_width + epsilon)).astype(BF16)
        lows.append(low)
        step = 2.0 * overlap + exact_dot(low, table[here, there])
        squares = jnp.maximum(
            squares + jnp.sum(low.astype(F32) * step, axis=1, keepdims=True), 0.0
        )
    return jnp.concatenate(lows, axis=1)


def adapt(rows, weights, table, layers, model_width):
    widened = rows.astype(F32)
    squares = jnp.sum(widened * widened, axis=1, keepdims=True)
    sketch = sum_mp(against(rows, weights))
    squares = sum_mp(squares)
    low = low_rank(sketch, squares, table, layers, model_width)
    half = weights.shape[0] // 2
    update = jnp.dot(low, weights[half:], preferred_element_type=F32)
    return (widened + update).astype(BF16)


def local(hidden, request_adapter, store_slot, down_store, up_store):
    count, width = hidden.shape
    owners = lax.axis_size("dp")
    adapters = store_slot.shape[0]
    assert adapters == owners and down_store.shape[0] == 1
    layers = down_store.shape[1]
    model_width = width * lax.axis_size("mp")
    slot_rows = count // adapters
    chunks = 2 if slot_rows % 32 == 0 else 1
    chunk_rows = slot_rows // chunks
    group = 1
    while group * group < owners:
        group *= 2
    planes = owners // group
    me = lax.axis_index("dp")
    my_plane, my_place = me // group, me % group

    adapter_ids = jnp.arange(adapters, dtype=jnp.int32)
    matches = request_adapter[:, None] == adapter_ids[None, :]
    slot = jnp.sum(jnp.where(matches, store_slot[None, :], 0), axis=1)
    request_ids = jnp.arange(count, dtype=jnp.int32)
    earlier = (slot[:, None] == slot[None, :]) & (request_ids[:, None] > request_ids[None, :])
    position = jnp.sum(earlier.astype(jnp.int32), axis=1)
    by_slot = slot[:, None] == adapter_ids[None, :]
    counts = jnp.sum(by_slot.astype(jnp.int32), axis=0)
    excess = lax.psum(jnp.maximum(counts - slot_rows, 0), "dp")

    arrived = []
    targets = []
    for chunk in range(chunks):
        offset = position - chunk * chunk_rows
        target = jnp.where(
            (offset >= 0) & (offset < chunk_rows), slot * chunk_rows + offset, -1
        )
        targets.append(target)
        packed = place(one_hot(jnp.arange(owners * chunk_rows), target), hidden)
        arrived.append(
            lax.all_to_all(
                packed.reshape(owners, chunk_rows, width), "dp", 0, 0, tiled=True
            ).reshape(owners * chunk_rows, width)
        )

    weights = sketch_weights(down_store[0], up_store[0])
    piece_rows = weights.shape[0] // group
    pieces = weights.reshape(group, piece_rows, width)
    spread = []
    for step in range(group):
        piece = lax.dynamic_index_in_dim(pieces, my_place ^ step, 0, keepdims=False)
        if step:
            piece = lax.ppermute(piece, "dp", [(i, i ^ step) for i in range(owners)])
        spread.append(piece)
    chosen = jnp.argmax(excess.reshape(planes, group), axis=1).astype(jnp.int32)
    mine = lax.dynamic_index_in_dim(
        jnp.stack(spread), my_place ^ chosen[my_plane], 0, keepdims=False
    )
    groups = [[p * group + q for q in range(group)] for p in range(planes)]
    plane_weights = lax.all_gather(mine, "dp", axis_index_groups=groups, tiled=True)
    table = gram(weights)
    plane_table = gram(plane_weights)

    plane = slot // group
    is_chosen = slot % group == jnp.sum(
        jnp.where(plane[:, None] == jnp.arange(planes)[None, :], chosen[None, :], 0), axis=1
    )
    over = position >= slot_rows
    over_target = jnp.where(
        over & is_chosen, (plane ^ my_plane) * slot_rows + position - slot_rows, -1
    )
    over_packed = place(one_hot(jnp.arange(planes * slot_rows), over_target), hidden)

    def swap_planes(rows):
        blocks = rows.reshape(planes, slot_rows, width)
        moved = [blocks[0]]
        for step in range(1, planes):
            pairs = [(i, i ^ (step * group)) for i in range(owners)]
            moved.append(lax.ppermute(blocks[step], "dp", pairs))
        return jnp.concatenate(moved, axis=0)

    over_arrived = swap_planes(over_packed)

    returned = []
    for rows in arrived:
        done = adapt(rows, weights, table, layers, model_width)
        returned.append(
            lax.all_to_all(
                done.reshape(owners, chunk_rows, width), "dp", 0, 0, tiled=True
            ).reshape(owners * chunk_rows, width)
        )
    returned.append(
        swap_planes(adapt(over_arrived, plane_weights, plane_table, layers, model_width))
    )
    targets.append(over_target)
    result = jnp.zeros((count, width), F32)
    for rows, target in zip(returned, targets):
        hot = one_hot(target, jnp.arange(rows.shape[0]))
        result = result + jnp.dot(hot, rows, preferred_element_type=F32)
    result = result.astype(BF16)

    served = jnp.sum(
        jnp.where(
            adapter_ids[:, None] // group == jnp.arange(planes)[None, :], chosen[None, :], 0
        ),
        axis=1,
    ) == adapter_ids % group
    waiting = jnp.where(served, 0, excess) > 0
    order = jnp.cumsum(waiting.astype(jnp.int32)) - 1
    rounds = jnp.sum(waiting.astype(jnp.int32))

    def one_round(state):
        at, filled = state
        owner = jnp.sum(jnp.where(waiting & (order == at), adapter_ids, 0))
        own = jnp.where(me == owner, weights, jnp.zeros_like(weights))
        round_weights = lax.psum(own, "dp")
        target = jnp.where(over & (slot == owner), position - slot_rows, -1)
        rows = place(one_hot(jnp.arange(slot_rows), target), hidden)
        done = adapt(rows, round_weights, gram(round_weights), layers, model_width)
        back = place(one_hot(target, jnp.arange(slot_rows)), done)
        return at + 1, jnp.where((target >= 0)[:, None], back, filled)

    _, result = lax.while_loop(lambda state: state[0] < rounds, one_round, (0, result))
    return result


def solution(mesh):
    return jax.shard_map(
        local,
        mesh=mesh,
        in_specs=(
            P("dp", "mp"),
            P("dp"),
            P(),
            P("dp", None, "mp", None),
            P("dp", None, None, "mp"),
        ),
        out_specs=P("dp", "mp"),
        check_vma=False,
    )
```

time: 587 us -> 330 us (0.56)
  blocking collectives: 209 us -> 10.1 us
  waiting for transfers between devices: 272 us -> 183 us
  starting transfers between devices: 6.17 us -> 40.4 us
  local copies, waits for them, and re-layouts: 38.3 us -> 7.22 us
  matrix products: 39.9 us -> 55.4 us
  other arithmetic: 6.93 us -> 16.9 us
    all_to_all x1 -> x0, blocking collectives: 189 us -> none  [local(): lax.all_to_all(outgoing.reshape(owners, adapters_per_replica * tile_rows,...]
    psum x4 -> x0, waiting for transfers between devices: 89.5 us -> none  [split_layer(): summed, sq_total = lax.psum((partial_value, squares), 'mp')]
    all_to_all x1 -> x4, waiting for transfers between devices: 183 us -> 99.3 us  [the longest x2 61.4 us: local(): lax.all_to_all(done.reshape(owners, chunk_rows, width), 'dp', 0, 0, tiled...]
    ppermute x0 -> x17, waiting for transfers between devices: none -> 82.3 us  [the longest x6 68.5 us: swap_planes(): moved.append(lax.ppermute(blocks[step], 'dp', pairs))]
    all_to_all x1 -> x4, starting transfers between devices: 6.05 us -> 24 us  [the longest x2 12.3 us: local(): lax.all_to_all(done.reshape(owners, chunk_rows, width), 'dp', 0, 0, tiled...]
    ppermute x0 -> x17, starting transfers between devices: none -> 16.2 us  [the longest x8 9.2 us: sum_mp(): return value + lax.ppermute(value, 'mp', [(0, 1), (1, 0)])]
    dot_general x8 -> x62, matrix products: 39.9 us -> 55.4 us  [the longest x5 16.6 us: against(): lax.dot_general(left, right, (((1,), (1,)), ((), ())), preferred_element_...]
    gather x1 -> x0, local copies, waits for them, and re-layouts: 13 us -> none  [local(): return returned.reshape(adapters * tile_rows, width_dev)[target]]
  transfers between devices with their start and end apart: 5 -> 22, of which waited for: 5 -> 11; matrix products, arithmetic and copies ran while one was open for 1% -> 20% of each run, Pallas kernels for 0% -> 0%
where the time goes in v1:
time: 330 us; the launch traced here: 329 us
  waiting for transfers between devices  183 us (55%)
  matrix products  55.4 us (17%)
  starting transfers between devices  40.4 us (12%)
  other arithmetic  16.9 us (5%)
  between operations  14.5 us (4%)
  blocking collectives  10.1 us (3%)
  local copies, waits for them, and re-layouts  7.22 us (2%)
    ppermute x6, waiting for transfers between devices, swap_planes(): moved.append(lax.ppermute(blocks[step], 'dp', pairs))  68.5 us
    all_to_all x2, waiting for transfers between devices, local(): lax.all_to_all(done.reshape(owners, chunk_rows, width), 'dp', 0, 0, tiled...  61.4 us
    all_to_all x2, waiting for transfers between devices, local(): lax.all_to_all(packed.reshape(owners, chunk_rows, width), 'dp', 0, 0, til...  37.9 us
    dot_general x5, matrix products, against(): lax.dot_general(left, right, (((1,), (1,)), ((), ())), preferred_element_...  16.6 us
    ppermute x8, waiting for transfers between devices, sum_mp(): return value + lax.ppermute(value, 'mp', [(0, 1), (1, 0)])  13.8 us
    all_to_all x2, starting transfers between devices, local(): lax.all_to_all(done.reshape(owners, chunk_rows, width), 'dp', 0, 0, tiled...  12.3 us
    all_to_all x2, starting transfers between devices, local(): lax.all_to_all(packed.reshape(owners, chunk_rows, width), 'dp', 0, 0, til...  11.7 us
    dot_general x3, matrix products, place(): return jnp.dot(hot, values, preferred_element_type=F32).astype(BF16)  10.4 us
  transfers between devices with their start and end apart: 22, of which 11 were waited for; matrix products, arithmetic and copies ran while one was open for 20% of the time, Pallas kernels for 0%

profile of v1, /device:TPU:16, one launch (start us, length us, event | category | flops | bytes accessed | tf_op | source)
XLA Modules:
  0.0 328.6 jit_solution(6331623416245850650)
XLA Ops:
  7.7 10.1 %psum.17 = s32[16]{0:T(128)S(1)} all-reduce(s32[16]{0:T(128)S(1)} %add_maximum_fusion.4), channel_id=1, replica_groups=mesh['dp'=16,'mp'=2] {'dp'}, use_global_device_ids=true, to_apply=%region_11.12 | all-reduce | flops 16 | bytes 128 | tf_op jit(solution)/shard_map/psum | solution.py:107
  18.6 4.8 %convolution_convert_fusion.2 = bf16[256,4096]{1,0:T(8,128)(2,1)} fusion(bf16[512,4096]{1,0:T(8,128)(2,1)} %param.7, s32[512]{0:T(512)S(1)} %get-tuple-element.238), kind=kOutput, calls=%fused_computation.107 | convolution fusion | flops 1074921472 | bytes 6293504 | tf_op jit(solution)/shard_map/dot_general | solution.py:23
  23.4 6.9 %all-to-all-start.2 = ((bf16[16,16,4096]{2,1,0:T(8,128)(2,1)}), bf16[16,16,4096]{2,1,0:T(8,128)(2,1)}, u32[]{:S(2)}, u32[]{:S(2)}) async-start(bf16[16,16,4096]{2,1,0:T(8,128)(2,1)} %bitcast.247), calls=%async_computation.2 | async-start | bytes 4194304 | tf_op jit(solution)/shard_map/all_to_all | solution.py:119
  30.3 1.9 pad_maximum_fusion.6
  32.3 1.7 dynamic-slice_bitcast_fusion
  34.0 1.9 copy-done.1
  36.1 1.5 collective-permute-start.12
  37.8 2.6 convolution_convert_fusion.3
  40.3 37.9 %all-to-all-done.2 = bf16[16,16,4096]{2,1,0:T(8,128)(2,1)} async-done(((bf16[16,16,4096]{2,1,0:T(8,128)(2,1)}), bf16[16,16,4096]{2,1,0:T(8,128)(2,1)}, u32[]{:S(2)}, u32[]{:S(2)}) %all-to-all-start.2) | async-done | bytes 2097184 | tf_op jit(solution)/shard_map/all_to_all | solution.py:119
  78.2 4.7 %all-to-all-start = ((bf16[16,16,4096]{2,1,0:T(8,128)(2,1)}), bf16[16,16,4096]{2,1,0:T(8,128)(2,1)}, u32[]{:S(2)}, u32[]{:S(2)}) async-start(bf16[16,16,4096]{2,1,0:T(8,128)(2,1)} %bitcast.246), calls=%async_computation | async-start | bytes 4194304 | tf_op jit(solution)/shard_map/all_to_all | solution.py:119
  83.2 3.0 convolution_convert_fusion.4
  87.8 2.1 convolution_bitcast_fusion
  91.2 50.0 %collective-permute-done.10 = bf16[32,4096]{1,0:T(8,128)(2,1)} collective-permute-done((bf16[32,4096]{1,0:T(8,128)(2,1)}, bf16[32,4096]{1,0:T(8,128)(2,1)}, u32[]{:S(2)}, u32[]{:S(2)}) %collective-permute-start.10) | collective-permute-done | bytes 262176 | tf_op jit(solution)/shard_map/ppermute | solution.py:157
  141.2 1.6 collective-permute-start.5
  142.8 9.9 %collective-permute-done.9 = bf16[32,4096]{1,0:T(8,128)(2,1)S(1)} collective-permute-done((bf16[32,4096]{1,0:T(8,128)(2,1)}, bf16[32,4096]{1,0:T(8,128)(2,1)S(1)}, u32[]{:S(2)}, u32[]{:S(2)}) %collective-permute-start.9) | collective-permute-done | bytes 262176 | tf_op jit(solution)/shard_map/ppermute | solution.py:157
  153.5 1.3 fusion.69
  154.8 1.6 collective-permute-start.15
  158.4 2.1 add.559
  160.5 1.8 fusion.72
  162.3 4.3 %fusion.206 = f32[256,512]{0,1:T(8,128)} fusion(bf16[256,4096]{1,0:T(8,128)(2,1)} %bitcast.17, bf16[256,4096]{1,0:T(8,128)(2,1)S(1)} %bitcast.239, bf16[256,4096]{1,0:T(8,128)(2,1)} %bitcast.249), kind=kOutput, calls=%fused_computation.409 | convolution fusion | flops 1082130432 | bytes 6815744 | tf_op jit(solution)/shard_map/dot_general | solution.py:33
  166.7 1.4 collective-permute-start.6
  168.1 2.1 multiply_reduce_fusion
  170.9 2.1 multiply_reduce_fusion.1
  173.0 1.5 collective-permute-start.4
  174.5 5.1 %fusion.207 = f32[256,512]{0,1:T(8,128)} fusion(bf16[256,4096]{1,0:T(8,128)(2,1)} %bitcast.1, bf16[256,4096]{1,0:T(8,128)(2,1)S(1)} %bitcast.240, bf16[256,4096]{1,0:T(8,128)(2,1)} %bitcast.250), kind=kOutput, calls=%fused_computation.410 | convolution fusion | flops 1082130432 | bytes 6815744 | tf_op jit(solution)/shard_map/dot_general | solution.py:33
  179.9 1.2 collective-permute-done.7
  181.2 1.3 add.584
  184.9 3.7 %fusion.63 = bf16[256,4096]{1,0:T(8,128)(2,1)} fusion(bf16[256,4096]{1,0:T(8,128)(2,1)S(1)} %bitcast.241, bf16[256,4096]{1,0:T(8,128)(2,1)} %bitcast.17, bf16[256,64]{0,1:T(8,128)(2,1)S(1)} %fusion.108, bf16[256,64]{0,1:T(8,128)(2,1)S(1)} %fusion.114, bf16[256,64]{0,1:T(8,128)(2,1)S(1)} %fusion.119, bf16[256,64]{0,1:T(8,128)(2,1)S(1)} %fusion.120), kind=kOutput, calls=%fused_computation.106 | convolution fusion | flops 540540928 | bytes 6422528 | tf_op jit(solution)/shard_map/dot_general | solution.py:78
  188.6 7.6 %all-to-all-start.3 = ((bf16[16,16,4096]{2,1,0:T(8,128)(2,1)}), bf16[16,16,4096]{2,1,0:T(8,128)(2,1)}, u32[]{:S(2)}, u32[]{:S(2)}) async-start(bf16[16,16,4096]{2,1,0:T(8,128)(2,1)} %bitcast.243), calls=%async_computation.3 | async-start | bytes 4194304 | tf_op jit(solution)/shard_map/all_to_all | solution.py:166
  196.2 1.3 add.556
  199.9 1.6 all-gather.3.cloned.1.call-done
  201.5 3.8 %fusion.67 = f32[128,512]{0,1:T(8,128)S(1)} fusion(bf16[1,512,4096]{2,1,0:T(8,128)(2,1)} %all-gather.3.cloned.1.call-done, bf16[32,4096]{1,0:T(8,128)(2,1)} %collective-permute-done.10, bf16[32,4096]{1,0:T(8,128)(2,1)} %copy-done.7, bf16[32,4096]{1,0:T(8,128)(2,1)} %collective-permute-done.8, bf16[32,4096]{1,0:T(8,128)(2,1)S(1)} %get-tuple-element.233), kind=kOutput, calls=%fused_computation.119 | convolution fusion | flops 541065216 | bytes 5505024 | tf_op jit(solution)/shard_map/dot_general | solution.py:33
  205.3 1.5 collective-permute-start.14
  206.8 1.3 fusion.65
  208.8 3.6 %fusion.62 = bf16[256,4096]{1,0:T(8,128)(2,1)} fusion(bf16[256,4096]{1,0:T(8,128)(2,1)S(1)} %bitcast.242, bf16[256,4096]{1,0:T(8,128)(2,1)} %bitcast.1, bf16[256,64]{0,1:T(8,128)(2,1)S(1)} %fusion.126, bf16[256,64]{0,1:T(8,128)(2,1)S(1)} %fusion.132, bf16[256,64]{0,1:T(8,128)(2,1)S(1)} %fusion.137, bf16[256,64]{0,1:T(8,128)(2,1)S(1)} %fusion.138), kind=kOutput, calls=%fused_computation.105 | convolution fusion | flops 540540928 | bytes 6422528 | tf_op jit(solution)/shard_map/dot_general | solution.py:78
  212.4 2.1 collective-permute-done.14
  214.6 10.5 %collective-permute-done.16 = f32[256,512]{1,0:T(8,128)S(1)} collective-permute-done((f32[256,512]{1,0:T(8,128)S(1)}, f32[256,512]{1,0:T(8,128)S(1)}, u32[]{:S(2)}, u32[]{:S(2)}) %collective-permute-start.16) | collective-permute-done | bytes 524320 | tf_op jit(solution)/shard_map/ppermute | solution.py:14
  226.9 17.0 %all-to-all-done.3 = bf16[16,16,4096]{2,1,0:T(8,128)(2,1)} async-done(((bf16[16,16,4096]{2,1,0:T(8,128)(2,1)}), bf16[16,16,4096]{2,1,0:T(8,128)(2,1)}, u32[]{:S(2)}, u32[]{:S(2)}) %all-to-all-start.3) | async-done | bytes 2097184 | tf_op jit(solution)/shard_map/all_to_all | solution.py:166
  243.9 4.7 %all-to-all-start.1 = ((bf16[16,16,4096]{2,1,0:T(8,128)(2,1)}), bf16[16,16,4096]{2,1,0:T(8,128)(2,1)S(1)}, u32[]{:S(2)}, u32[]{:S(2)}) async-start(bf16[16,16,4096]{2,1,0:T(8,128)(2,1)} %bitcast.244), calls=%async_computation.1 | async-start | bytes 4194304 | tf_op jit(solution)/shard_map/all_to_all | solution.py:166
  250.7 2.2 fusion.64
  253.8 1.5 collective-permute-start.17
  255.8 1.5 collective-permute-start.19
  257.3 6.2 %fusion.82 = f32[512,4096]{1,0:T(8,128)} fusion(bf16[256,4096]{1,0:T(8,128)(2,1)} %bitcast.26, s32[512]{0:T(512)S(1)} %get-tuple-element.238), kind=kOutput, calls=%fused_computation.173 | convolution fusion | flops 1073872896 | bytes 10487808 | tf_op jit(solution)/shard_map/dot_general | solution.py:177
  263.5 44.5 %all-to-all-done.1 = bf16[16,16,4096]{2,1,0:T(8,128)(2,1)S(1)} async-done(((bf16[16,16,4096]{2,1,0:T(8,128)(2,1)}), bf16[16,16,4096]{2,1,0:T(8,128)(2,1)S(1)}, u32[]{:S(2)}, u32[]{:S(2)}) %all-to-all-start.1) | async-done | bytes 2097184 | tf_op jit(solution)/shard_map/all_to_all | solution.py:166
  308.0 1.3 fusion.81
  309.3 2.6 collective-permute-done.18
  311.8 6.1 %collective-permute-done.19 = bf16[32,4096]{1,0:T(8,128)(2,1)S(1)} collective-permute-done((bf16[32,4096]{1,0:T(8,128)(2,1)S(1)}, bf16[32,4096]{1,0:T(8,128)(2,1)S(1)}, u32[]{:S(2)}, u32[]{:S(2)}) %collective-permute-start.19) | collective-permute-done | bytes 262176 | tf_op jit(solution)/shard_map/ppermute | solution.py:157
  317.9 2.9 add_convert_fusion
  (125 shorter events, 20.6 us)
Async XLA Ops:
  23.4 6.9 %copy-start.4 = (bf16[1,4,64,4096]{3,2,1,0:T(8,128)(2,1)S(1)}, bf16[1,4,64,4096]{3,2,1,0:T(8,128)(2,1)}, u32[]{:S(2)}) copy-start(bf16[1,4,64,4096]{3,2,1,0:T(8,128)(2,1)} %param.11) | copy-start | bytes 6291460
  23.4 54.8 %all-to-all-start.2 = ((bf16[16,16,4096]{2,1,0:T(8,128)(2,1)}), bf16[16,16,4096]{2,1,0:T(8,128)(2,1)}, u32[]{:S(2)}, u32[]{:S(2)}) async-start(bf16[16,16,4096]{2,1,0:T(8,128)(2,1)} %bitcast.247), calls=%async_computation.2 | async-start | bytes 4194304 | tf_op jit(solution)/shard_map/all_to_all | solution.py:119
  32.3 3.6 %copy-start.1 = (bf16[512,4096]{1,0:T(8,128)(2,1)}, bf16[512,4096]{1,0:T(8,128)(2,1)S(1)}, u32[]{:S(2)}) copy-start(bf16[512,4096]{1,0:T(8,128)(2,1)S(1)} %pad_maximum_fusion.6) | copy-start | bytes 12582916
  32.3 5.5 %copy-start.2 = (bf16[512,4096]{1,0:T(8,128)(2,1)S(1)}, bf16[512,4096]{1,0:T(8,128)(2,1)}, u32[]{:S(2)}) copy-start(bf16[512,4096]{1,0:T(8,128)(2,1)} %param.7) | copy-start | bytes 12582916
  35.9 124.6 %collective-permute-start.11 = (bf16[128,4096]{1,0:T(8,128)(2,1)}, bf16[128,4096]{1,0:T(8,128)(2,1)}, u32[]{:S(2)}, u32[]{:S(2)}) collective-permute-start(bf16[128,4096]{1,0:T(8,128)(2,1)} %get-tuple-element.227), channel_id=1, source_target_pairs={{0,2},{2,0},{4,6},{6,4},{8,10},{10,8},{12,14},{14,12},{16,18},{18,... | collective-permute-start | bytes 3145736 | tf_op jit(solution)/shard_map/ppermute | solution.py:131
  36.1 124.5 %collective-permute-start.12 = (bf16[128,4096]{1,0:T(8,128)(2,1)}, bf16[128,4096]{1,0:T(8,128)(2,1)}, u32[]{:S(2)}, u32[]{:S(2)}) collective-permute-start(bf16[128,4096]{1,0:T(8,128)(2,1)} %get-tuple-element.226), channel_id=1, source_target_pairs={{0,4},{2,6},{4,0},{6,2},{8,12},{10,14},{12,8},{14,10},{16,20},{18,... | collective-permute-start | bytes 3145736 | tf_op jit(solution)/shard_map/ppermute | solution.py:131
  37.5 123.0 %collective-permute-start.13 = (bf16[128,4096]{1,0:T(8,128)(2,1)}, bf16[128,4096]{1,0:T(8,128)(2,1)}, u32[]{:S(2)}, u32[]{:S(2)}) collective-permute-start(bf16[128,4096]{1,0:T(8,128)(2,1)} %get-tuple-element.225), channel_id=1, source_target_pairs={{0,6},{2,4},{4,2},{6,0},{8,14},{10,12},{12,10},{14,8},{16,22},{18,... | collective-permute-start | bytes 3145736 | tf_op jit(solution)/shard_map/ppermute | solution.py:131
  78.2 92.7 %all-to-all-start = ((bf16[16,16,4096]{2,1,0:T(8,128)(2,1)}), bf16[16,16,4096]{2,1,0:T(8,128)(2,1)}, u32[]{:S(2)}, u32[]{:S(2)}) async-start(bf16[16,16,4096]{2,1,0:T(8,128)(2,1)} %bitcast.246), calls=%async_computation | async-start | bytes 4194304 | tf_op jit(solution)/shard_map/all_to_all | solution.py:119
  82.9 118.5 %all-gather.3.cloned.1.call-start = ((), (), s32[]{:S(2)}) async-start(), calls=%async_computation.4 | async-start | bytes 5242880 | tf_op jit(solution)/shard_map/all_gather | solution.py:138
  83.2 4.6 %copy-start.6 = (bf16[1,4,4096,64]{2,3,1,0:T(8,128)(2,1)S(1)}, bf16[1,4,4096,64]{2,3,1,0:T(8,128)(2,1)}, u32[]{:S(2)}) copy-start(bf16[1,4,4096,64]{2,3,1,0:T(8,128)(2,1)} %param.10) | copy-start | bytes 6291460
  87.2 53.9 %collective-permute-start.10 = (bf16[32,4096]{1,0:T(8,128)(2,1)}, bf16[32,4096]{1,0:T(8,128)(2,1)}, u32[]{:S(2)}, u32[]{:S(2)}) collective-permute-start(bf16[32,4096]{1,0:T(8,128)(2,1)} %get-tuple-element.234), channel_id=1, source_target_pairs={{0,24},{2,26},{4,28},{6,30},{8,16},{10,18},{12,20},{14,22},{16,8},... | collective-permute-start | bytes 786440 | tf_op jit(solution)/shard_map/ppermute | solution.py:157
  90.0 51.2 %collective-permute-start.8 = (bf16[32,4096]{1,0:T(8,128)(2,1)}, bf16[32,4096]{1,0:T(8,128)(2,1)}, u32[]{:S(2)}, u32[]{:S(2)}) collective-permute-start(bf16[32,4096]{1,0:T(8,128)(2,1)} %get-tuple-element.236), channel_id=1, source_target_pairs={{0,8},{2,10},{4,12},{6,14},{8,0},{10,2},{12,4},{14,6},{16,24},{18,... | collective-permute-start | bytes 786440 | tf_op jit(solution)/shard_map/ppermute | solution.py:157
  141.2 11.6 %collective-permute-start.9 = (bf16[32,4096]{1,0:T(8,128)(2,1)}, bf16[32,4096]{1,0:T(8,128)(2,1)S(1)}, u32[]{:S(2)}, u32[]{:S(2)}) collective-permute-start(bf16[32,4096]{1,0:T(8,128)(2,1)} %get-tuple-element.235), channel_id=1, source_target_pairs={{0,16},{2,18},{4,20},{6,22},{8,24},{10,26},{12,28},{14,30},{16,0},... | collective-permute-start | bytes 786440 | tf_op jit(solution)/shard_map/ppermute | solution.py:157
  141.2 17.3 %collective-permute-start.5 = (f32[256,512]{0,1:T(8,128)}, f32[256,512]{0,1:T(8,128)}, u32[]{:S(2)}, u32[]{:S(2)}) collective-permute-start(f32[256,512]{0,1:T(8,128)} %convolution_bitcast_fusion), channel_id=1, source_target_pairs={{0,1},{1,0},{2,3},{3,2},{4,5},{5,4},{6,7},{7,6},{8,9},{9,8},{10,11... | collective-permute-start | bytes 1572872 | tf_op jit(solution)/shard_map/ppermute | solution.py:14
  152.7 0.7 copy-start.7
  154.8 3.6 %collective-permute-start.15 = (f32[128,1]{0,1:T(1,128)S(1)}, f32[128,1]{0,1:T(1,128)S(1)}, u32[]{:S(2)}, u32[]{:S(2)}) collective-permute-start(f32[128,1]{0,1:T(1,128)S(1)} %bitcast.267), channel_id=1, source_target_pairs={{0,1},{1,0},{2,3},{3,2},{4,5},{5,4},{6,7},{7,6},{8,9},{9,8},{10,11... | collective-permute-start | bytes 1544 | tf_op jit(solution)/shard_map/ppermute | solution.py:14
  166.7 14.5 %collective-permute-start.6 = (f32[256,512]{0,1:T(8,128)}, f32[256,512]{0,1:T(8,128)}, u32[]{:S(2)}, u32[]{:S(2)}) collective-permute-start(f32[256,512]{0,1:T(8,128)} %fusion.206), channel_id=1, source_target_pairs={{0,1},{1,0},{2,3},{3,2},{4,5},{5,4},{6,7},{7,6},{8,9},{9,8},{10,11... | collective-permute-start | bytes 1572872 | tf_op jit(solution)/shard_map/ppermute | solution.py:14
  170.2 10.9 %collective-permute-start.7 = (f32[256,1]{0,1:T(1,128)S(1)}, f32[256,1]{0,1:T(1,128)S(1)}, u32[]{:S(2)}, u32[]{:S(2)}) collective-permute-start(f32[256,1]{0,1:T(1,128)S(1)} %broadcast_in_dim.166), channel_id=1, source_target_pairs={{0,1},{1,0},{2,3},{3,2},{4,5},{5,4},{6,7},{7,6},{8,9},{9,8},{10,11... | collective-permute-start | bytes 3080 | tf_op jit(solution)/shard_map/ppermute | solution.py:14
  173.0 8.1 %collective-permute-start.4 = (f32[256,1]{0,1:T(1,128)S(1)}, f32[256,1]{0,1:T(1,128)S(1)}, u32[]{:S(2)}, u32[]{:S(2)}) collective-permute-start(f32[256,1]{0,1:T(1,128)S(1)} %broadcast_in_dim.162), channel_id=1, source_target_pairs={{0,1},{1,0},{2,3},{3,2},{4,5},{5,4},{6,7},{7,6},{8,9},{9,8},{10,11... | collective-permute-start | bytes 3080 | tf_op jit(solution)/shard_map/ppermute | solution.py:14
  174.5 8.0 %copy-start.5 = (f32[256,512]{0,1:T(8,128)S(1)}, f32[256,512]{0,1:T(8,128)}, u32[]{:S(2)}) copy-start(f32[256,512]{0,1:T(8,128)} %add.559) | copy-start | bytes 1572868
  179.5 16.6 %collective-permute-start.3 = (f32[256,512]{0,1:T(8,128)}, f32[256,512]{0,1:T(8,128)}, u32[]{:S(2)}, u32[]{:S(2)}) collective-permute-start(f32[256,512]{0,1:T(8,128)} %fusion.207), channel_id=1, source_target_pairs={{0,1},{1,0},{2,3},{3,2},{4,5},{5,4},{6,7},{7,6},{8,9},{9,8},{10,11... | collective-permute-start | bytes 1572872 | tf_op jit(solution)/shard_map/ppermute | solution.py:14
  188.6 55.4 %all-to-all-start.3 = ((bf16[16,16,4096]{2,1,0:T(8,128)(2,1)}), bf16[16,16,4096]{2,1,0:T(8,128)(2,1)}, u32[]{:S(2)}, u32[]{:S(2)}) async-start(bf16[16,16,4096]{2,1,0:T(8,128)(2,1)} %bitcast.243), calls=%async_computation.3 | async-start | bytes 4194304 | tf_op jit(solution)/shard_map/all_to_all | solution.py:166
  201.5 5.3 %copy-start.8 = (bf16[1,512,4096]{2,1,0:T(8,128)(2,1)S(1)}, bf16[1,512,4096]{2,1,0:T(8,128)(2,1)}, u32[]{:S(2)}) copy-start(bf16[1,512,4096]{2,1,0:T(8,128)(2,1)} %all-gather.3.cloned.1.call-done) | copy-start | bytes 12582916
  205.3 9.2 %collective-permute-start.14 = (f32[128,512]{0,1:T(8,128)S(1)}, f32[128,512]{0,1:T(8,128)S(1)}, u32[]{:S(2)}, u32[]{:S(2)}) collective-permute-start(f32[128,512]{0,1:T(8,128)S(1)} %fusion.67), channel_id=1, source_target_pairs={{0,1},{1,0},{2,3},{3,2},{4,5},{5,4},{6,7},{7,6},{8,9},{9,8},{10,11... | collective-permute-start | bytes 786440 | tf_op jit(solution)/shard_map/ppermute | solution.py:14
  208.1 17.0 %collective-permute-start.16 = (f32[256,512]{1,0:T(8,128)S(1)}, f32[256,512]{1,0:T(8,128)S(1)}, u32[]{:S(2)}, u32[]{:S(2)}) collective-permute-start(f32[256,512]{1,0:T(8,128)S(1)} %fusion.65), channel_id=1, source_target_pairs={{0,1},{1,0},{2,3},{3,2},{4,5},{5,4},{6,7},{7,6},{8,9},{9,8},{10,11... | collective-permute-start | bytes 1572872 | tf_op jit(solution)/shard_map/ppermute | solution.py:14
  243.9 64.1 %all-to-all-start.1 = ((bf16[16,16,4096]{2,1,0:T(8,128)(2,1)}), bf16[16,16,4096]{2,1,0:T(8,128)(2,1)S(1)}, u32[]{:S(2)}, u32[]{:S(2)}) async-start(bf16[16,16,4096]{2,1,0:T(8,128)(2,1)} %bitcast.244), calls=%async_computation.1 | async-start | bytes 4194304 | tf_op jit(solution)/shard_map/all_to_all | solution.py:166
  253.8 55.5 %collective-permute-start.17 = (bf16[32,4096]{1,0:T(8,128)(2,1)}, bf16[32,4096]{1,0:T(8,128)(2,1)S(1)}, u32[]{:S(2)}, u32[]{:S(2)}) collective-permute-start(bf16[32,4096]{1,0:T(8,128)(2,1)} %get-tuple-element.232), channel_id=1, source_target_pairs={{0,8},{2,10},{4,12},{6,14},{8,0},{10,2},{12,4},{14,6},{16,24},{18,... | collective-permute-start | bytes 786440 | tf_op jit(solution)/shard_map/ppermute | solution.py:157
  255.3 56.6 %collective-permute-start.18 = (bf16[32,4096]{1,0:T(8,128)(2,1)}, bf16[32,4096]{1,0:T(8,128)(2,1)S(1)}, u32[]{:S(2)}, u32[]{:S(2)}) collective-permute-start(bf16[32,4096]{1,0:T(8,128)(2,1)} %get-tuple-element.231), channel_id=1, source_target_pairs={{0,16},{2,18},{4,20},{6,22},{8,24},{10,26},{12,28},{14,30},{16,0},... | collective-permute-start | bytes 786440 | tf_op jit(solution)/shard_map/ppermute | solution.py:157
  255.8 62.0 %collective-permute-start.19 = (bf16[32,4096]{1,0:T(8,128)(2,1)S(1)}, bf16[32,4096]{1,0:T(8,128)(2,1)S(1)}, u32[]{:S(2)}, u32[]{:S(2)}) collective-permute-start(bf16[32,4096]{1,0:T(8,128)(2,1)S(1)} %get-tuple-element.230), channel_id=1, source_target_pairs={{0,24},{2,26},{4,28},{6,30},{8,16},{10,18},{12,20},{14,22},{16,8},... | collective-permute-start | bytes 786440 | tf_op jit(solution)/shard_map/ppermute | solution.py:157
  308.0 9.9 %copy-start.3 = (f32[512,4096]{1,0:T(8,128)S(1)}, f32[512,4096]{1,0:T(8,128)}, u32[]{:S(2)}) copy-start(f32[512,4096]{1,0:T(8,128)} %fusion.82) | copy-start | bytes 25165828
Sparse Core Ops, SparseCore 0:
  162.5 38.9 all-gather.2

commit v2 on v0

v2 whole, which is shorter than its diff:
```python
import math

import jax
import jax.numpy as jnp
import numpy as np
from jax import lax
from jax.experimental import pallas as pl
from jax.experimental.pallas import tpu as pltpu
from jax.sharding import PartitionSpec as P

epsilon = 1e-05
F32 = jnp.float32
BF16 = jnp.bfloat16
VMEM_BYTES = 40 * 2**20


def parts_mp(value):
    size = lax.axis_size("mp")
    if size == 2:
        return [value, lax.ppermute(value, "mp", [(0, 1), (1, 0)])]
    return [lax.psum(value, "mp")]


def whole(array):
    return pl.BlockSpec(array.shape, lambda step: (0,) * array.ndim)


def columns(rows, tile, part=0):
    return pl.BlockSpec((rows, tile), lambda step: (part, step))


def call(body, outs, out_specs, operands, in_specs, steps, scratch=(), aliases=None):
    return pl.pallas_call(
        body,
        grid=(steps,),
        out_shape=outs,
        in_specs=in_specs,
        out_specs=out_specs,
        scratch_shapes=list(scratch),
        input_output_aliases=aliases or {},
        compiler_params=pltpu.CompilerParams(vmem_limit_bytes=VMEM_BYTES),
        cost_estimate=pl.CostEstimate(flops=1, bytes_accessed=1, transcendentals=0),
    )(*operands)


def tiling(width):
    tile = math.gcd(width, 2048)
    return tile, width // tile


def pack(target, hidden, total):
    count, width = hidden.shape
    tile, steps = tiling(width)

    def body(target_ref, hidden_ref, out_ref):
        at = lax.broadcasted_iota(jnp.int32, (total, count), 0)
        hot = (at == target_ref[...]).astype(F32).astype(BF16)
        out_ref[...] = jnp.dot(hot, hidden_ref[...], preferred_element_type=F32).astype(BF16)

    target = target.reshape(1, count)
    return call(
        body,
        jax.ShapeDtypeStruct((total, width), BF16),
        columns(total, tile),
        (target, hidden),
        [whole(target), columns(count, tile)],
        steps,
    )


def unpack(targets, arrays):
    count = targets[0].shape[0]
    width = arrays[0].shape[1]
    tile, steps = tiling(width)

    def body(*refs):
        target_refs, array_refs, out_ref = refs[: len(arrays)], refs[len(arrays) : -1], refs[-1]
        total = jnp.zeros((count, tile), F32)
        for target_ref, array_ref in zip(target_refs, array_refs):
            at = lax.broadcasted_iota(jnp.int32, (count, array_ref.shape[0]), 1)
            hot = (at == target_ref[...]).astype(F32).astype(BF16)
            total = total + jnp.dot(hot, array_ref[...], preferred_element_type=F32)
        out_ref[...] = total.astype(BF16)

    targets = [target.reshape(count, 1) for target in targets]
    return call(
        body,
        jax.ShapeDtypeStruct((count, width), BF16),
        columns(count, tile),
        (*targets, *arrays),
        [whole(t) for t in targets] + [columns(a.shape[0], tile) for a in arrays],
        steps,
    )


def sketch_weights(down, up):
    layers, width, rank = down.shape
    flat_down = jnp.swapaxes(down, 1, 2).reshape(layers * rank, width)
    return jnp.concatenate([flat_down, up.reshape(layers * rank, width)], axis=0)


def against(left, right):
    return lax.dot_general(left, right, (((1,), (1,)), ((), ())), preferred_element_type=F32)


def gram(weights):
    total, width = weights.shape
    half = total // 2
    tile, steps = tiling(width)

    def body(weights_ref, out_ref):
        @pl.when(pl.program_id(0) == 0)
        def _():
            out_ref[...] = jnp.zeros_like(out_ref)

        out_ref[...] += against(weights_ref[half:, :], weights_ref[...])

    return call(
        body,
        jax.ShapeDtypeStruct((half, total), F32),
        pl.BlockSpec((half, total), lambda step: (0, 0)),
        (weights,),
        [columns(total, tile)],
        steps,
    )


def sketch(rows, weights, part=0, parts=1):
    count, width = rows.shape
    count //= parts
    total = weights.shape[0]
    tile, steps = tiling(width)

    def body(rows_ref, weights_ref, out_ref, narrow_ref):
        step = pl.program_id(0)

        @pl.when(step == 0)
        def _():
            out_ref[...] = jnp.zeros_like(out_ref)

        values = rows_ref[...]
        out_ref[:, :total] += against(values, weights_ref[...])
        widened = values.astype(F32)
        out_ref[:, total:] += jnp.sum(widened * widened, axis=1, keepdims=True)

        @pl.when(step == steps - 1)
        def _():
            narrow_ref[:, :total] = out_ref[:, :total].astype(BF16)
            squares = out_ref[:, total:]
            column = lax.broadcasted_iota(jnp.int32, squares.shape, 1)
            first = squares.astype(BF16).astype(F32)
            second = (squares - first).astype(BF16).astype(F32)
            third = squares - first - second
            terms = jnp.where(column == 0, first, jnp.where(column == 1, second, third))
            narrow_ref[:, total:] = jnp.where(column < 3, terms, 0.0).astype(BF16)

    shape = (count, total + 128)
    return call(
        body,
        [jax.ShapeDtypeStruct(shape, F32), jax.ShapeDtypeStruct(shape, BF16)],
        [pl.BlockSpec(shape, lambda step: (0, 0))] * 2,
        (rows, weights),
        [columns(count, tile, part), columns(total, tile)],
        steps,
    )


def sketch_parts(sketched, narrow):
    if lax.axis_size("mp") == 2:
        return [sketched, lax.ppermute(narrow, "mp", [(0, 1), (1, 0)])]
    return [lax.psum(sketched, "mp")]


def widen(part, total):
    if part.dtype == F32:
        return part
    part = part.astype(F32)
    squares = jnp.sum(part[:, total:], axis=1, keepdims=True)
    return jnp.concatenate([part[:, :total], jnp.broadcast_to(squares, part[:, total:].shape)], 1)


def low_rank(sketched, table, layers, model_width):
    half = table.shape[0]
    total = table.shape[1]
    rank = half // layers
    high = table.astype(BF16)
    rest = (table - high.astype(F32)).astype(BF16)
    projected, overlap = sketched[:, :half], sketched[:, half:total]
    squares = sketched[:, total : total + 1]
    column = lax.broadcasted_iota(jnp.int32, (sketched.shape[0], half), 1)
    low = jnp.zeros((sketched.shape[0], half), F32)
    added = jnp.zeros((sketched.shape[0], total), F32)
    for layer in range(layers):
        here = (column >= layer * rank) & (column < (layer + 1) * rank)
        scaled = (projected + added[:, :half]) * lax.rsqrt(squares / model_width + epsilon)
        scaled = scaled.astype(BF16).astype(F32)
        low = jnp.where(here, scaled, low)
        if layer + 1 < layers:
            narrow = low.astype(BF16)
            after = jnp.dot(narrow, high, preferred_element_type=F32) + jnp.dot(
                narrow, rest, preferred_element_type=F32
            )
            step = 2.0 * overlap + added[:, half:] + after[:, half:]
            change = jnp.sum(jnp.where(here, scaled * step, 0.0), axis=1, keepdims=True)
            squares = jnp.maximum(squares + change, 0.0)
            added = after
    return low.astype(BF16)


def finish(rows, sketched, tables, weights, layers, model_width, part=0, parts=1, filled=None):
    whole_count, width = rows.shape
    count = whole_count // parts
    half = weights.shape[0] // 2
    tile, steps = tiling(width)

    filled = [] if filled is None else [filled]

    def body(*refs):
        rows_ref, up_ref = refs[:2]
        sketch_refs = refs[2 : 2 + len(sketched)]
        table_refs = refs[2 + len(sketched) :][: len(tables)]
        out_ref, low_ref = refs[-2:]

        @pl.when(pl.program_id(0) == 0)
        def _():
            whole_sketch = sum(widen(ref[...], 2 * half) for ref in sketch_refs)
            whole_table = sum(ref[...] for ref in table_refs)
            low_ref[...] = low_rank(whole_sketch, whole_table, layers, model_width)

        update = jnp.dot(low_ref[...], up_ref[...], preferred_element_type=F32)
        out_ref[...] = (rows_ref[...].astype(F32) + update).astype(BF16)

    return call(
        body,
        jax.ShapeDtypeStruct((whole_count, width), BF16),
        columns(count, tile, part),
        (rows, weights, *sketched, *tables, *filled),
        [columns(count, tile, part), columns(half, tile, 1)]
        + [whole(a) for a in (*sketched, *tables)]
        + [pl.BlockSpec(memory_space=pl.ANY) for _ in filled],
        steps,
        scratch=[pltpu.VMEM((count, half), BF16)],
        aliases={2 + len(sketched) + len(tables): 0} if filled else None,
    )


def adapt(rows, weights, tables, layers, model_width):
    sketched = sketch_parts(*sketch(rows, weights))
    return finish(rows, sketched, tables, weights, layers, model_width)


def local(hidden, request_adapter, store_slot, down_store, up_store):
    count, width = hidden.shape
    owners = lax.axis_size("dp")
    adapters = store_slot.shape[0]
    assert adapters == owners and down_store.shape[0] == 1
    layers = down_store.shape[1]
    model_width = width * lax.axis_size("mp")
    slot_rows = count // adapters
    group = 1
    while group * group < owners:
        group *= 2
    planes = owners // group
    me = lax.axis_index("dp")
    my_plane, my_place = me // group, me % group

    adapter_ids = jnp.arange(adapters, dtype=jnp.int32)
    matches = request_adapter[:, None] == adapter_ids[None, :]
    slot = jnp.sum(jnp.where(matches, store_slot[None, :], 0), axis=1)
    request_ids = jnp.arange(count, dtype=jnp.int32)
    earlier = (slot[:, None] == slot[None, :]) & (request_ids[:, None] > request_ids[None, :])
    position = jnp.sum(earlier.astype(jnp.int32), axis=1)
    by_slot = slot[:, None] == adapter_ids[None, :]
    counts = jnp.sum(by_slot.astype(jnp.int32), axis=0)
    over = position >= slot_rows
    excess = jnp.maximum(counts - slot_rows, 0)

    plane = slot // group
    my_choice = jnp.argmax(excess.reshape(planes, group), axis=1).astype(jnp.int32)

    is_mine = jnp.sum(
        jnp.where(adapter_ids[:, None] // group == jnp.arange(planes)[None, :], my_choice, 0), axis=1
    ) == adapter_ids % group
    row_is_mine = jnp.any(by_slot & is_mine[None, :], axis=1)

    def add_over(value, steps):
        pairs = [[(i, i ^ step) for i in range(owners)] for step in steps]
        return value + sum(lax.ppermute(value, "dp", p) for p in pairs)

    def exchange(rows):
        blocks = rows.reshape(owners, slot_rows, width)
        return lax.all_to_all(blocks, "dp", 0, 0, tiled=True).reshape(owners * slot_rows, width)

    target = jnp.where(over, -1, slot * slot_rows + position)
    packed = pack(target, hidden, owners * slot_rows)
    tallies = add_over(jnp.stack([excess, jnp.where(is_mine, 0, excess)]), range(1, group))
    packed, tallies = lax.optimization_barrier((packed, tallies))
    arrived = exchange(packed)

    over_target = jnp.where(
        over & row_is_mine, (plane ^ my_plane) * slot_rows + position - slot_rows, -1
    )
    over_packed = pack(over_target, hidden, planes * slot_rows)

    weights = sketch_weights(down_store[0], up_store[0])
    table = parts_mp(gram(weights))

    plane_excess = tallies[0].reshape(planes, group)
    choice = jnp.argmax(
        lax.dynamic_index_in_dim(plane_excess, my_plane, 0, keepdims=False)
    ).astype(jnp.int32)
    is_choice = adapter_ids == my_plane * group + choice
    tallies = jnp.concatenate([tallies, is_choice.astype(jnp.int32)[None, :]])
    mine = weights
    rows_left = weights.shape[0] // group
    step = 1
    while step < group:
        my_bit = (my_place // step) % 2
        halves = mine.reshape(-1, 2, rows_left, width)
        keep = lax.dynamic_index_in_dim(halves, my_bit, 1, keepdims=False)
        give = lax.dynamic_index_in_dim(halves, 1 - my_bit, 1, keepdims=False)
        taken = lax.ppermute(give, "dp", [(i, i ^ step) for i in range(owners)])
        mine = jnp.where((choice // step) % 2 == my_bit, keep, taken)
        step *= 2
    mine = mine.reshape(rows_left, width)
    mine, tallies = lax.optimization_barrier((mine, tallies))
    tallies = add_over(tallies, range(group, owners, group))
    mine, tallies, over_packed, arrived, *table = lax.optimization_barrier(
        (mine, tallies, over_packed, arrived, *table)
    )

    groups = [[p * group + q for q in range(group)] for p in range(planes)]
    plane_weights = lax.all_gather(mine, "dp", axis_index_groups=groups, tiled=True)

    def swap_planes(rows):
        blocks = rows.reshape(planes, slot_rows, width)
        moved = [blocks[0]]
        for step in range(1, planes):
            pairs = [(i, i ^ (step * group)) for i in range(owners)]
            moved.append(lax.ppermute(blocks[step], "dp", pairs))
        return moved

    sketched, narrow = sketch(arrived, weights)
    narrow, over_packed = lax.optimization_barrier((narrow, over_packed))
    sketched = sketch_parts(sketched, narrow)
    over_arrived = swap_planes(over_packed)
    *over_arrived, sketched[0] = lax.optimization_barrier((*over_arrived, sketched[0]))
    done = finish(arrived, sketched, table, weights, layers, model_width)

    returned = [exchange(done)]
    plane_weights, over_arrived[0], done = lax.optimization_barrier(
        (plane_weights, over_arrived[0], done)
    )
    plane_table = parts_mp(gram(plane_weights))
    over_done = adapt(
        jnp.concatenate(over_arrived), plane_weights, plane_table, layers, model_width
    )

    excess, stayed, chosen = tallies
    shared = jnp.argmax(excess * chosen).astype(jnp.int32)

    def back_from(source):
        def moved(rows):
            blocks = rows.reshape(planes, slot_rows, width)
            got = [jnp.where(my_plane == source, blocks[0], jnp.zeros_like(blocks[0]))]
            for step in range(1, planes):
                pairs = [(source * group + q, (source ^ step) * group + q) for q in range(group)]
                got.append(lax.ppermute(blocks[step], "dp", pairs))
            return sum(got)

        return moved

    returned.append(
        lax.switch(shared // group, [back_from(source) for source in range(planes)], over_done)
    )
    over_target = jnp.where(
        over & row_is_mine & (slot == shared), position - slot_rows, -1
    )
    waiting = jnp.where(adapter_ids == shared, stayed, excess) > 0
    targets = [target, over_target]
    result = unpack(targets, returned)

    order = jnp.cumsum(waiting.astype(jnp.int32)) - 1
    rounds = jnp.sum(waiting.astype(jnp.int32))

    def one_round(state):
        at, filled = state
        owner = jnp.sum(jnp.where(waiting & (order == at), adapter_ids, 0))
        own = jnp.where(me == owner, weights, jnp.zeros_like(weights))
        round_weights = lax.psum(own, "dp")
        left = over & (slot == owner) & (over_target < 0)
        target = jnp.where(left, position - slot_rows, -1)
        rows = pack(target, hidden, slot_rows)
        round_table = parts_mp(gram(round_weights))
        done = adapt(rows, round_weights, round_table, layers, model_width)
        back = unpack([target], [done])
        return at + 1, jnp.where((target >= 0)[:, None], back, filled)

    _, result = lax.while_loop(lambda state: state[0] < rounds, one_round, (0, result))
    return result


def solution(mesh):
    return jax.shard_map(
        local,
        mesh=mesh,
        in_specs=(
            P("dp", "mp"),
            P("dp"),
            P(),
            P("dp", None, "mp", None),
            P("dp", None, None, "mp"),
        ),
        out_specs=P("dp", "mp"),
        check_vma=False,
    )
```

time: 587 us -> 284 us (0.48)
  blocking collectives: 209 us -> 0 us
  waiting for transfers between devices: 272 us -> 161 us
  matrix products: 39.9 us -> 0 us
  Pallas kernels: 0 us -> 33.4 us
  starting transfers between devices: 6.17 us -> 39.1 us
  local copies, waits for them, and re-layouts: 38.3 us -> 15.9 us
  between operations: 13.2 us -> 19.8 us
  other arithmetic: 6.93 us -> 12.9 us
    all_to_all x1 -> x0, blocking collectives: 189 us -> none  [local(): lax.all_to_all(outgoing.reshape(owners, adapters_per_replica * tile_rows,...]
    all_to_all x1 -> x2, waiting for transfers between devices: 183 us -> 0.01 us  [exchange(): lax.all_to_all(blocks, 'dp', 0, 0, tiled=True)]
    ppermute x0 -> x18, waiting for transfers between devices: none -> 161 us  [the longest x3 71.7 us: moved(): got.append(lax.ppermute(blocks[step], 'dp', pairs))]
    psum x4 -> x0, waiting for transfers between devices: 89.5 us -> none  [split_layer(): summed, sq_total = lax.psum((partial_value, squares), 'mp')]
    dot_general x8 -> x0, matrix products: 39.9 us -> none  [the longest x4 23.2 us: split_layer(): jnp.einsum('sjmr,jrd->sjmd', reduced, up_b, preferred_element_type=jnp.fl...]
    pallas_call x0 -> x9, Pallas kernels: none -> 33.4 us  [call(): pl.pallas_call(body, grid=(steps,), out_shape=outs, in_specs=in_specs, ou...]
    ppermute x0 -> x18, starting transfers between devices: none -> 27.5 us  [the longest x6 14.5 us: add_over(): return value + sum((lax.ppermute(value, 'dp', p) for p in pairs))]
    psum x4 -> x0, blocking collectives: 20.4 us -> none  [split_layer(): summed, sq_total = lax.psum((partial_value, squares), 'mp')]
  transfers between devices with their start and end apart: 5 -> 21, of which waited for: 5 -> 9; matrix products, arithmetic and copies ran while one was open for 1% -> 5% of each run, Pallas kernels for 0% -> 7%
where the time goes in v2:
time: 284 us; the launch traced here: 283 us
  waiting for transfers between devices  161 us (57%)
  starting transfers between devices  39.1 us (14%)
  Pallas kernels  33.4 us (12%)
  between operations  19.8 us (7%)
  local copies, waits for them, and re-layouts  15.9 us (6%)
  other arithmetic  12.9 us (5%)
    ppermute x3, waiting for transfers between devices, moved(): got.append(lax.ppermute(blocks[step], 'dp', pairs))  71.7 us
    ppermute x2, waiting for transfers between devices, local(): taken = lax.ppermute(give, 'dp', [(i, i ^ step) for i in range(owners)])  38.7 us
    pallas_call x9, Pallas kernels, call(): pl.pallas_call(body, grid=(steps,), out_shape=outs, in_specs=in_specs, ou...  33.4 us
    ppermute x3, waiting for transfers between devices, swap_planes(): moved.append(lax.ppermute(blocks[step], 'dp', pairs))  22.3 us
    ppermute x6, waiting for transfers between devices, add_over(): return value + sum((lax.ppermute(value, 'dp', p) for p in pairs))  20.6 us
    ppermute x6, starting transfers between devices, add_over(): return value + sum((lax.ppermute(value, 'dp', p) for p in pairs))  14.5 us
    unnamed x31, local copies, waits for them, and re-layouts  12.3 us
    all_to_all x2, starting transfers between devices, exchange(): lax.all_to_all(blocks, 'dp', 0, 0, tiled=True)  11.5 us
  transfers between devices with their start and end apart: 21, of which 9 were waited for; matrix products, arithmetic and copies ran while one was open for 5% of the time, Pallas kernels for 7%

profile of v2, /device:TPU:16, one launch (start us, length us, event | category | flops | bytes accessed | tf_op | source)
XLA Modules:
  0.0 283.0 jit_solution(2977003953603760523)
XLA Ops:
  6.5 0.8 select_reduce_fusion
  8.3 1.6 collective-permute-start.15
  10.6 4.4 %shard_map.55 = bf16[512,4096]{1,0:T(8,128)(2,1)S(1)} custom-call(s32[1,512]{1,0:T(1,128)S(1)} %get-tuple-element.328.target_ref, bf16[512,4096]{1,0:T(8,128)(2,1)} %hidden_ref.3), custom_call_target="tpu_custom_call" | custom-call | flops 1 | bytes 1 | tf_op jit(solution)/shard_map/pallas_call | solution.py:33
  15.0 2.0 copy-done.6
  17.1 6.3 %all-to-all-start = ((bf16[16,32,4096]{2,1,0:T(8,128)(2,1)}), bf16[16,32,4096]{2,1,0:T(8,128)(2,1)}, u32[]{:S(2)}, u32[]{:S(2)}) async-start(bf16[16,32,4096]{2,1,0:T(8,128)(2,1)} %bitcast.55), calls=%async_computation | async-start | bytes 8388608 | tf_op jit(solution)/shard_map/all_to_all | solution.py:292
  23.5 2.0 pad_maximum_fusion.weights_ref.refs_1_
  25.5 1.9 copy-done.10
  30.5 1.4 collective-permute-done.17
  31.9 1.8 bitcast_select_fusion
  33.7 1.0 constant_dynamic-slice_fusion
  34.8 1.5 collective-permute-start.18
  36.2 1.8 shard_map.57.refs_4_
  38.1 1.5 collective-permute-start.22
  41.0 37.3 %collective-permute-done.18 = bf16[1,128,4096]{2,1,0:T(8,128)(2,1)} collective-permute-done((bf16[1,128,4096]{2,1,0:T(8,128)(2,1)}, bf16[1,128,4096]{2,1,0:T(8,128)(2,1)}, u32[]{:S(2)}, u32[]{:S(2)}) %collective-permute-start.18) | collective-permute-done | bytes 1048608 | tf_op jit(solution)/shard_map/ppermute | solution.py:322
  78.3 1.2 select_bitcast_fusion
  79.5 11.1 %collective-permute-start.19 = (s32[3,16]{1,0:T(4,128)S(1)}, s32[3,16]{1,0:T(4,128)S(1)}, u32[]{:S(2)}, u32[]{:S(2)}) collective-permute-start(s32[3,16]{1,0:T(4,128)S(1)} %pad_add_fusion), channel_id=1, source_target_pairs={{0,8},{2,10},{4,12},{6,14},{8,0},{10,2},{12,4},{14,6},{16,24},{18,... | collective-permute-start | bytes 584 | tf_op jit(solution)/shard_map/ppermute | solution.py:288
  90.6 1.5 collective-permute-start.21
  92.1 2.7 shard_map.56
  94.8 19.6 %collective-permute-done.20 = s32[3,16]{1,0:T(4,128)S(1)} collective-permute-done((s32[3,16]{1,0:T(4,128)S(1)}, s32[3,16]{1,0:T(4,128)S(1)}, u32[]{:S(2)}, u32[]{:S(2)}) %collective-permute-start.20) | collective-permute-done | bytes 224 | tf_op jit(solution)/shard_map/ppermute | solution.py:288
  114.5 0.9 collective-permute-done.21
  116.0 0.8 copy-done.8
  116.8 6.0 %shard_map.58 = (f32[512,640]{1,0:T(8,128)S(1)}, bf16[512,640]{1,0:T(8,128)(2,1)}) custom-call(bf16[512,4096]{1,0:T(8,128)(2,1)} %bitcast.15.rows_ref.refs_0_, bf16[512,4096]{1,0:T(8,128)(2,1)} %copy-done.10), custom_call_target="tpu_custom_call" | custom-call | flops 1 | bytes 1 | tf_op jit(solution)/shard_map/pallas_call | solution.py:33
  122.9 1.5 collective-permute-start.26
  124.4 0.8 fusion.17
  125.1 1.5 collective-permute-start.23
  126.6 1.5 collective-permute-start.24
  128.6 7.1 %collective-permute-done.23 = bf16[32,4096]{1,0:T(8,128)(2,1)S(1)} collective-permute-done((bf16[32,4096]{1,0:T(8,128)(2,1)S(1)}, bf16[32,4096]{1,0:T(8,128)(2,1)S(1)}, u32[]{:S(2)}, u32[]{:S(2)}) %collective-permute-start.23) | collective-permute-done | bytes 262176 | tf_op jit(solution)/shard_map/ppermute | solution.py:340
  135.8 10.3 %collective-permute-done.24 = bf16[32,4096]{1,0:T(8,128)(2,1)S(1)} collective-permute-done((bf16[32,4096]{1,0:T(8,128)(2,1)S(1)}, bf16[32,4096]{1,0:T(8,128)(2,1)S(1)}, u32[]{:S(2)}, u32[]{:S(2)}) %collective-permute-start.24) | collective-permute-done | bytes 262176 | tf_op jit(solution)/shard_map/ppermute | solution.py:340
  146.1 4.8 %collective-permute-done.25 = bf16[32,4096]{1,0:T(8,128)(2,1)S(1)} collective-permute-done((bf16[32,4096]{1,0:T(8,128)(2,1)S(1)}, bf16[32,4096]{1,0:T(8,128)(2,1)S(1)}, u32[]{:S(2)}, u32[]{:S(2)}) %collective-permute-start.25) | collective-permute-done | bytes 262176 | tf_op jit(solution)/shard_map/ppermute | solution.py:340
  150.9 1.0 copy-done.9
  151.9 5.7 %shard_map.59 = bf16[512,4096]{1,0:T(8,128)(2,1)S(1)} custom-call(bf16[512,4096]{1,0:T(8,128)(2,1)} %bitcast.15.rows_ref.refs_0_, bf16[512,4096]{1,0:T(8,128)(2,1)} %copy-done.10, f32[512,640]{1,0:T(8,128)S(1)} %get-tuple-element.238.refs_2_, bf16[512,640]{1,0:T(8,128)(2,1)S(1)} %collective-permute-done.26.refs_3_, f32[256,512]{1,0:T(8,128)S(1)} %shard_map.57.refs_4_, ...), custom_call_target="tpu_custom_call" | custom-call | flops 1 | bytes 1 | tf_op jit(solution)/shard_map/pallas_call | solution.py:33
  157.7 2.0 copy-done.7
  159.7 5.2 %all-to-all-start.1 = ((bf16[16,32,4096]{2,1,0:T(8,128)(2,1)}), bf16[16,32,4096]{2,1,0:T(8,128)(2,1)}, u32[]{:S(2)}, u32[]{:S(2)}) async-start(bf16[16,32,4096]{2,1,0:T(8,128)(2,1)} %bitcast.56), calls=%async_computation.1 | async-start | bytes 8388608 | tf_op jit(solution)/shard_map/all_to_all | solution.py:292
  164.9 0.7 fusion.10
  166.3 2.2 copy-done.3
  168.5 1.8 shard_map.61.refs_4_
  171.8 2.1 shard_map.60
  173.9 1.6 collective-permute-start.27
  175.5 1.4 convert_reduce_fusion.2
  180.1 7.8 %collective-permute-done.27.refs_3_ = bf16[128,640]{1,0:T(8,128)(2,1)S(1)} collective-permute-done((bf16[128,640]{1,0:T(8,128)(2,1)S(1)}, bf16[128,640]{1,0:T(8,128)(2,1)S(1)}, u32[]{:S(2)}, u32[]{:S(2)}) %collective-permute-start.27) | collective-permute-done | bytes 163872 | tf_op jit(solution)/shard_map/ppermute | solution.py:170
  187.9 2.2 copy-done.5
  190.1 2.2 shard_map.62
  192.3 76.5 %conditional.1 = (bf16[32,4096]{1,0:T(8,128)(2,1)S(1)}) conditional(s32[]{:T(128)} %clamp.3, (s32[]{:T(128)}, bf16[128,4096]{1,0:T(8,128)(2,1)S(1)}) %tuple.47, (s32[]{:T(128)}, bf16[128,4096]{1,0:T(8,128)(2,1)S(1)}) %tuple.47, (s32[]{:T(128)}, bf16[128,4096]{1,0:T(8,128)(2,1)S(1)}) %tuple.47, (s32[]{:T(128)}, ...), branch_computations={%region_8.9_spmd, %region_9.10_spmd, %region_10.11_spmd, %region_1... | conditional | flops 524289 | bytes 10223782 | solution.py:374
  192.3 1.0 copy-done.15
  194.8 1.3 collective-permute-start.5
  196.1 71.7 %collective-permute-done.5 = bf16[32,4096]{1,0:T(8,128)(2,1)S(1)} collective-permute-done((bf16[32,4096]{1,0:T(8,128)(2,1)S(1)}, bf16[32,4096]{1,0:T(8,128)(2,1)S(1)}, u32[]{:S(2)}, u32[]{:S(2)}) %collective-permute-start.5) | collective-permute-done | bytes 262176 | tf_op jit(solution)/shard_map/cond/branch_1_fun/ppermute | solution.py:368
  267.8 1.0 add_add_fusion.1
  268.8 6.7 %shard_map.63 = bf16[512,4096]{1,0:T(8,128)(2,1)} custom-call(s32[512,1]{1,0:T(8,128)S(1)} %copy.18.refs_0_, s32[512,1]{1,0:T(8,128)S(1)} %copy.19.refs_1_, bf16[512,4096]{1,0:T(8,128)(2,1)} %bitcast.20.refs_2_, bf16[32,4096]{1,0:T(8,128)(2,1)S(1)} %get-tuple-element.453.refs_3_), custom_call_target="tpu_custom_call" | custom-call | flops 1 | bytes 1 | tf_op jit(solution)/shard_map/pallas_call | solution.py:33
  (77 shorter events, 8.8 us)
Async XLA Ops:
  8.3 8.8 %collective-permute-start.14 = (s32[2,16]{1,0:T(2,128)S(1)}, s32[2,16]{1,0:T(2,128)S(1)}, u32[]{:S(2)}, u32[]{:S(2)}) collective-permute-start(s32[2,16]{1,0:T(2,128)S(1)} %pad_add_fusion.1), channel_id=1, source_target_pairs={{0,2},{2,0},{4,6},{6,4},{8,10},{10,8},{12,14},{14,12},{16,18},{18,... | collective-permute-start | bytes 392 | tf_op jit(solution)/shard_map/ppermute | solution.py:288
  8.3 8.7 %collective-permute-start.15 = (s32[2,16]{1,0:T(2,128)S(1)}, s32[2,16]{1,0:T(2,128)S(1)}, u32[]{:S(2)}, u32[]{:S(2)}) collective-permute-start(s32[2,16]{1,0:T(2,128)S(1)} %pad_add_fusion.1), channel_id=1, source_target_pairs={{0,4},{2,6},{4,0},{6,2},{8,12},{10,14},{12,8},{14,10},{16,20},{18,... | collective-permute-start | bytes 392 | tf_op jit(solution)/shard_map/ppermute | solution.py:288
  9.9 7.1 %collective-permute-start.16 = (s32[2,16]{1,0:T(2,128)S(1)}, s32[2,16]{1,0:T(2,128)S(1)}, u32[]{:S(2)}, u32[]{:S(2)}) collective-permute-start(s32[2,16]{1,0:T(2,128)S(1)} %pad_add_fusion.1), channel_id=1, source_target_pairs={{0,6},{2,4},{4,2},{6,0},{8,14},{10,12},{12,10},{14,8},{16,22},{18,... | collective-permute-start | bytes 392 | tf_op jit(solution)/shard_map/ppermute | solution.py:288
  10.6 4.4 %copy-start.21 = (pred[512]{0:T(512)(128)(4,1)}, pred[512]{0:T(512)(128)(4,1)S(1)}, u32[]{:S(2)}) copy-start(pred[512]{0:T(512)(128)(4,1)S(1)} %fusion.5) | copy-start | bytes 1540
  15.0 2.0 copy-start.6
  17.1 6.4 %copy-start.18 = (bf16[1,4,64,4096]{3,2,1,0:T(8,128)(2,1)S(1)}, bf16[1,4,64,4096]{3,2,1,0:T(8,128)(2,1)}, u32[]{:S(2)}) copy-start(bf16[1,4,64,4096]{3,2,1,0:T(8,128)(2,1)} %param.15) | copy-start | bytes 6291460
  17.1 99.8 %all-to-all-start = ((bf16[16,32,4096]{2,1,0:T(8,128)(2,1)}), bf16[16,32,4096]{2,1,0:T(8,128)(2,1)}, u32[]{:S(2)}, u32[]{:S(2)}) async-start(bf16[16,32,4096]{2,1,0:T(8,128)(2,1)} %bitcast.55), calls=%async_computation | async-start | bytes 8388608 | tf_op jit(solution)/shard_map/all_to_all | solution.py:292
  23.4 142.9 %all-gather.2.cloned.1.call-start = ((), (), s32[]{:S(2)}) async-start(), calls=%async_computation.2 | async-start | bytes 5242880 | tf_op jit(solution)/shard_map/all_gather | solution.py:333
  25.5 2.0 copy-start.10
  27.6 4.4 %collective-permute-start.17 = (bf16[2,128,4096]{2,1,0:T(8,128)(2,1)S(1)}, bf16[2,128,4096]{2,1,0:T(8,128)(2,1)}, u32[]{:S(2)}, u32[]{:S(2)}) collective-permute-start(bf16[2,128,4096]{2,1,0:T(8,128)(2,1)S(1)} %dynamic-slice_bitcast_fusion), channel_id=1, source_target_pairs={{0,2},{2,0},{4,6},{6,4},{8,10},{10,8},{12,14},{14,12},{16,18},{18,... | collective-permute-start | bytes 6291464 | tf_op jit(solution)/shard_map/ppermute | solution.py:322
  30.5 5.8 %copy-start.11 = (bf16[512,4096]{1,0:T(8,128)(2,1)S(1)}, bf16[512,4096]{1,0:T(8,128)(2,1)}, u32[]{:S(2)}) copy-start(bf16[512,4096]{1,0:T(8,128)(2,1)} %copy-done.10) | copy-start | bytes 12582916
  34.8 43.5 %collective-permute-start.18 = (bf16[1,128,4096]{2,1,0:T(8,128)(2,1)}, bf16[1,128,4096]{2,1,0:T(8,128)(2,1)}, u32[]{:S(2)}, u32[]{:S(2)}) collective-permute-start(bf16[1,128,4096]{2,1,0:T(8,128)(2,1)} %constant_dynamic-slice_fusion), channel_id=1, source_target_pairs={{0,4},{2,6},{4,0},{6,2},{8,12},{10,14},{12,8},{14,10},{16,20},{18,... | collective-permute-start | bytes 3145736 | tf_op jit(solution)/shard_map/ppermute | solution.py:322
  38.1 78.0 %collective-permute-start.22 = (f32[256,512]{1,0:T(8,128)S(1)}, f32[256,512]{1,0:T(8,128)S(1)}, u32[]{:S(2)}, u32[]{:S(2)}) collective-permute-start(f32[256,512]{1,0:T(8,128)S(1)} %shard_map.57.refs_4_), channel_id=1, source_target_pairs={{0,1},{1,0},{2,3},{3,2},{4,5},{5,4},{6,7},{7,6},{8,9},{9,8},{10,11... | collective-permute-start | bytes 1572872 | tf_op jit(solution)/shard_map/ppermute | solution.py:20
  41.0 53.8 %copy-start.20 = (s32[3,16]{1,0:T(4,128)}, s32[3,16]{1,0:T(4,128)S(1)}, u32[]{:S(2)}) copy-start(s32[3,16]{1,0:T(4,128)S(1)} %pad_add_fusion) | copy-start | bytes 580
  79.5 15.3 %collective-permute-start.19 = (s32[3,16]{1,0:T(4,128)S(1)}, s32[3,16]{1,0:T(4,128)S(1)}, u32[]{:S(2)}, u32[]{:S(2)}) collective-permute-start(s32[3,16]{1,0:T(4,128)S(1)} %pad_add_fusion), channel_id=1, source_target_pairs={{0,8},{2,10},{4,12},{6,14},{8,0},{10,2},{12,4},{14,6},{16,24},{18,... | collective-permute-start | bytes 584 | tf_op jit(solution)/shard_map/ppermute | solution.py:288
  90.6 23.8 %collective-permute-start.20 = (s32[3,16]{1,0:T(4,128)S(1)}, s32[3,16]{1,0:T(4,128)S(1)}, u32[]{:S(2)}, u32[]{:S(2)}) collective-permute-start(s32[3,16]{1,0:T(4,128)S(1)} %pad_add_fusion), channel_id=1, source_target_pairs={{0,16},{2,18},{4,20},{6,22},{8,24},{10,26},{12,28},{14,30},{16,0},... | collective-permute-start | bytes 584 | tf_op jit(solution)/shard_map/ppermute | solution.py:288
  90.6 24.8 %collective-permute-start.21 = (s32[3,16]{1,0:T(4,128)S(1)}, s32[3,16]{1,0:T(4,128)S(1)}, u32[]{:S(2)}, u32[]{:S(2)}) collective-permute-start(s32[3,16]{1,0:T(4,128)S(1)} %pad_add_fusion), channel_id=1, source_target_pairs={{0,24},{2,26},{4,28},{6,30},{8,16},{10,18},{12,20},{14,22},{16,8},... | collective-permute-start | bytes 584 | tf_op jit(solution)/shard_map/ppermute | solution.py:288
  116.0 0.8 copy-start.8
  122.9 28.0 %collective-permute-start.26 = (bf16[512,640]{1,0:T(8,128)(2,1)}, bf16[512,640]{1,0:T(8,128)(2,1)S(1)}, u32[]{:S(2)}, u32[]{:S(2)}) collective-permute-start(bf16[512,640]{1,0:T(8,128)(2,1)} %get-tuple-element.239), channel_id=1, source_target_pairs={{0,1},{1,0},{2,3},{3,2},{4,5},{5,4},{6,7},{7,6},{8,9},{9,8},{10,11... | collective-permute-start | bytes 1966088 | tf_op jit(solution)/shard_map/ppermute | solution.py:170
  125.1 10.6 %collective-permute-start.23 = (bf16[32,4096]{1,0:T(8,128)(2,1)S(1)}, bf16[32,4096]{1,0:T(8,128)(2,1)S(1)}, u32[]{:S(2)}, u32[]{:S(2)}) collective-permute-start(bf16[32,4096]{1,0:T(8,128)(2,1)S(1)} %get-tuple-element.323), channel_id=1, source_target_pairs={{0,8},{2,10},{4,12},{6,14},{8,0},{10,2},{12,4},{14,6},{16,24},{18,... | collective-permute-start | bytes 786440 | tf_op jit(solution)/shard_map/ppermute | solution.py:340
  126.6 19.5 %collective-permute-start.24 = (bf16[32,4096]{1,0:T(8,128)(2,1)S(1)}, bf16[32,4096]{1,0:T(8,128)(2,1)S(1)}, u32[]{:S(2)}, u32[]{:S(2)}) collective-permute-start(bf16[32,4096]{1,0:T(8,128)(2,1)S(1)} %get-tuple-element.322), channel_id=1, source_target_pairs={{0,16},{2,18},{4,20},{6,22},{8,24},{10,26},{12,28},{14,30},{16,0},... | collective-permute-start | bytes 786440 | tf_op jit(solution)/shard_map/ppermute | solution.py:340
  128.1 22.8 %collective-permute-start.25 = (bf16[32,4096]{1,0:T(8,128)(2,1)S(1)}, bf16[32,4096]{1,0:T(8,128)(2,1)S(1)}, u32[]{:S(2)}, u32[]{:S(2)}) collective-permute-start(bf16[32,4096]{1,0:T(8,128)(2,1)S(1)} %get-tuple-element.321), channel_id=1, source_target_pairs={{0,24},{2,26},{4,28},{6,30},{8,16},{10,18},{12,20},{14,22},{16,8},... | collective-permute-start | bytes 786440 | tf_op jit(solution)/shard_map/ppermute | solution.py:340
  150.9 1.0 copy-start.9
  157.6 2.0 copy-start.7
  159.7 5.9 %copy-start.22 = (pred[512]{0:T(512)(128)(4,1)S(1)}, pred[512]{0:T(512)(128)(4,1)}, u32[]{:S(2)}) copy-start(pred[512]{0:T(512)(128)(4,1)} %copy-done.21) | copy-start | bytes 1540
  159.7 11.3 %copy-start.19 = (bf16[32,4096]{1,0:T(8,128)(2,1)S(1)}, bf16[32,4096]{1,0:T(8,128)(2,1)}, u32[]{:S(2)}) copy-start(bf16[32,4096]{1,0:T(8,128)(2,1)} %get-tuple-element.244) | copy-start | bytes 786436
  159.7 109.2 %all-to-all-start.1 = ((bf16[16,32,4096]{2,1,0:T(8,128)(2,1)}), bf16[16,32,4096]{2,1,0:T(8,128)(2,1)}, u32[]{:S(2)}, u32[]{:S(2)}) async-start(bf16[16,32,4096]{2,1,0:T(8,128)(2,1)} %bitcast.56), calls=%async_computation.1 | async-start | bytes 8388608 | tf_op jit(solution)/shard_map/all_to_all | solution.py:292
  166.3 2.2 copy-start.3
  168.5 3.3 %copy-start.4 = (bf16[512,4096]{1,0:T(8,128)(2,1)S(1)}, bf16[512,4096]{1,0:T(8,128)(2,1)}, u32[]{:S(2)}) copy-start(bf16[512,4096]{1,0:T(8,128)(2,1)} %all-gather.2.cloned.1.call-done.weights_ref.refs_1_) | copy-start | bytes 12582916
  170.4 17.6 %collective-permute-start.28 = (f32[256,512]{1,0:T(8,128)S(1)}, f32[256,512]{1,0:T(8,128)S(1)}, u32[]{:S(2)}, u32[]{:S(2)}) collective-permute-start(f32[256,512]{1,0:T(8,128)S(1)} %shard_map.61.refs_4_), channel_id=1, source_target_pairs={{0,1},{1,0},{2,3},{3,2},{4,5},{5,4},{6,7},{7,6},{8,9},{9,8},{10,11... | collective-permute-start | bytes 1572872 | tf_op jit(solution)/shard_map/ppermute | solution.py:20
  173.9 14.0 %collective-permute-start.27 = (bf16[128,640]{1,0:T(8,128)(2,1)S(1)}, bf16[128,640]{1,0:T(8,128)(2,1)S(1)}, u32[]{:S(2)}, u32[]{:S(2)}) collective-permute-start(bf16[128,640]{1,0:T(8,128)(2,1)S(1)} %get-tuple-element.250), channel_id=1, source_target_pairs={{0,1},{1,0},{2,3},{3,2},{4,5},{5,4},{6,7},{7,6},{8,9},{9,8},{10,11... | collective-permute-start | bytes 491528 | tf_op jit(solution)/shard_map/ppermute | solution.py:170
  187.9 2.2 copy-start.5
  192.3 1.1 copy-start.15
  193.4 2.7 collective-permute-start.3
  194.1 2.0 collective-permute-start.4
  194.8 73.0 %collective-permute-start.5 = (bf16[32,4096]{1,0:T(8,128)(2,1)S(1)}, bf16[32,4096]{1,0:T(8,128)(2,1)S(1)}, u32[]{:S(2)}, u32[]{:S(2)}) collective-permute-start(bf16[32,4096]{1,0:T(8,128)(2,1)S(1)} %get-tuple-element.313), channel_id=1, source_target_pairs={{8,16},{10,18},{12,20},{14,22},{9,17},{11,19},{13,21},{15,23}} | collective-permute-start | bytes 786440 | tf_op jit(solution)/shard_map/cond/branch_1_fun/ppermute | solution.py:368
Sparse Core Ops, SparseCore 0:
  124.5 34.3 all-gather.1

commit v3 on v2

--- a/solution.py
+++ b/solution.py
@@ -11,7 +11,6 @@
 epsilon = 1e-05
 F32 = jnp.float32
 BF16 = jnp.bfloat16
-VMEM_BYTES = 40 * 2**20
 
 
 def parts_mp(value):
@@ -21,76 +20,127 @@
     return [lax.psum(value, "mp")]
 
 
-def whole(array):
-    return pl.BlockSpec(array.shape, lambda step: (0,) * array.ndim)
-
-
-def columns(rows, tile, part=0):
-    return pl.BlockSpec((rows, tile), lambda step: (part, step))
-
-
-def call(body, outs, out_specs, operands, in_specs, steps, scratch=(), aliases=None):
+def tiling(width):
+    tile = math.gcd(width, 1024)
+    return [pl.ds(step * tile, tile) for step in range(width // tile)]
+
+
+def call(body, outs, operands, streamed, scratch, vmem=40):
+    in_specs = [
+        pl.BlockSpec(memory_space=pl.ANY if step in streamed else pltpu.VMEM)
+        for step in range(len(operands))
+    ]
+    out_specs = [
+        pl.BlockSpec(memory_space=pltpu.HBM if wide else pltpu.VMEM) for _, wide in outs
+    ]
     return pl.pallas_call(
         body,
-        grid=(steps,),
-        out_shape=outs,
+        out_shape=[out for out, _ in outs],
         in_specs=in_specs,
         out_specs=out_specs,
         scratch_shapes=list(scratch),
-        input_output_aliases=aliases or {},
-        compiler_params=pltpu.CompilerParams(vmem_limit_bytes=VMEM_BYTES),
+        compiler_params=pltpu.CompilerParams(vmem_limit_bytes=vmem * 2**20),
         cost_estimate=pl.CostEstimate(flops=1, bytes_accessed=1, transcendentals=0),
     )(*operands)
 
 
-def tiling(width):
-    tile = math.gcd(width, 2048)
-    return tile, width // tile
+def start_all(sources, targets, sems, tiles):
+    copies = []
+    for step, at in enumerate(tiles):
+        copies.append([])
+        for number, (source, target) in enumerate(zip(sources, targets)):
+            copy = pltpu.make_async_copy(
+                source.at[:, at], target.at[:, at], sems.at[number, step]
+            )
+            copy.start()
+            copies[-1].append(copy)
+    return copies
+
+
+def wait_all(copies):
+    for copy in copies:
+        copy.wait()
 
 
 def pack(target, hidden, total):
     count, width = hidden.shape
-    tile, steps = tiling(width)
-
-    def body(target_ref, hidden_ref, out_ref):
+    tiles = tiling(width)
+
+    def body(target_ref, hidden_ref, out_ref, hidden_buf, out_buf, in_sems, out_sems):
+        copies = start_all([hidden_ref], [hidden_buf], in_sems, tiles)
         at = lax.broadcasted_iota(jnp.int32, (total, count), 0)
         hot = (at == target_ref[...]).astype(F32).astype(BF16)
-        out_ref[...] = jnp.dot(hot, hidden_ref[...], preferred_element_type=F32).astype(BF16)
-
-    target = target.reshape(1, count)
+        sent = []
+        for step, tile in enumerate(tiles):
+            wait_all(copies[step])
+            out_buf[:, tile] = jnp.dot(
+                hot, hidden_buf[:, tile], preferred_element_type=F32
+            ).astype(BF16)
+            sent.append(
+                pltpu.make_async_copy(
+                    out_buf.at[:, tile], out_ref.at[:, tile], out_sems.at[0, step]
+                )
+            )
+            sent[-1].start()
+        wait_all(sent)
+
     return call(
         body,
-        jax.ShapeDtypeStruct((total, width), BF16),
-        columns(total, tile),
-        (target, hidden),
-        [whole(target), columns(count, tile)],
-        steps,
-    )
+        [(jax.ShapeDtypeStruct((total, width), BF16), True)],
+        (target.reshape(1, count), hidden),
+        [1],
+        [
+            pltpu.VMEM((count, width), BF16),
+            pltpu.VMEM((total, width), BF16),
+            pltpu.SemaphoreType.DMA((1, len(tiles))),
+            pltpu.SemaphoreType.DMA((1, len(tiles))),
+        ],
+        vmem=60,
+    )[0]
 
 
 def unpack(targets, arrays):
     count = targets[0].shape[0]
     width = arrays[0].shape[1]
-    tile, steps = tiling(width)
+    tiles = tiling(width)
+    kinds = len(arrays)
 
     def body(*refs):
-        target_refs, array_refs, out_ref = refs[: len(arrays)], refs[len(arrays) : -1], refs[-1]
-        total = jnp.zeros((count, tile), F32)
+        target_refs, array_refs, out_ref = refs[:kinds], refs[kinds : 2 * kinds], refs[2 * kinds]
+        buffers, out_buf, in_sems, out_sems = refs[2 * kinds + 1 : -3], *refs[-3:]
+        copies = start_all(array_refs, buffers, in_sems, tiles)
+        hots = []
         for target_ref, array_ref in zip(target_refs, array_refs):
             at = lax.broadcasted_iota(jnp.int32, (count, array_ref.shape[0]), 1)
-            hot = (at == target_ref[...]).astype(F32).astype(BF16)
-            total = total + jnp.dot(hot, array_ref[...], preferred_element_type=F32)
-        out_ref[...] = total.astype(BF16)
-
-    targets = [target.reshape(count, 1) for target in targets]
+            hots.append((at == target_ref[...]).astype(F32).astype(BF16))
+        sent = []
+        for step, tile in enumerate(tiles):
+            wait_all(copies[step])
+            total = sum(
+                jnp.dot(hot, buffer[:, tile], preferred_element_type=F32)
+                for hot, buffer in zip(hots, buffers)
+            )
+            out_buf[:, tile] = total.astype(BF16)
+            sent.append(
+                pltpu.make_async_copy(
+                    out_buf.at[:, tile], out_ref.at[:, tile], out_sems.at[0, step]
+                )
+            )
+            sent[-1].start()
+        wait_all(sent)
+
     return call(
         body,
-        jax.ShapeDtypeStruct((count, width), BF16),
-        columns(count, tile),
-        (*targets, *arrays),
-        [whole(t) for t in targets] + [columns(a.shape[0], tile) for a in arrays],
-        steps,
-    )
+        [(jax.ShapeDtypeStruct((count, width), BF16), True)],
+        (*[target.reshape(count, 1) for target in targets], *arrays),
+        range(kinds, 2 * kinds),
+        [pltpu.VMEM(array.shape, BF16) for array in arrays]
+        + [
+            pltpu.VMEM((count, width), BF16),
+            pltpu.SemaphoreType.DMA((kinds, len(tiles))),
+            pltpu.SemaphoreType.DMA((1, len(tiles))),
+        ],
+    )[0]
 
 
 def sketch_weights(down, up):
@@ -106,62 +156,66 @@
 def gram(weights):
     total, width = weights.shape
     half = total // 2
-    tile, steps = tiling(width)
-
-    def body(weights_ref, out_ref):
-        @pl.when(pl.program_id(0) == 0)
-        def _():
-            out_ref[...] = jnp.zeros_like(out_ref)
-
-        out_ref[...] += against(weights_ref[half:, :], weights_ref[...])
+    tiles = tiling(width)
+
+    def body(weights_ref, out_ref, weights_buf, sems):
+        copies = start_all([weights_ref], [weights_buf], sems, tiles)
+        for step, tile in enumerate(tiles):
+            wait_all(copies[step])
+            values = weights_buf[:, tile]
+            product = against(values[half:], values)
+            out_ref[...] = product if step == 0 else out_ref[...] + product
 
     return call(
         body,
-        jax.ShapeDtypeStruct((half, total), F32),
-        pl.BlockSpec((half, total), lambda step: (0, 0)),
+        [(jax.ShapeDtypeStruct((half, total), F32), False)],
         (weights,),
-        [columns(total, tile)],
-        steps,
-    )
-
-
-def sketch(rows, weights, part=0, parts=1):
+        [0],
+        [pltpu.VMEM((total, width), BF16), pltpu.SemaphoreType.DMA((1, len(tiles)))],
+    )[0]
+
+
+def sketch(rows, weights):
     count, width = rows.shape
-    count //= parts
     total = weights.shape[0]
-    tile, steps = tiling(width)
-
-    def body(rows_ref, weights_ref, out_ref, narrow_ref):
-        step = pl.program_id(0)
-
-        @pl.when(step == 0)
-        def _():
-            out_ref[...] = jnp.zeros_like(out_ref)
-
-        values = rows_ref[...]
-        out_ref[:, :total] += against(values, weights_ref[...])
-        widened = values.astype(F32)
-        out_ref[:, total:] += jnp.sum(widened * widened, axis=1, keepdims=True)
-
-        @pl.when(step == steps - 1)
-        def _():
-            narrow_ref[:, :total] = out_ref[:, :total].astype(BF16)
-            squares = out_ref[:, total:]
-            column = lax.broadcasted_iota(jnp.int32, squares.shape, 1)
-            first = squares.astype(BF16).astype(F32)
-            second = (squares - first).astype(BF16).astype(F32)
-            third = squares - first - second
-            terms = jnp.where(column == 0, first, jnp.where(column == 1, second, third))
-            narrow_ref[:, total:] = jnp.where(column < 3, terms, 0.0).astype(BF16)
+    tiles = tiling(width)
+
+    def body(rows_ref, weights_ref, out_ref, narrow_ref, rows_buf, weights_buf, sems):
+        copies = start_all([rows_ref, weights_ref], [rows_buf, weights_buf], sems, tiles)
+        for step, tile in enumerate(tiles):
+            wait_all(copies[step])
+            values = rows_buf[:, tile]
+            product = against(values, weights_buf[:, tile])
+            widened = values.astype(F32)
+            squares = jnp.broadcast_to(
+                jnp.sum(widened * widened, axis=1, keepdims=True), (count, 128)
+            )
+            if step == 0:
+                out_ref[:, :total] = product
+                out_ref[:, total:] = squares
+            else:
+                out_ref[:, :total] += product
+                out_ref[:, total:] += squares
+        narrow_ref[:, :total] = out_ref[:, :total].astype(BF16)
+        squares = out_ref[:, total:]
+        column = lax.broadcasted_iota(jnp.int32, squares.shape, 1)
+        first = squares.astype(BF16).astype(F32)
+        second = (squares - first).astype(BF16).astype(F32)
+        third = squares - first - second
+        terms = jnp.where(column == 0, first, jnp.where(column == 1, second, third))
+        narrow_ref[:, total:] = jnp.where(column < 3, terms, 0.0).astype(BF16)
 
     shape = (count, total + 128)
     return call(
         body,
-        [jax.ShapeDtypeStruct(shape, F32), jax.ShapeDtypeStruct(shape, BF16)],
-        [pl.BlockSpec(shape, lambda step: (0, 0))] * 2,
+        [(jax.ShapeDtypeStruct(shape, F32), False), (jax.ShapeDtypeStruct(shape, BF16), False)],
         (rows, weights),
-        [columns(count, tile, part), columns(total, tile)],
-        steps,
+        [0, 1],
+        [
+            pltpu.VMEM((count, width), BF16),
+            pltpu.VMEM((total, width), BF16),
+            pltpu.SemaphoreType.DMA((2, len(tiles))),
+        ],
     )
 
 
@@ -207,41 +261,48 @@
     return low.astype(BF16)
 
 
-def finish(rows, sketched, tables, weights, layers, model_width, part=0, parts=1, filled=None):
-    whole_count, width = rows.shape
-    count = whole_count // parts
+def finish(rows, sketched, tables, weights, layers, model_width):
+    count, width = rows.shape
     half = weights.shape[0] // 2
-    tile, steps = tiling(width)
-
-    filled = [] if filled is None else [filled]
+    tiles = tiling(width)
 
     def body(*refs):
-        rows_ref, up_ref = refs[:2]
+        rows_ref, weights_ref = refs[:2]
         sketch_refs = refs[2 : 2 + len(sketched)]
         table_refs = refs[2 + len(sketched) :][: len(tables)]
-        out_ref, low_ref = refs[-2:]
-
-        @pl.when(pl.program_id(0) == 0)
-        def _():
-            whole_sketch = sum(widen(ref[...], 2 * half) for ref in sketch_refs)
-            whole_table = sum(ref[...] for ref in table_refs)
-            low_ref[...] = low_rank(whole_sketch, whole_table, layers, model_width)
-
-        update = jnp.dot(low_ref[...], up_ref[...], preferred_element_type=F32)
-        out_ref[...] = (rows_ref[...].astype(F32) + update).astype(BF16)
+        out_ref, rows_buf, up_buf, out_buf, in_sems, out_sems = refs[-6:]
+        up_ref = weights_ref.at[pl.ds(half, half), :]
+        copies = start_all([rows_ref, up_ref], [rows_buf, up_buf], in_sems, tiles)
+        whole_sketch = sum(widen(ref[...], 2 * half) for ref in sketch_refs)
+        whole_table = sum(ref[...] for ref in table_refs)
+        low = low_rank(whole_sketch, whole_table, layers, model_width)
+        sent = []
+        for step, tile in enumerate(tiles):
+            wait_all(copies[step])
+            update = jnp.dot(low, up_buf[:, tile], preferred_element_type=F32)
+            out_buf[:, tile] = (rows_buf[:, tile].astype(F32) + update).astype(BF16)
+            sent.append(
+                pltpu.make_async_copy(
+                    out_buf.at[:, tile], out_ref.at[:, tile], out_sems.at[0, step]
+                )
+            )
+            sent[-1].start()
+        wait_all(sent)
 
     return call(
         body,
-        jax.ShapeDtypeStruct((whole_count, width), BF16),
-        columns(count, tile, part),
-        (rows, weights, *sketched, *tables, *filled),
-        [columns(count, tile, part), columns(half, tile, 1)]
-        + [whole(a) for a in (*sketched, *tables)]
-        + [pl.BlockSpec(memory_space=pl.ANY) for _ in filled],
-        steps,
-        scratch=[pltpu.VMEM((count, half), BF16)],
-        aliases={2 + len(sketched) + len(tables): 0} if filled else None,
-    )
+        [(jax.ShapeDtypeStruct((count, width), BF16), True)],
+        (rows, weights, *sketched, *tables),
+        [0, 1],
+        [
+            pltpu.VMEM((count, width), BF16),
+            pltpu.VMEM((half, width), BF16),
+            pltpu.VMEM((count, width), BF16),
+            pltpu.SemaphoreType.DMA((2, len(tiles))),
+            pltpu.SemaphoreType.DMA((1, len(tiles))),
+        ],
+        vmem=60,
+    )[0]
 
 
 def adapt(rows, weights, tables, layers, model_width):
@@ -325,27 +386,28 @@
     mine = mine.reshape(rows_left, width)
     mine, tallies = lax.optimization_barrier((mine, tallies))
     tallies = add_over(tallies, range(group, owners, group))
-    mine, tallies, over_packed, arrived, *table = lax.optimization_barrier(
-        (mine, tallies, over_packed, arrived, *table)
-    )
+
+    over_blocks = over_packed.reshape(planes, slot_rows, width)
+
+    def to_plane(step, block):
+        return lax.ppermute(block, "dp", [(i, i ^ (step * group)) for i in range(owners)])
+
+    over_arrived = [over_blocks[0]] + [to_plane(step, over_blocks[step]) for step in range(1, 2)]
+    mine, tallies, over_blocks, arrived, *rest = lax.optimization_barrier(
+        (mine, tallies, over_blocks, arrived, *over_arrived, *table)
+    )
+    over_arrived, table = rest[: len(over_arrived)], rest[len(over_arrived) :]
 
     groups = [[p * group + q for q in range(group)] for p in range(planes)]
     plane_weights = lax.all_gather(mine, "dp", axis_index_groups=groups, tiled=True)
 
-    def swap_planes(rows):
-        blocks = rows.reshape(planes, slot_rows, width)
-        moved = [blocks[0]]
-        for step in range(1, planes):
-            pairs = [(i, i ^ (step * group)) for i in range(owners)]
-            moved.append(lax.ppermute(blocks[step], "dp", pairs))
-        return moved
-
     sketched, narrow = sketch(arrived, weights)
-    narrow, over_packed = lax.optimization_barrier((narrow, over_packed))
     sketched = sketch_parts(sketched, narrow)
-    over_arrived = swap_planes(over_packed)
-    *over_arrived, sketched[0] = lax.optimization_barrier((*over_arrived, sketched[0]))
+    later = [to_plane(step, over_blocks[step]) for step in range(2, planes)]
+    *later[:-1], sketched[0] = lax.optimization_barrier((*later[:-1], sketched[0]))
     done = finish(arrived, sketched, table, weights, layers, model_width)
+    *later, done = lax.optimization_barrier((*later, done))
+    over_arrived = over_arrived + later
 
     returned = [exchange(done)]
     plane_weights, over_arrived[0], done = lax.optimization_barrier(

time: 284 us -> 275 us (0.968)
  waiting for transfers between devices: 161 us -> 145 us
  starting transfers between devices: 39.1 us -> 44.7 us
  Pallas kernels: 33.4 us -> 38.7 us
  local copies, waits for them, and re-layouts: 15.9 us -> 11.3 us
    ppermute x2, waiting for transfers between devices: 38.7 us -> 31.2 us  [local(): taken = lax.ppermute(give, 'dp', [(i, i ^ step) for i in range(owners)])]
    ppermute x3, waiting for transfers between devices: 22.3 us -> 15.6 us  [to_plane(): lax.ppermute(block, 'dp', [(i, i ^ step * group) for i in range(owners)])]
    pallas_call x9, Pallas kernels: 33.4 us -> 38.7 us  [call(): pl.pallas_call(body, out_shape=[out for out, _ in outs], in_specs=in_spec...]
    ppermute x3, waiting for transfers between devices: 71.7 us -> 67.5 us  [moved(): got.append(lax.ppermute(blocks[step], 'dp', pairs))]
    unnamed x31 -> x35, local copies, waits for them, and re-layouts: 12.3 us -> 8.66 us
    ppermute x3, starting transfers between devices: 2.65 us -> 6.02 us  [moved(): got.append(lax.ppermute(blocks[step], 'dp', pairs))]
  transfers between devices with their start and end apart: 21 -> 21, of which waited for: 9 -> 10; matrix products, arithmetic and copies ran while one was open for 5% -> 5% of each run, Pallas kernels for 7% -> 10%
where the time goes in v3:
time: 275 us; the launch traced here: 272 us
  waiting for transfers between devices  145 us (53%)
  starting transfers between devices  44.7 us (16%)
  Pallas kernels  38.7 us (14%)
  between operations  19.9 us (7%)
  other arithmetic  12.5 us (5%)
  local copies, waits for them, and re-layouts  11.3 us (4%)
    ppermute x3, waiting for transfers between devices, moved(): got.append(lax.ppermute(blocks[step], 'dp', pairs))  67.5 us
    pallas_call x9, Pallas kernels, call(): pl.pallas_call(body, out_shape=[out for out, _ in outs], in_specs=in_spec...  38.7 us
    ppermute x2, waiting for transfers between devices, local(): taken = lax.ppermute(give, 'dp', [(i, i ^ step) for i in range(owners)])  31.2 us
    ppermute x6, waiting for transfers between devices, add_over(): return value + sum((lax.ppermute(value, 'dp', p) for p in pairs))  23.4 us
    ppermute x3, waiting for transfers between devices, to_plane(): lax.ppermute(block, 'dp', [(i, i ^ step * group) for i in range(owners)])  15.6 us
    ppermute x6, starting transfers between devices, add_over(): return value + sum((lax.ppermute(value, 'dp', p) for p in pairs))  14.5 us
    all_to_all x2, starting transfers between devices, exchange(): lax.all_to_all(blocks, 'dp', 0, 0, tiled=True)  14 us
    unnamed x35, local copies, waits for them, and re-layouts  8.66 us
  transfers between devices with their start and end apart: 21, of which 10 were waited for; matrix products, arithmetic and copies ran while one was open for 5% of the time, Pallas kernels for 10%

profile of v3, /device:TPU:16, one launch (start us, length us, event | category | flops | bytes accessed | tf_op | source)
XLA Modules:
  0.0 272.5 jit_solution(17669730654369304791)
XLA Ops:
  6.5 0.8 select_reduce_fusion
  8.3 1.6 collective-permute-start.15
  11.2 5.8 %shard_map.55 = bf16[512,4096]{1,0:T(8,128)(2,1)} custom-call(s32[1,512]{1,0:T(1,128)} %get-tuple-element.328.target_ref, bf16[512,4096]{1,0:T(8,128)(2,1)} %hidden_ref.3), custom_call_target="tpu_custom_call" | custom-call | flops 1 | bytes 1 | tf_op jit(solution)/shard_map/pallas_call | solution.py:36
  17.1 6.3 %all-to-all-start = ((bf16[16,32,4096]{2,1,0:T(8,128)(2,1)}), bf16[16,32,4096]{2,1,0:T(8,128)(2,1)}, u32[]{:S(2)}, u32[]{:S(2)}) async-start(bf16[16,32,4096]{2,1,0:T(8,128)(2,1)} %bitcast.62), calls=%async_computation | async-start | bytes 8388608 | tf_op jit(solution)/shard_map/all_to_all | solution.py:353
  23.7 1.9 pad_maximum_fusion.weights_ref.refs_1_
  25.6 2.0 copy-done.13
  27.9 3.9 %shard_map.56 = bf16[128,4096]{1,0:T(8,128)(2,1)} custom-call(s32[1,512]{1,0:T(1,128)} %get-tuple-element.327.target_ref, bf16[512,4096]{1,0:T(8,128)(2,1)} %hidden_ref.3), custom_call_target="tpu_custom_call" | custom-call | flops 1 | bytes 1 | tf_op jit(solution)/shard_map/pallas_call | solution.py:36
  34.8 2.6 bitcast_select_fusion
  37.4 1.1 constant_dynamic-slice_fusion
  38.5 1.5 collective-permute-start.18
  40.7 0.8 collective-permute-start.22
  41.5 2.6 shard_map.57.refs_4_
  44.1 1.6 collective-permute-start.23
  47.1 31.2 %collective-permute-done.18 = bf16[1,128,4096]{2,1,0:T(8,128)(2,1)} collective-permute-done((bf16[1,128,4096]{2,1,0:T(8,128)(2,1)}, bf16[1,128,4096]{2,1,0:T(8,128)(2,1)}, u32[]{:S(2)}, u32[]{:S(2)}) %collective-permute-start.18) | collective-permute-done | bytes 1048608 | tf_op jit(solution)/shard_map/ppermute | solution.py:383
  78.3 1.1 select_bitcast_fusion
  79.4 11.1 %collective-permute-start.19 = (s32[3,16]{1,0:T(4,128)S(1)}, s32[3,16]{1,0:T(4,128)S(1)}, u32[]{:S(2)}, u32[]{:S(2)}) collective-permute-start(s32[3,16]{1,0:T(4,128)S(1)} %pad_add_fusion), channel_id=1, source_target_pairs={{0,8},{2,10},{4,12},{6,14},{8,0},{10,2},{12,4},{14,6},{16,24},{18,... | collective-permute-start | bytes 584 | tf_op jit(solution)/shard_map/ppermute | solution.py:349
  90.5 1.5 collective-permute-start.21
  92.0 7.6 %collective-permute-done.19 = s32[3,16]{1,0:T(4,128)S(1)} collective-permute-done((s32[3,16]{1,0:T(4,128)S(1)}, s32[3,16]{1,0:T(4,128)S(1)}, u32[]{:S(2)}, u32[]{:S(2)}) %collective-permute-start.19) | collective-permute-done | bytes 224 | tf_op jit(solution)/shard_map/ppermute | solution.py:349
  99.6 14.9 %collective-permute-done.20 = s32[3,16]{1,0:T(4,128)S(1)} collective-permute-done((s32[3,16]{1,0:T(4,128)S(1)}, s32[3,16]{1,0:T(4,128)S(1)}, u32[]{:S(2)}, u32[]{:S(2)}) %collective-permute-start.20) | collective-permute-done | bytes 224 | tf_op jit(solution)/shard_map/ppermute | solution.py:349
  114.4 0.9 collective-permute-done.21
  115.4 0.8 all-to-all-done
  116.3 4.5 %shard_map.58 = (f32[512,640]{1,0:T(8,128)S(1)}, bf16[512,640]{1,0:T(8,128)(2,1)S(1)}) custom-call(bf16[512,4096]{1,0:T(8,128)(2,1)} %bitcast.16.rows_ref.refs_0_, bf16[512,4096]{1,0:T(8,128)(2,1)} %copy-done.13), custom_call_target="tpu_custom_call" | custom-call | flops 1 | bytes 1 | tf_op jit(solution)/shard_map/pallas_call | solution.py:36
  120.8 1.1 copy-done.11
  121.9 1.5 collective-permute-start.26
  123.5 1.7 collective-permute-start.24
  125.7 15.6 %collective-permute-done.24 = bf16[32,4096]{1,0:T(8,128)(2,1)S(1)} collective-permute-done((bf16[32,4096]{1,0:T(8,128)(2,1)S(1)}, bf16[32,4096]{1,0:T(8,128)(2,1)S(1)}, u32[]{:S(2)}, u32[]{:S(2)}) %collective-permute-start.24) | collective-permute-done | bytes 262176 | tf_op jit(solution)/shard_map/ppermute | solution.py:393
  141.3 0.8 copy-done.22
  142.2 6.7 %shard_map.59 = bf16[512,4096]{1,0:T(8,128)(2,1)} custom-call(bf16[512,4096]{1,0:T(8,128)(2,1)} %bitcast.16.rows_ref.refs_0_, bf16[512,4096]{1,0:T(8,128)(2,1)} %copy-done.13, f32[512,640]{1,0:T(8,128)} %copy-done.11, bf16[512,640]{1,0:T(8,128)(2,1)} %copy-done.22, f32[256,512]{1,0:T(8,128)} %copy-done.9, f32[256,512]{1,0:T(8,128)} %copy-done.24), custom_call_target="tpu_custom_call" | custom-call | flops 1 | bytes 1 | tf_op jit(solution)/shard_map/pallas_call | solution.py:36
  148.9 7.7 %all-to-all-start.1 = ((bf16[16,32,4096]{2,1,0:T(8,128)(2,1)}), bf16[16,32,4096]{2,1,0:T(8,128)(2,1)}, u32[]{:S(2)}, u32[]{:S(2)}) async-start(bf16[16,32,4096]{2,1,0:T(8,128)(2,1)} %bitcast.63), calls=%async_computation.1 | async-start | bytes 8388608 | tf_op jit(solution)/shard_map/all_to_all | solution.py:353
  158.0 2.2 copy-done.4
  160.2 2.6 shard_map.61.refs_4_
  162.8 0.8 collective-permute-start.28
  163.6 1.0 constant_dynamic-update-slice_fusion.2
  165.3 2.8 %shard_map.60 = (f32[128,640]{1,0:T(8,128)S(1)}, bf16[128,640]{1,0:T(8,128)(2,1)S(1)}) custom-call(bf16[128,4096]{1,0:T(8,128)(2,1)S(1)} %constant_dynamic-update-slice_fusion.rows_ref.refs_0_, bf16[512,4096]{1,0:T(8,128)(2,1)S(1)} %copy-done.5), custom_call_target="tpu_custom_call" | custom-call | flops 1 | bytes 1 | tf_op jit(solution)/shard_map/pallas_call | solution.py:36
  168.8 1.3 collective-permute-start.27
  170.1 1.3 convert_reduce_fusion.2
  174.4 5.9 %collective-permute-done.27.refs_3_ = bf16[128,640]{1,0:T(8,128)(2,1)S(1)} collective-permute-done((bf16[128,640]{1,0:T(8,128)(2,1)S(1)}, bf16[128,640]{1,0:T(8,128)(2,1)S(1)}, u32[]{:S(2)}, u32[]{:S(2)}) %collective-permute-start.27) | collective-permute-done | bytes 163872 | tf_op jit(solution)/shard_map/ppermute | solution.py:224
  180.3 0.8 copy-done.23
  181.2 3.7 %shard_map.62 = bf16[128,4096]{1,0:T(8,128)(2,1)S(1)} custom-call(bf16[128,4096]{1,0:T(8,128)(2,1)} %copy-done.7, bf16[512,4096]{1,0:T(8,128)(2,1)} %all-gather.2.cloned.1.call-done.weights_ref.refs_1_, f32[128,640]{1,0:T(8,128)} %copy-done.12, bf16[128,640]{1,0:T(8,128)(2,1)} %copy-done.26, f32[256,512]{1,0:T(8,128)} %copy-done.8, f32[256,512]{1,0:T(8,128)} %copy-done.23), custom_call_target="tpu_custom_call" | custom-call | flops 1 | bytes 1 | tf_op jit(solution)/shard_map/pallas_call | solution.py:36
  184.9 73.7 %conditional.1 = (bf16[32,4096]{1,0:T(8,128)(2,1)S(1)}) conditional(s32[]{:T(128)} %clamp.3, (s32[]{:T(128)}, bf16[128,4096]{1,0:T(8,128)(2,1)S(1)}) %tuple.47, (s32[]{:T(128)}, bf16[128,4096]{1,0:T(8,128)(2,1)S(1)}) %tuple.47, (s32[]{:T(128)}, bf16[128,4096]{1,0:T(8,128)(2,1)S(1)}) %tuple.47, (s32[]{:T(128)}, ...), branch_computations={%region_8.9_spmd, %region_9.10_spmd, %region_10.11_spmd, %region_1... | conditional | flops 524289 | bytes 6029450 | solution.py:436
  185.0 3.4 %collective-permute-start.6 = (bf16[32,4096]{1,0:T(8,128)(2,1)S(1)}, bf16[32,4096]{1,0:T(8,128)(2,1)S(1)}, u32[]{:S(2)}, u32[]{:S(2)}) collective-permute-start(bf16[32,4096]{1,0:T(8,128)(2,1)S(1)} %get-tuple-element.315), channel_id=1, source_target_pairs={{16,24},{18,26},{20,28},{22,30},{17,25},{19,27},{21,29},{23,31}} | collective-permute-start | bytes 786440 | tf_op jit(solution)/shard_map/cond/branch_2_fun/ppermute | solution.py:430
  188.4 1.3 collective-permute-start.7
  189.7 1.3 collective-permute-start.8
  191.1 16.6 %collective-permute-done.6 = bf16[32,4096]{1,0:T(8,128)(2,1)S(1)} collective-permute-done((bf16[32,4096]{1,0:T(8,128)(2,1)S(1)}, bf16[32,4096]{1,0:T(8,128)(2,1)S(1)}, u32[]{:S(2)}, u32[]{:S(2)}) %collective-permute-start.6) | collective-permute-done | bytes 262176 | tf_op jit(solution)/shard_map/cond/branch_2_fun/ppermute | solution.py:430
  207.7 45.8 %collective-permute-done.7 = bf16[32,4096]{1,0:T(8,128)(2,1)S(1)} collective-permute-done((bf16[32,4096]{1,0:T(8,128)(2,1)S(1)}, bf16[32,4096]{1,0:T(8,128)(2,1)S(1)}, u32[]{:S(2)}, u32[]{:S(2)}) %collective-permute-start.7) | collective-permute-done | bytes 262176 | tf_op jit(solution)/shard_map/cond/branch_2_fun/ppermute | solution.py:430
  253.5 5.1 %collective-permute-done.8 = bf16[32,4096]{1,0:T(8,128)(2,1)S(1)} collective-permute-done((bf16[32,4096]{1,0:T(8,128)(2,1)S(1)}, bf16[32,4096]{1,0:T(8,128)(2,1)S(1)}, u32[]{:S(2)}, u32[]{:S(2)}) %collective-permute-start.8) | collective-permute-done | bytes 262176 | tf_op jit(solution)/shard_map/cond/branch_2_fun/ppermute | solution.py:430
  258.7 6.1 %shard_map.63 = bf16[512,4096]{1,0:T(8,128)(2,1)} custom-call(s32[512,1]{1,0:T(8,128)S(1)} %copy.18.refs_0_, s32[512,1]{1,0:T(8,128)S(1)} %copy.19.refs_1_, bf16[512,4096]{1,0:T(8,128)(2,1)} %bitcast.23.refs_2_, bf16[32,4096]{1,0:T(8,128)(2,1)S(1)} %get-tuple-element.453.refs_3_), custom_call_target="tpu_custom_call" | custom-call | flops 1 | bytes 1 | tf_op jit(solution)/shard_map/pallas_call | solution.py:36
  264.8 0.8 while.13
  (80 shorter events, 8.5 us)
Async XLA Ops:
  8.3 8.7 %collective-permute-start.14 = (s32[2,16]{1,0:T(2,128)S(1)}, s32[2,16]{1,0:T(2,128)S(1)}, u32[]{:S(2)}, u32[]{:S(2)}) collective-permute-start(s32[2,16]{1,0:T(2,128)S(1)} %pad_add_fusion.1), channel_id=1, source_target_pairs={{0,2},{2,0},{4,6},{6,4},{8,10},{10,8},{12,14},{14,12},{16,18},{18,... | collective-permute-start | bytes 392 | tf_op jit(solution)/shard_map/ppermute | solution.py:349
  8.3 8.7 %collective-permute-start.15 = (s32[2,16]{1,0:T(2,128)S(1)}, s32[2,16]{1,0:T(2,128)S(1)}, u32[]{:S(2)}, u32[]{:S(2)}) collective-permute-start(s32[2,16]{1,0:T(2,128)S(1)} %pad_add_fusion.1), channel_id=1, source_target_pairs={{0,4},{2,6},{4,0},{6,2},{8,12},{10,14},{12,8},{14,10},{16,20},{18,... | collective-permute-start | bytes 392 | tf_op jit(solution)/shard_map/ppermute | solution.py:349
  9.9 7.1 %collective-permute-start.16 = (s32[2,16]{1,0:T(2,128)S(1)}, s32[2,16]{1,0:T(2,128)S(1)}, u32[]{:S(2)}, u32[]{:S(2)}) collective-permute-start(s32[2,16]{1,0:T(2,128)S(1)} %pad_add_fusion.1), channel_id=1, source_target_pairs={{0,6},{2,4},{4,2},{6,0},{8,14},{10,12},{12,10},{14,8},{16,22},{18,... | collective-permute-start | bytes 392 | tf_op jit(solution)/shard_map/ppermute | solution.py:349
  17.0 6.6 %copy-start.20 = (bf16[1,4,64,4096]{3,2,1,0:T(8,128)(2,1)S(1)}, bf16[1,4,64,4096]{3,2,1,0:T(8,128)(2,1)}, u32[]{:S(2)}) copy-start(bf16[1,4,64,4096]{3,2,1,0:T(8,128)(2,1)} %param.15) | copy-start | bytes 6291460
  17.1 99.2 %all-to-all-start = ((bf16[16,32,4096]{2,1,0:T(8,128)(2,1)}), bf16[16,32,4096]{2,1,0:T(8,128)(2,1)}, u32[]{:S(2)}, u32[]{:S(2)}) async-start(bf16[16,32,4096]{2,1,0:T(8,128)(2,1)} %bitcast.62), calls=%async_computation | async-start | bytes 8388608 | tf_op jit(solution)/shard_map/all_to_all | solution.py:353
  23.4 134.6 %all-gather.2.cloned.1.call-start = ((), (), s32[]{:S(2)}) async-start(), calls=%async_computation.2 | async-start | bytes 5242880 | tf_op jit(solution)/shard_map/all_gather | solution.py:402
  25.6 2.0 copy-start.13
  27.7 7.1 %collective-permute-start.17 = (bf16[2,128,4096]{2,1,0:T(8,128)(2,1)S(1)}, bf16[2,128,4096]{2,1,0:T(8,128)(2,1)}, u32[]{:S(2)}, u32[]{:S(2)}) collective-permute-start(bf16[2,128,4096]{2,1,0:T(8,128)(2,1)S(1)} %dynamic-slice_bitcast_fusion), channel_id=1, source_target_pairs={{0,2},{2,0},{4,6},{6,4},{8,10},{10,8},{12,14},{14,12},{16,18},{18,... | collective-permute-start | bytes 6291464 | tf_op jit(solution)/shard_map/ppermute | solution.py:383
  34.8 5.1 %copy-start.18 = (bf16[128,4096]{1,0:T(8,128)(2,1)S(1)}, bf16[128,4096]{1,0:T(8,128)(2,1)}, u32[]{:S(2)}) copy-start(bf16[128,4096]{1,0:T(8,128)(2,1)} %shard_map.56) | copy-start | bytes 3145732
  34.8 6.7 %copy-start.14 = (bf16[512,4096]{1,0:T(8,128)(2,1)S(1)}, bf16[512,4096]{1,0:T(8,128)(2,1)}, u32[]{:S(2)}) copy-start(bf16[512,4096]{1,0:T(8,128)(2,1)} %copy-done.13) | copy-start | bytes 12582916
  38.5 39.8 %collective-permute-start.18 = (bf16[1,128,4096]{2,1,0:T(8,128)(2,1)}, bf16[1,128,4096]{2,1,0:T(8,128)(2,1)}, u32[]{:S(2)}, u32[]{:S(2)}) collective-permute-start(bf16[1,128,4096]{2,1,0:T(8,128)(2,1)} %constant_dynamic-slice_fusion), channel_id=1, source_target_pairs={{0,4},{2,6},{4,0},{6,2},{8,12},{10,14},{12,8},{14,10},{16,20},{18,... | collective-permute-start | bytes 3145736 | tf_op jit(solution)/shard_map/ppermute | solution.py:383
  40.7 74.7 %collective-permute-start.22 = (bf16[32,4096]{1,0:T(8,128)(2,1)}, bf16[32,4096]{1,0:T(8,128)(2,1)}, u32[]{:S(2)}, u32[]{:S(2)}) collective-permute-start(bf16[32,4096]{1,0:T(8,128)(2,1)} %get-tuple-element.323), channel_id=1, source_target_pairs={{0,8},{2,10},{4,12},{6,14},{8,0},{10,2},{12,4},{14,6},{16,24},{18,... | collective-permute-start | bytes 786440 | tf_op jit(solution)/shard_map/ppermute | solution.py:393
  44.1 76.7 %copy-start.9 = (f32[256,512]{1,0:T(8,128)}, f32[256,512]{1,0:T(8,128)S(1)}, u32[]{:S(2)}) copy-start(f32[256,512]{1,0:T(8,128)S(1)} %shard_map.57.refs_4_) | copy-start | bytes 1572868
  44.1 71.3 %collective-permute-start.23 = (f32[256,512]{1,0:T(8,128)S(1)}, f32[256,512]{1,0:T(8,128)S(1)}, u32[]{:S(2)}, u32[]{:S(2)}) collective-permute-start(f32[256,512]{1,0:T(8,128)S(1)} %shard_map.57.refs_4_), channel_id=1, source_target_pairs={{0,1},{1,0},{2,3},{3,2},{4,5},{5,4},{6,7},{7,6},{8,9},{9,8},{10,11... | collective-permute-start | bytes 1572872 | tf_op jit(solution)/shard_map/ppermute | solution.py:19
  79.4 20.2 %collective-permute-start.19 = (s32[3,16]{1,0:T(4,128)S(1)}, s32[3,16]{1,0:T(4,128)S(1)}, u32[]{:S(2)}, u32[]{:S(2)}) collective-permute-start(s32[3,16]{1,0:T(4,128)S(1)} %pad_add_fusion), channel_id=1, source_target_pairs={{0,8},{2,10},{4,12},{6,14},{8,0},{10,2},{12,4},{14,6},{16,24},{18,... | collective-permute-start | bytes 584 | tf_op jit(solution)/shard_map/ppermute | solution.py:349
  90.5 23.9 %collective-permute-start.20 = (s32[3,16]{1,0:T(4,128)S(1)}, s32[3,16]{1,0:T(4,128)S(1)}, u32[]{:S(2)}, u32[]{:S(2)}) collective-permute-start(s32[3,16]{1,0:T(4,128)S(1)} %pad_add_fusion), channel_id=1, source_target_pairs={{0,16},{2,18},{4,20},{6,22},{8,24},{10,26},{12,28},{14,30},{16,0},... | collective-permute-start | bytes 584 | tf_op jit(solution)/shard_map/ppermute | solution.py:349
  90.5 24.8 %collective-permute-start.21 = (s32[3,16]{1,0:T(4,128)S(1)}, s32[3,16]{1,0:T(4,128)S(1)}, u32[]{:S(2)}, u32[]{:S(2)}) collective-permute-start(s32[3,16]{1,0:T(4,128)S(1)} %pad_add_fusion), channel_id=1, source_target_pairs={{0,24},{2,26},{4,28},{6,30},{8,16},{10,18},{12,20},{14,22},{16,8},... | collective-permute-start | bytes 584 | tf_op jit(solution)/shard_map/ppermute | solution.py:349
  115.4 5.4 %copy-start.24 = (f32[256,512]{1,0:T(8,128)}, f32[256,512]{1,0:T(8,128)S(1)}, u32[]{:S(2)}) copy-start(f32[256,512]{1,0:T(8,128)S(1)} %collective-permute-done.23.refs_5_) | copy-start | bytes 1572868
  116.3 7.2 %copy-start.19 = (bf16[128,4096]{1,0:T(8,128)(2,1)S(1)}, bf16[128,4096]{1,0:T(8,128)(2,1)}, u32[]{:S(2)}) copy-start(bf16[128,4096]{1,0:T(8,128)(2,1)} %shard_map.56) | copy-start | bytes 3145732
  120.8 1.1 copy-start.11
  121.9 19.4 %collective-permute-start.26 = (bf16[512,640]{1,0:T(8,128)(2,1)S(1)}, bf16[512,640]{1,0:T(8,128)(2,1)S(1)}, u32[]{:S(2)}, u32[]{:S(2)}) collective-permute-start(bf16[512,640]{1,0:T(8,128)(2,1)S(1)} %get-tuple-element.238), channel_id=1, source_target_pairs={{0,1},{1,0},{2,3},{3,2},{4,5},{5,4},{6,7},{7,6},{8,9},{9,8},{10,11... | collective-permute-start | bytes 1966088 | tf_op jit(solution)/shard_map/ppermute | solution.py:224
  123.5 17.9 %collective-permute-start.24 = (bf16[32,4096]{1,0:T(8,128)(2,1)S(1)}, bf16[32,4096]{1,0:T(8,128)(2,1)S(1)}, u32[]{:S(2)}, u32[]{:S(2)}) collective-permute-start(bf16[32,4096]{1,0:T(8,128)(2,1)S(1)} %get-tuple-element.322), channel_id=1, source_target_pairs={{0,16},{2,18},{4,20},{6,22},{8,24},{10,26},{12,28},{14,30},{16,0},... | collective-permute-start | bytes 786440 | tf_op jit(solution)/shard_map/ppermute | solution.py:393
  125.2 23.7 %collective-permute-start.25 = (bf16[32,4096]{1,0:T(8,128)(2,1)S(1)}, bf16[32,4096]{1,0:T(8,128)(2,1)S(1)}, u32[]{:S(2)}, u32[]{:S(2)}) collective-permute-start(bf16[32,4096]{1,0:T(8,128)(2,1)S(1)} %get-tuple-element.321), channel_id=1, source_target_pairs={{0,24},{2,26},{4,28},{6,30},{8,16},{10,18},{12,20},{14,22},{16,8},... | collective-permute-start | bytes 786440 | tf_op jit(solution)/shard_map/ppermute | solution.py:393
  141.3 0.8 copy-start.22
  148.9 109.8 %all-to-all-start.1 = ((bf16[16,32,4096]{2,1,0:T(8,128)(2,1)}), bf16[16,32,4096]{2,1,0:T(8,128)(2,1)}, u32[]{:S(2)}, u32[]{:S(2)}) async-start(bf16[16,32,4096]{2,1,0:T(8,128)(2,1)} %bitcast.63), calls=%async_computation.1 | async-start | bytes 8388608 | tf_op jit(solution)/shard_map/all_to_all | solution.py:353
  158.0 2.2 copy-start.4
  160.2 5.1 %copy-start.5 = (bf16[512,4096]{1,0:T(8,128)(2,1)S(1)}, bf16[512,4096]{1,0:T(8,128)(2,1)}, u32[]{:S(2)}) copy-start(bf16[512,4096]{1,0:T(8,128)(2,1)} %all-gather.2.cloned.1.call-done.weights_ref.refs_1_) | copy-start | bytes 12582916
  162.8 18.4 %copy-start.8 = (f32[256,512]{1,0:T(8,128)}, f32[256,512]{1,0:T(8,128)S(1)}, u32[]{:S(2)}) copy-start(f32[256,512]{1,0:T(8,128)S(1)} %shard_map.61.refs_4_) | copy-start | bytes 1572868
  162.8 17.6 %collective-permute-start.28 = (f32[256,512]{1,0:T(8,128)S(1)}, f32[256,512]{1,0:T(8,128)S(1)}, u32[]{:S(2)}, u32[]{:S(2)}) collective-permute-start(f32[256,512]{1,0:T(8,128)S(1)} %shard_map.61.refs_4_), channel_id=1, source_target_pairs={{0,1},{1,0},{2,3},{3,2},{4,5},{5,4},{6,7},{7,6},{8,9},{9,8},{10,11... | collective-permute-start | bytes 1572872 | tf_op jit(solution)/shard_map/ppermute | solution.py:19
  164.6 16.5 %copy-start.7 = (bf16[128,4096]{1,0:T(8,128)(2,1)}, bf16[128,4096]{1,0:T(8,128)(2,1)S(1)}, u32[]{:S(2)}) copy-start(bf16[128,4096]{1,0:T(8,128)(2,1)S(1)} %constant_dynamic-update-slice_fusion.rows_ref.refs_0_) | copy-start | bytes 3145732
  168.1 0.7 copy-start.12
  168.8 11.5 %collective-permute-start.27 = (bf16[128,640]{1,0:T(8,128)(2,1)S(1)}, bf16[128,640]{1,0:T(8,128)(2,1)S(1)}, u32[]{:S(2)}, u32[]{:S(2)}) collective-permute-start(bf16[128,640]{1,0:T(8,128)(2,1)S(1)} %get-tuple-element.250), channel_id=1, source_target_pairs={{0,1},{1,0},{2,3},{3,2},{4,5},{5,4},{6,7},{7,6},{8,9},{9,8},{10,11... | collective-permute-start | bytes 491528 | tf_op jit(solution)/shard_map/ppermute | solution.py:224
  180.3 0.8 copy-start.26
  180.3 0.8 copy-start.23
  185.0 22.7 %collective-permute-start.6 = (bf16[32,4096]{1,0:T(8,128)(2,1)S(1)}, bf16[32,4096]{1,0:T(8,128)(2,1)S(1)}, u32[]{:S(2)}, u32[]{:S(2)}) collective-permute-start(bf16[32,4096]{1,0:T(8,128)(2,1)S(1)} %get-tuple-element.315), channel_id=1, source_target_pairs={{16,24},{18,26},{20,28},{22,30},{17,25},{19,27},{21,29},{23,31}} | collective-permute-start | bytes 786440 | tf_op jit(solution)/shard_map/cond/branch_2_fun/ppermute | solution.py:430
  188.4 65.0 %collective-permute-start.7 = (bf16[32,4096]{1,0:T(8,128)(2,1)S(1)}, bf16[32,4096]{1,0:T(8,128)(2,1)S(1)}, u32[]{:S(2)}, u32[]{:S(2)}) collective-permute-start(bf16[32,4096]{1,0:T(8,128)(2,1)S(1)} %get-tuple-element.317), channel_id=1, source_target_pairs={{16,0},{18,2},{20,4},{22,6},{17,1},{19,3},{21,5},{23,7}} | collective-permute-start | bytes 786440 | tf_op jit(solution)/shard_map/cond/branch_2_fun/ppermute | solution.py:430
  189.7 68.9 %collective-permute-start.8 = (bf16[32,4096]{1,0:T(8,128)(2,1)S(1)}, bf16[32,4096]{1,0:T(8,128)(2,1)S(1)}, u32[]{:S(2)}, u32[]{:S(2)}) collective-permute-start(bf16[32,4096]{1,0:T(8,128)(2,1)S(1)} %get-tuple-element.316), channel_id=1, source_target_pairs={{16,8},{18,10},{20,12},{22,14},{17,9},{19,11},{21,13},{23,15}} | collective-permute-start | bytes 786440 | tf_op jit(solution)/shard_map/cond/branch_2_fun/ppermute | solution.py:430
Sparse Core Ops, SparseCore 0:
  123.5 33.6 all-gather.1

commit v4 on v3

--- a/solution.py
+++ b/solution.py
@@ -175,7 +175,7 @@
     )[0]
 
 
-def sketch(rows, weights):
+def sketch(rows, weights, rank):
     count, width = rows.shape
     total = weights.shape[0]
     tiles = tiling(width)
@@ -196,19 +196,22 @@
             else:
                 out_ref[:, :total] += product
                 out_ref[:, total:] += squares
-        narrow_ref[:, :total] = out_ref[:, :total].astype(BF16)
-        squares = out_ref[:, total:]
-        column = lax.broadcasted_iota(jnp.int32, squares.shape, 1)
+        squares = out_ref[:, total : total + 1]
+        column = lax.broadcasted_iota(jnp.int32, (count, total), 1) - (total - rank)
         first = squares.astype(BF16).astype(F32)
         second = (squares - first).astype(BF16).astype(F32)
         third = squares - first - second
         terms = jnp.where(column == 0, first, jnp.where(column == 1, second, third))
-        narrow_ref[:, total:] = jnp.where(column < 3, terms, 0.0).astype(BF16)
+        terms = jnp.where(column < 3, terms, 0.0)
+        narrow_ref[...] = jnp.where(column < 0, out_ref[:, :total], terms).astype(BF16)
 
     shape = (count, total + 128)
     return call(
         body,
-        [(jax.ShapeDtypeStruct(shape, F32), False), (jax.ShapeDtypeStruct(shape, BF16), False)],
+        [
+            (jax.ShapeDtypeStruct(shape, F32), False),
+            (jax.ShapeDtypeStruct((count, total), BF16), False),
+        ],
         (rows, weights),
         [0, 1],
         [
@@ -225,12 +228,13 @@
     return [lax.psum(sketched, "mp")]
 
 
-def widen(part, total):
+def widen(part, total, rank):
     if part.dtype == F32:
         return part
     part = part.astype(F32)
-    squares = jnp.sum(part[:, total:], axis=1, keepdims=True)
-    return jnp.concatenate([part[:, :total], jnp.broadcast_to(squares, part[:, total:].shape)], 1)
+    column = lax.broadcasted_iota(jnp.int32, part.shape, 1)
+    squares = jnp.sum(jnp.where(column < total - rank, 0.0, part), axis=1, keepdims=True)
+    return jnp.concatenate([part, jnp.broadcast_to(squares, (part.shape[0], 128))], 1)
 
 
 def low_rank(sketched, table, layers, model_width):
@@ -273,7 +277,7 @@
         out_ref, rows_buf, up_buf, out_buf, in_sems, out_sems = refs[-6:]
         up_ref = weights_ref.at[pl.ds(half, half), :]
         copies = start_all([rows_ref, up_ref], [rows_buf, up_buf], in_sems, tiles)
-        whole_sketch = sum(widen(ref[...], 2 * half) for ref in sketch_refs)
+        whole_sketch = sum(widen(ref[...], 2 * half, half // layers) for ref in sketch_refs)
         whole_table = sum(ref[...] for ref in table_refs)
         low = low_rank(whole_sketch, whole_table, layers, model_width)
         sent = []
@@ -306,7 +310,8 @@
 
 
 def adapt(rows, weights, tables, layers, model_width):
-    sketched = sketch_parts(*sketch(rows, weights))
+    rank = weights.shape[0] // (2 * layers)
+    sketched = sketch_parts(*sketch(rows, weights, rank))
     return finish(rows, sketched, tables, weights, layers, model_width)
 
 
@@ -315,7 +320,7 @@
     owners = lax.axis_size("dp")
     adapters = store_slot.shape[0]
     assert adapters == owners and down_store.shape[0] == 1
-    layers = down_store.shape[1]
+    layers, rank = down_store.shape[1], down_store.shape[3]
     model_width = width * lax.axis_size("mp")
     slot_rows = count // adapters
     group = 1
@@ -388,23 +393,22 @@
     tallies = add_over(tallies, range(group, owners, group))
 
     over_blocks = over_packed.reshape(planes, slot_rows, width)
+    over_blocks = [over_blocks[step] for step in range(planes)]
 
     def to_plane(step, block):
         return lax.ppermute(block, "dp", [(i, i ^ (step * group)) for i in range(owners)])
 
     over_arrived = [over_blocks[0]] + [to_plane(step, over_blocks[step]) for step in range(1, 2)]
-    mine, tallies, over_blocks, arrived, *rest = lax.optimization_barrier(
-        (mine, tallies, over_blocks, arrived, *over_arrived, *table)
-    )
-    over_arrived, table = rest[: len(over_arrived)], rest[len(over_arrived) :]
+    mine, tallies, arrived, over_arrived, over_blocks, table = lax.optimization_barrier(
+        (mine, tallies, arrived, over_arrived, over_blocks, table)
+    )
 
     groups = [[p * group + q for q in range(group)] for p in range(planes)]
     plane_weights = lax.all_gather(mine, "dp", axis_index_groups=groups, tiled=True)
 
-    sketched, narrow = sketch(arrived, weights)
+    sketched, narrow = sketch(arrived, weights, rank)
     sketched = sketch_parts(sketched, narrow)
     later = [to_plane(step, over_blocks[step]) for step in range(2, planes)]
-    *later[:-1], sketched[0] = lax.optimization_barrier((*later[:-1], sketched[0]))
     done = finish(arrived, sketched, table, weights, layers, model_width)
     *later, done = lax.optimization_barrier((*later, done))
     over_arrived = over_arrived + later

time: 275 us -> 271 us (0.985)
  starting transfers between devices: 44.7 us -> 39.4 us
  waiting for transfers between devices: 145 us -> 149 us
    ppermute x3, waiting for transfers between devices: 15.6 us -> 4.89 us  [to_plane(): lax.ppermute(block, 'dp', [(i, i ^ step * group) for i in range(owners)])]
    ppermute x2, waiting for transfers between devices: 5.91 us -> 15 us  [sketch_parts(): return [sketched, lax.ppermute(narrow, 'mp', [(0, 1), (1, 0)])]]
    ppermute x3, waiting for transfers between devices: 67.5 us -> 72.8 us  [moved(): got.append(lax.ppermute(blocks[step], 'dp', pairs))]
    ppermute x3, starting transfers between devices: 6.02 us -> 2.65 us  [moved(): got.append(lax.ppermute(blocks[step], 'dp', pairs))]
    unnamed x35 -> x37, local copies, waits for them, and re-layouts: 8.66 us -> 8.64 us
  transfers between devices with their start and end apart: 21 -> 21, of which waited for: 10 -> 9; matrix products, arithmetic and copies ran while one was open for 5% -> 5% of each run, Pallas kernels for 10% -> 12%
where the time goes in v4:
time: 271 us; the launch traced here: 270 us
  waiting for transfers between devices  149 us (55%)
  starting transfers between devices  39.4 us (15%)
  Pallas kernels  38.6 us (14%)
  between operations  19.2 us (7%)
  other arithmetic  11.7 us (4%)
  local copies, waits for them, and re-layouts  11.4 us (4%)
    ppermute x3, waiting for transfers between devices, moved(): got.append(lax.ppermute(blocks[step], 'dp', pairs))  72.8 us
    pallas_call x9, Pallas kernels, call(): pl.pallas_call(body, out_shape=[out for out, _ in outs], in_specs=in_spec...  38.6 us
    ppermute x2, waiting for transfers between devices, local(): taken = lax.ppermute(give, 'dp', [(i, i ^ step) for i in range(owners)])  31.6 us
    ppermute x6, waiting for transfers between devices, add_over(): return value + sum((lax.ppermute(value, 'dp', p) for p in pairs))  23.4 us
    ppermute x2, waiting for transfers between devices, sketch_parts(): return [sketched, lax.ppermute(narrow, 'mp', [(0, 1), (1, 0)])]  15 us
    ppermute x6, starting transfers between devices, add_over(): return value + sum((lax.ppermute(value, 'dp', p) for p in pairs))  14.5 us
    all_to_all x2, starting transfers between devices, exchange(): lax.all_to_all(blocks, 'dp', 0, 0, tiled=True)  11.5 us
    unnamed x37, local copies, waits for them, and re-layouts  8.64 us
  transfers between devices with their start and end apart: 21, of which 9 were waited for; matrix products, arithmetic and copies ran while one was open for 5% of the time, Pallas kernels for 12%

profile of v4, /device:TPU:16, one launch (start us, length us, event | category | flops | bytes accessed | tf_op | source)
XLA Modules:
  0.0 269.9 jit_solution(7915691695450557511)
XLA Ops:
  6.5 0.8 select_reduce_fusion
  8.3 1.6 collective-permute-start.15
  11.2 5.8 %shard_map.55 = bf16[512,4096]{1,0:T(8,128)(2,1)} custom-call(s32[1,512]{1,0:T(1,128)} %get-tuple-element.326.target_ref, bf16[512,4096]{1,0:T(8,128)(2,1)} %hidden_ref.3), custom_call_target="tpu_custom_call" | custom-call | flops 1 | bytes 1 | tf_op jit(solution)/shard_map/pallas_call | solution.py:36
  17.1 6.3 %all-to-all-start = ((bf16[16,32,4096]{2,1,0:T(8,128)(2,1)}), bf16[16,32,4096]{2,1,0:T(8,128)(2,1)}, u32[]{:S(2)}, u32[]{:S(2)}) async-start(bf16[16,32,4096]{2,1,0:T(8,128)(2,1)} %bitcast.57), calls=%async_computation | async-start | bytes 8388608 | tf_op jit(solution)/shard_map/all_to_all | solution.py:358
  23.7 1.9 pad_maximum_fusion.weights_ref.refs_1_
  25.6 2.0 copy-done.13
  27.9 3.9 %shard_map.56 = bf16[128,4096]{1,0:T(8,128)(2,1)} custom-call(s32[1,512]{1,0:T(1,128)} %get-tuple-element.325.target_ref, bf16[512,4096]{1,0:T(8,128)(2,1)} %hidden_ref.3), custom_call_target="tpu_custom_call" | custom-call | flops 1 | bytes 1 | tf_op jit(solution)/shard_map/pallas_call | solution.py:36
  32.0 0.7 fusion.8
  34.4 2.0 bitcast_select_fusion
  36.4 1.1 constant_dynamic-slice_fusion
  37.5 1.5 collective-permute-start.18
  38.9 0.9 fusion.17
  39.9 1.5 collective-permute-start.22
  41.3 2.6 shard_map.57.refs_4_
  43.9 1.6 collective-permute-start.23
  46.6 31.6 %collective-permute-done.18 = bf16[1,128,4096]{2,1,0:T(8,128)(2,1)} collective-permute-done((bf16[1,128,4096]{2,1,0:T(8,128)(2,1)}, bf16[1,128,4096]{2,1,0:T(8,128)(2,1)}, u32[]{:S(2)}, u32[]{:S(2)}) %collective-permute-start.18) | collective-permute-done | bytes 1048608 | tf_op jit(solution)/shard_map/ppermute | solution.py:388
  78.3 1.1 select_bitcast_fusion
  79.4 11.1 %collective-permute-start.19 = (s32[3,16]{1,0:T(4,128)S(1)}, s32[3,16]{1,0:T(4,128)S(1)}, u32[]{:S(2)}, u32[]{:S(2)}) collective-permute-start(s32[3,16]{1,0:T(4,128)S(1)} %pad_add_fusion), channel_id=1, source_target_pairs={{0,8},{2,10},{4,12},{6,14},{8,0},{10,2},{12,4},{14,6},{16,24},{18,... | collective-permute-start | bytes 584 | tf_op jit(solution)/shard_map/ppermute | solution.py:354
  90.5 1.5 collective-permute-start.21
  92.0 7.6 %collective-permute-done.19 = s32[3,16]{1,0:T(4,128)S(1)} collective-permute-done((s32[3,16]{1,0:T(4,128)S(1)}, s32[3,16]{1,0:T(4,128)S(1)}, u32[]{:S(2)}, u32[]{:S(2)}) %collective-permute-start.19) | collective-permute-done | bytes 224 | tf_op jit(solution)/shard_map/ppermute | solution.py:354
  99.6 14.9 %collective-permute-done.20 = s32[3,16]{1,0:T(4,128)S(1)} collective-permute-done((s32[3,16]{1,0:T(4,128)S(1)}, s32[3,16]{1,0:T(4,128)S(1)}, u32[]{:S(2)}, u32[]{:S(2)}) %collective-permute-start.20) | collective-permute-done | bytes 224 | tf_op jit(solution)/shard_map/ppermute | solution.py:354
  114.4 0.9 collective-permute-done.21
  115.4 0.8 all-to-all-done
  116.3 4.5 %shard_map.58 = (f32[512,640]{1,0:T(8,128)S(1)}, bf16[512,512]{1,0:T(8,128)(2,1)S(1)}) custom-call(bf16[512,4096]{1,0:T(8,128)(2,1)} %bitcast.15.rows_ref.refs_0_, bf16[512,4096]{1,0:T(8,128)(2,1)} %copy-done.13), custom_call_target="tpu_custom_call" | custom-call | flops 1 | bytes 1 | tf_op jit(solution)/shard_map/pallas_call | solution.py:36
  120.8 1.1 copy-done.11
  121.9 1.5 collective-permute-start.26
  123.4 1.6 collective-permute-start.24
  125.6 9.7 %collective-permute-done.26.refs_3_ = bf16[512,512]{1,0:T(8,128)(2,1)S(1)} collective-permute-done((bf16[512,512]{1,0:T(8,128)(2,1)S(1)}, bf16[512,512]{1,0:T(8,128)(2,1)S(1)}, u32[]{:S(2)}, u32[]{:S(2)}) %collective-permute-start.26) | collective-permute-done | bytes 524320 | tf_op jit(solution)/shard_map/ppermute | solution.py:227
  135.4 0.8 copy-done.23
  136.2 6.6 %shard_map.59 = bf16[512,4096]{1,0:T(8,128)(2,1)} custom-call(bf16[512,4096]{1,0:T(8,128)(2,1)} %bitcast.15.rows_ref.refs_0_, bf16[512,4096]{1,0:T(8,128)(2,1)} %copy-done.13, f32[512,640]{1,0:T(8,128)} %copy-done.11, bf16[512,512]{1,0:T(8,128)(2,1)} %copy-done.23, f32[256,512]{1,0:T(8,128)} %copy-done.9, f32[256,512]{1,0:T(8,128)} %copy-done.22), custom_call_target="tpu_custom_call" | custom-call | flops 1 | bytes 1 | tf_op jit(solution)/shard_map/pallas_call | solution.py:36
  142.8 4.9 %collective-permute-done.25 = bf16[32,4096]{1,0:T(8,128)(2,1)S(1)} collective-permute-done((bf16[32,4096]{1,0:T(8,128)(2,1)S(1)}, bf16[32,4096]{1,0:T(8,128)(2,1)S(1)}, u32[]{:S(2)}, u32[]{:S(2)}) %collective-permute-start.25) | collective-permute-done | bytes 262176 | tf_op jit(solution)/shard_map/ppermute | solution.py:399
  147.7 5.2 %all-to-all-start.1 = ((bf16[16,32,4096]{2,1,0:T(8,128)(2,1)}), bf16[16,32,4096]{2,1,0:T(8,128)(2,1)}, u32[]{:S(2)}, u32[]{:S(2)}) async-start(bf16[16,32,4096]{2,1,0:T(8,128)(2,1)} %bitcast.58), calls=%async_computation.1 | async-start | bytes 8388608 | tf_op jit(solution)/shard_map/all_to_all | solution.py:358
  154.2 2.2 copy-done.4
  156.4 2.6 shard_map.61.refs_4_
  159.6 1.0 constant_dynamic-update-slice_fusion.2
  161.3 2.8 %shard_map.60 = (f32[128,640]{1,0:T(8,128)S(1)}, bf16[128,512]{1,0:T(8,128)(2,1)S(1)}) custom-call(bf16[128,4096]{1,0:T(8,128)(2,1)S(1)} %constant_dynamic-update-slice_fusion.rows_ref.refs_0_, bf16[512,4096]{1,0:T(8,128)(2,1)S(1)} %copy-done.5), custom_call_target="tpu_custom_call" | custom-call | flops 1 | bytes 1 | tf_op jit(solution)/shard_map/pallas_call | solution.py:36
  164.1 0.7 copy-done.12
  164.8 1.5 collective-permute-start.27
  166.3 1.2 convert_reduce_fusion.2
  170.6 5.3 %collective-permute-done.27.refs_3_ = bf16[128,512]{1,0:T(8,128)(2,1)S(1)} collective-permute-done((bf16[128,512]{1,0:T(8,128)(2,1)S(1)}, bf16[128,512]{1,0:T(8,128)(2,1)S(1)}, u32[]{:S(2)}, u32[]{:S(2)}) %collective-permute-start.27) | collective-permute-done | bytes 131104 | tf_op jit(solution)/shard_map/ppermute | solution.py:227
  175.9 0.8 copy-done.21
  176.7 3.7 %shard_map.62 = bf16[128,4096]{1,0:T(8,128)(2,1)S(1)} custom-call(bf16[128,4096]{1,0:T(8,128)(2,1)} %copy-done.7, bf16[512,4096]{1,0:T(8,128)(2,1)} %all-gather.2.cloned.1.call-done.weights_ref.refs_1_, f32[128,640]{1,0:T(8,128)} %copy-done.12, bf16[128,512]{1,0:T(8,128)(2,1)} %copy-done.27, f32[256,512]{1,0:T(8,128)} %copy-done.8, f32[256,512]{1,0:T(8,128)} %copy-done.21), custom_call_target="tpu_custom_call" | custom-call | flops 1 | bytes 1 | tf_op jit(solution)/shard_map/pallas_call | solution.py:36
  180.4 75.7 %conditional.1 = (bf16[32,4096]{1,0:T(8,128)(2,1)S(1)}) conditional(s32[]{:T(128)} %clamp.3, (s32[]{:T(128)}, bf16[128,4096]{1,0:T(8,128)(2,1)S(1)}) %tuple.46, (s32[]{:T(128)}, bf16[128,4096]{1,0:T(8,128)(2,1)S(1)}) %tuple.46, (s32[]{:T(128)}, bf16[128,4096]{1,0:T(8,128)(2,1)S(1)}) %tuple.46, (s32[]{:T(128)}, ...), branch_computations={%region_8.9_spmd, %region_9.10_spmd, %region_10.11_spmd, %region_1... | conditional | flops 524289 | bytes 6029450 | solution.py:440
  180.5 0.7 collective-permute-start.3
  181.9 1.3 collective-permute-start.5
  183.2 72.8 %collective-permute-done.5 = bf16[32,4096]{1,0:T(8,128)(2,1)S(1)} collective-permute-done((bf16[32,4096]{1,0:T(8,128)(2,1)S(1)}, bf16[32,4096]{1,0:T(8,128)(2,1)S(1)}, u32[]{:S(2)}, u32[]{:S(2)}) %collective-permute-start.5) | collective-permute-done | bytes 262176 | tf_op jit(solution)/shard_map/cond/branch_1_fun/ppermute | solution.py:434
  256.1 6.1 %shard_map.63 = bf16[512,4096]{1,0:T(8,128)(2,1)} custom-call(s32[512,1]{1,0:T(8,128)S(1)} %copy.18.refs_0_, s32[512,1]{1,0:T(8,128)S(1)} %copy.19.refs_1_, bf16[512,4096]{1,0:T(8,128)(2,1)} %bitcast.20.refs_2_, bf16[32,4096]{1,0:T(8,128)(2,1)S(1)} %get-tuple-element.451.refs_3_), custom_call_target="tpu_custom_call" | custom-call | flops 1 | bytes 1 | tf_op jit(solution)/shard_map/pallas_call | solution.py:36
  262.2 0.8 while.13
  (81 shorter events, 7.5 us)
Async XLA Ops:
  8.3 8.7 %collective-permute-start.14 = (s32[2,16]{1,0:T(2,128)S(1)}, s32[2,16]{1,0:T(2,128)S(1)}, u32[]{:S(2)}, u32[]{:S(2)}) collective-permute-start(s32[2,16]{1,0:T(2,128)S(1)} %pad_add_fusion.1), channel_id=1, source_target_pairs={{0,2},{2,0},{4,6},{6,4},{8,10},{10,8},{12,14},{14,12},{16,18},{18,... | collective-permute-start | bytes 392 | tf_op jit(solution)/shard_map/ppermute | solution.py:354
  8.3 8.7 %collective-permute-start.15 = (s32[2,16]{1,0:T(2,128)S(1)}, s32[2,16]{1,0:T(2,128)S(1)}, u32[]{:S(2)}, u32[]{:S(2)}) collective-permute-start(s32[2,16]{1,0:T(2,128)S(1)} %pad_add_fusion.1), channel_id=1, source_target_pairs={{0,4},{2,6},{4,0},{6,2},{8,12},{10,14},{12,8},{14,10},{16,20},{18,... | collective-permute-start | bytes 392 | tf_op jit(solution)/shard_map/ppermute | solution.py:354
  9.9 7.1 %collective-permute-start.16 = (s32[2,16]{1,0:T(2,128)S(1)}, s32[2,16]{1,0:T(2,128)S(1)}, u32[]{:S(2)}, u32[]{:S(2)}) collective-permute-start(s32[2,16]{1,0:T(2,128)S(1)} %pad_add_fusion.1), channel_id=1, source_target_pairs={{0,6},{2,4},{4,2},{6,0},{8,14},{10,12},{12,10},{14,8},{16,22},{18,... | collective-permute-start | bytes 392 | tf_op jit(solution)/shard_map/ppermute | solution.py:354
  17.0 6.6 %copy-start.19 = (bf16[1,4,64,4096]{3,2,1,0:T(8,128)(2,1)S(1)}, bf16[1,4,64,4096]{3,2,1,0:T(8,128)(2,1)}, u32[]{:S(2)}) copy-start(bf16[1,4,64,4096]{3,2,1,0:T(8,128)(2,1)} %param.15) | copy-start | bytes 6291460
  17.1 99.2 %all-to-all-start = ((bf16[16,32,4096]{2,1,0:T(8,128)(2,1)}), bf16[16,32,4096]{2,1,0:T(8,128)(2,1)}, u32[]{:S(2)}, u32[]{:S(2)}) async-start(bf16[16,32,4096]{2,1,0:T(8,128)(2,1)} %bitcast.57), calls=%async_computation | async-start | bytes 8388608 | tf_op jit(solution)/shard_map/all_to_all | solution.py:358
  23.4 130.8 %all-gather.2.cloned.1.call-start = ((), (), s32[]{:S(2)}) async-start(), calls=%async_computation.2 | async-start | bytes 5242880 | tf_op jit(solution)/shard_map/all_gather | solution.py:407
  25.6 2.0 copy-start.13
  27.7 6.7 %collective-permute-start.17 = (bf16[2,128,4096]{2,1,0:T(8,128)(2,1)S(1)}, bf16[2,128,4096]{2,1,0:T(8,128)(2,1)}, u32[]{:S(2)}, u32[]{:S(2)}) collective-permute-start(bf16[2,128,4096]{2,1,0:T(8,128)(2,1)S(1)} %dynamic-slice_bitcast_fusion), channel_id=1, source_target_pairs={{0,2},{2,0},{4,6},{6,4},{8,10},{10,8},{12,14},{14,12},{16,18},{18,... | collective-permute-start | bytes 6291464 | tf_op jit(solution)/shard_map/ppermute | solution.py:388
  34.4 4.5 %copy-start.18 = (bf16[128,4096]{1,0:T(8,128)(2,1)S(1)}, bf16[128,4096]{1,0:T(8,128)(2,1)}, u32[]{:S(2)}) copy-start(bf16[128,4096]{1,0:T(8,128)(2,1)} %shard_map.56) | copy-start | bytes 3145732
  34.4 6.9 %copy-start.14 = (bf16[512,4096]{1,0:T(8,128)(2,1)S(1)}, bf16[512,4096]{1,0:T(8,128)(2,1)}, u32[]{:S(2)}) copy-start(bf16[512,4096]{1,0:T(8,128)(2,1)} %copy-done.13) | copy-start | bytes 12582916
  37.5 40.8 %collective-permute-start.18 = (bf16[1,128,4096]{2,1,0:T(8,128)(2,1)}, bf16[1,128,4096]{2,1,0:T(8,128)(2,1)}, u32[]{:S(2)}, u32[]{:S(2)}) collective-permute-start(bf16[1,128,4096]{2,1,0:T(8,128)(2,1)} %constant_dynamic-slice_fusion), channel_id=1, source_target_pairs={{0,4},{2,6},{4,0},{6,2},{8,12},{10,14},{12,8},{14,10},{16,20},{18,... | collective-permute-start | bytes 3145736 | tf_op jit(solution)/shard_map/ppermute | solution.py:388
  39.9 75.5 %collective-permute-start.22 = (bf16[32,4096]{1,0:T(8,128)(2,1)}, bf16[32,4096]{1,0:T(8,128)(2,1)}, u32[]{:S(2)}, u32[]{:S(2)}) collective-permute-start(bf16[32,4096]{1,0:T(8,128)(2,1)} %get-tuple-element.321), channel_id=1, source_target_pairs={{0,8},{2,10},{4,12},{6,14},{8,0},{10,2},{12,4},{14,6},{16,24},{18,... | collective-permute-start | bytes 786440 | tf_op jit(solution)/shard_map/ppermute | solution.py:399
  43.9 76.9 %copy-start.9 = (f32[256,512]{1,0:T(8,128)}, f32[256,512]{1,0:T(8,128)S(1)}, u32[]{:S(2)}) copy-start(f32[256,512]{1,0:T(8,128)S(1)} %shard_map.57.refs_4_) | copy-start | bytes 1572868
  43.9 71.5 %collective-permute-start.23 = (f32[256,512]{1,0:T(8,128)S(1)}, f32[256,512]{1,0:T(8,128)S(1)}, u32[]{:S(2)}, u32[]{:S(2)}) collective-permute-start(f32[256,512]{1,0:T(8,128)S(1)} %shard_map.57.refs_4_), channel_id=1, source_target_pairs={{0,1},{1,0},{2,3},{3,2},{4,5},{5,4},{6,7},{7,6},{8,9},{9,8},{10,11... | collective-permute-start | bytes 1572872 | tf_op jit(solution)/shard_map/ppermute | solution.py:19
  79.4 20.2 %collective-permute-start.19 = (s32[3,16]{1,0:T(4,128)S(1)}, s32[3,16]{1,0:T(4,128)S(1)}, u32[]{:S(2)}, u32[]{:S(2)}) collective-permute-start(s32[3,16]{1,0:T(4,128)S(1)} %pad_add_fusion), channel_id=1, source_target_pairs={{0,8},{2,10},{4,12},{6,14},{8,0},{10,2},{12,4},{14,6},{16,24},{18,... | collective-permute-start | bytes 584 | tf_op jit(solution)/shard_map/ppermute | solution.py:354
  90.5 23.9 %collective-permute-start.20 = (s32[3,16]{1,0:T(4,128)S(1)}, s32[3,16]{1,0:T(4,128)S(1)}, u32[]{:S(2)}, u32[]{:S(2)}) collective-permute-start(s32[3,16]{1,0:T(4,128)S(1)} %pad_add_fusion), channel_id=1, source_target_pairs={{0,16},{2,18},{4,20},{6,22},{8,24},{10,26},{12,28},{14,30},{16,0},... | collective-permute-start | bytes 584 | tf_op jit(solution)/shard_map/ppermute | solution.py:354
  90.5 24.9 %collective-permute-start.21 = (s32[3,16]{1,0:T(4,128)S(1)}, s32[3,16]{1,0:T(4,128)S(1)}, u32[]{:S(2)}, u32[]{:S(2)}) collective-permute-start(s32[3,16]{1,0:T(4,128)S(1)} %pad_add_fusion), channel_id=1, source_target_pairs={{0,24},{2,26},{4,28},{6,30},{8,16},{10,18},{12,20},{14,22},{16,8},... | collective-permute-start | bytes 584 | tf_op jit(solution)/shard_map/ppermute | solution.py:354
  115.4 5.4 %copy-start.22 = (f32[256,512]{1,0:T(8,128)}, f32[256,512]{1,0:T(8,128)S(1)}, u32[]{:S(2)}) copy-start(f32[256,512]{1,0:T(8,128)S(1)} %collective-permute-done.23.refs_5_) | copy-start | bytes 1572868
  116.3 7.2 %copy-start.26 = (bf16[32,4096]{1,0:T(8,128)(2,1)S(1)}, bf16[32,4096]{1,0:T(8,128)(2,1)}, u32[]{:S(2)}) copy-start(bf16[32,4096]{1,0:T(8,128)(2,1)} %get-tuple-element.232) | copy-start | bytes 786436
  116.3 8.8 %copy-start.25 = (bf16[32,4096]{1,0:T(8,128)(2,1)S(1)}, bf16[32,4096]{1,0:T(8,128)(2,1)}, u32[]{:S(2)}) copy-start(bf16[32,4096]{1,0:T(8,128)(2,1)} %get-tuple-element.233) | copy-start | bytes 786436
  120.8 1.1 copy-start.11
  121.9 13.4 %collective-permute-start.26 = (bf16[512,512]{1,0:T(8,128)(2,1)S(1)}, bf16[512,512]{1,0:T(8,128)(2,1)S(1)}, u32[]{:S(2)}, u32[]{:S(2)}) collective-permute-start(bf16[512,512]{1,0:T(8,128)(2,1)S(1)} %get-tuple-element.236), channel_id=1, source_target_pairs={{0,1},{1,0},{2,3},{3,2},{4,5},{5,4},{6,7},{7,6},{8,9},{9,8},{10,11... | collective-permute-start | bytes 1572872 | tf_op jit(solution)/shard_map/ppermute | solution.py:227
  123.4 19.4 %collective-permute-start.24 = (bf16[32,4096]{1,0:T(8,128)(2,1)S(1)}, bf16[32,4096]{1,0:T(8,128)(2,1)S(1)}, u32[]{:S(2)}, u32[]{:S(2)}) collective-permute-start(bf16[32,4096]{1,0:T(8,128)(2,1)S(1)} %copy-done.26), channel_id=1, source_target_pairs={{0,16},{2,18},{4,20},{6,22},{8,24},{10,26},{12,28},{14,30},{16,0},... | collective-permute-start | bytes 786440 | tf_op jit(solution)/shard_map/ppermute | solution.py:399
  125.1 22.6 %collective-permute-start.25 = (bf16[32,4096]{1,0:T(8,128)(2,1)S(1)}, bf16[32,4096]{1,0:T(8,128)(2,1)S(1)}, u32[]{:S(2)}, u32[]{:S(2)}) collective-permute-start(bf16[32,4096]{1,0:T(8,128)(2,1)S(1)} %copy-done.25), channel_id=1, source_target_pairs={{0,24},{2,26},{4,28},{6,30},{8,16},{10,18},{12,20},{14,22},{16,8},... | collective-permute-start | bytes 786440 | tf_op jit(solution)/shard_map/ppermute | solution.py:399
  135.4 0.8 copy-start.23
  147.7 108.4 %all-to-all-start.1 = ((bf16[16,32,4096]{2,1,0:T(8,128)(2,1)}), bf16[16,32,4096]{2,1,0:T(8,128)(2,1)}, u32[]{:S(2)}, u32[]{:S(2)}) async-start(bf16[16,32,4096]{2,1,0:T(8,128)(2,1)} %bitcast.58), calls=%async_computation.1 | async-start | bytes 8388608 | tf_op jit(solution)/shard_map/all_to_all | solution.py:358
  154.2 2.2 copy-start.4
  156.4 4.9 %copy-start.5 = (bf16[512,4096]{1,0:T(8,128)(2,1)S(1)}, bf16[512,4096]{1,0:T(8,128)(2,1)}, u32[]{:S(2)}) copy-start(bf16[512,4096]{1,0:T(8,128)(2,1)} %all-gather.2.cloned.1.call-done.weights_ref.refs_1_) | copy-start | bytes 12582916
  159.0 17.7 %copy-start.8 = (f32[256,512]{1,0:T(8,128)}, f32[256,512]{1,0:T(8,128)S(1)}, u32[]{:S(2)}) copy-start(f32[256,512]{1,0:T(8,128)S(1)} %shard_map.61.refs_4_) | copy-start | bytes 1572868
  159.0 16.9 %collective-permute-start.28 = (f32[256,512]{1,0:T(8,128)S(1)}, f32[256,512]{1,0:T(8,128)S(1)}, u32[]{:S(2)}, u32[]{:S(2)}) collective-permute-start(f32[256,512]{1,0:T(8,128)S(1)} %shard_map.61.refs_4_), channel_id=1, source_target_pairs={{0,1},{1,0},{2,3},{3,2},{4,5},{5,4},{6,7},{7,6},{8,9},{9,8},{10,11... | collective-permute-start | bytes 1572872 | tf_op jit(solution)/shard_map/ppermute | solution.py:19
  160.7 16.0 %copy-start.7 = (bf16[128,4096]{1,0:T(8,128)(2,1)}, bf16[128,4096]{1,0:T(8,128)(2,1)S(1)}, u32[]{:S(2)}) copy-start(bf16[128,4096]{1,0:T(8,128)(2,1)S(1)} %constant_dynamic-update-slice_fusion.rows_ref.refs_0_) | copy-start | bytes 3145732
  164.1 0.7 copy-start.12
  164.8 11.0 %collective-permute-start.27 = (bf16[128,512]{1,0:T(8,128)(2,1)S(1)}, bf16[128,512]{1,0:T(8,128)(2,1)S(1)}, u32[]{:S(2)}, u32[]{:S(2)}) collective-permute-start(bf16[128,512]{1,0:T(8,128)(2,1)S(1)} %get-tuple-element.248), channel_id=1, source_target_pairs={{0,1},{1,0},{2,3},{3,2},{4,5},{5,4},{6,7},{7,6},{8,9},{9,8},{10,11... | collective-permute-start | bytes 393224 | tf_op jit(solution)/shard_map/ppermute | solution.py:227
  175.9 0.8 copy-start.27
  175.9 0.8 copy-start.21
  180.5 2.7 collective-permute-start.3
  181.2 2.0 collective-permute-start.4
  181.9 74.2 %collective-permute-start.5 = (bf16[32,4096]{1,0:T(8,128)(2,1)S(1)}, bf16[32,4096]{1,0:T(8,128)(2,1)S(1)}, u32[]{:S(2)}, u32[]{:S(2)}) collective-permute-start(bf16[32,4096]{1,0:T(8,128)(2,1)S(1)} %get-tuple-element.311), channel_id=1, source_target_pairs={{8,16},{10,18},{12,20},{14,22},{9,17},{11,19},{13,21},{15,23}} | collective-permute-start | bytes 786440 | tf_op jit(solution)/shard_map/cond/branch_1_fun/ppermute | solution.py:434
Sparse Core Ops, SparseCore 0:
  116.4 34.4 all-gather.1

commit v5 on v4

--- a/solution.py
+++ b/solution.py
@@ -341,12 +341,14 @@
     over = position >= slot_rows
     excess = jnp.maximum(counts - slot_rows, 0)
 
-    plane = slot // group
-    my_choice = jnp.argmax(excess.reshape(planes, group), axis=1).astype(jnp.int32)
-
-    is_mine = jnp.sum(
-        jnp.where(adapter_ids[:, None] // group == jnp.arange(planes)[None, :], my_choice, 0), axis=1
-    ) == adapter_ids % group
+    half = max(planes // 2, 1)
+    per_half = half * group
+    my_choice = jnp.argmax(excess.reshape(-1, per_half), axis=1).astype(jnp.int32)
+    is_mine = jnp.any(
+        jnp.arange(adapters // per_half)[None, :] * per_half + my_choice[None, :]
+        == adapter_ids[:, None],
+        axis=1,
+    )
     row_is_mine = jnp.any(by_slot & is_mine[None, :], axis=1)
 
     def add_over(value, steps):
@@ -363,10 +365,10 @@
     packed, tallies = lax.optimization_barrier((packed, tallies))
     arrived = exchange(packed)
 
-    over_target = jnp.where(
-        over & row_is_mine, (plane ^ my_plane) * slot_rows + position - slot_rows, -1
-    )
-    over_packed = pack(over_target, hidden, planes * slot_rows)
+    sides = planes // half
+    other_side = (slot // per_half != my_plane // half).astype(jnp.int32)
+    over_target = jnp.where(over & row_is_mine, other_side * slot_rows + position - slot_rows, -1)
+    over_packed = pack(over_target, hidden, sides * slot_rows)
 
     weights = sketch_weights(down_store[0], up_store[0])
     table = parts_mp(gram(weights))
@@ -392,13 +394,20 @@
     mine, tallies = lax.optimization_barrier((mine, tallies))
     tallies = add_over(tallies, range(group, owners, group))
 
-    over_blocks = over_packed.reshape(planes, slot_rows, width)
-    over_blocks = [over_blocks[step] for step in range(planes)]
+    over_blocks = over_packed.reshape(sides, slot_rows, width)
+    over_blocks = [over_blocks[side] for side in range(sides)]
 
     def to_plane(step, block):
         return lax.ppermute(block, "dp", [(i, i ^ (step * group)) for i in range(owners)])
 
-    over_arrived = [over_blocks[0]] + [to_plane(step, over_blocks[step]) for step in range(1, 2)]
+    def round_half(blocks):
+        step = 1
+        while step < half:
+            blocks = blocks + [to_plane(step, block) for block in blocks]
+            step *= 2
+        return blocks
+
+    over_arrived = round_half(over_blocks[:1])
     mine, tallies, arrived, over_arrived, over_blocks, table = lax.optimization_barrier(
         (mine, tallies, arrived, over_arrived, over_blocks, table)
     )
@@ -408,12 +417,14 @@
 
     sketched, narrow = sketch(arrived, weights, rank)
     sketched = sketch_parts(sketched, narrow)
-    later = [to_plane(step, over_blocks[step]) for step in range(2, planes)]
+    crossed = [to_plane(half, block) for block in over_blocks[1:]]
+    crossed, sketched[0] = lax.optimization_barrier((crossed, sketched[0]))
+    crossed = round_half(crossed)
     done = finish(arrived, sketched, table, weights, layers, model_width)
-    *later, done = lax.optimization_barrier((*later, done))
-    over_arrived = over_arrived + later
+    *crossed, done = lax.optimization_barrier((*crossed, done))
 
     returned = [exchange(done)]
+    over_arrived = over_arrived + crossed
     plane_weights, over_arrived[0], done = lax.optimization_barrier(
         (plane_weights, over_arrived[0], done)
     )

time: 271 us -> 270 us (level)
  waiting for transfers between devices: 149 us -> 142 us
  starting transfers between devices: 39.4 us -> 42.7 us
    ppermute x3, waiting for transfers between devices: 72.8 us -> 56.8 us  [moved(): got.append(lax.ppermute(blocks[step], 'dp', pairs))]
    all_to_all x2, waiting for transfers between devices: 0.85 us -> 15.7 us  [exchange(): lax.all_to_all(blocks, 'dp', 0, 0, tiled=True)]
    ppermute x2, waiting for transfers between devices: 15 us -> 4.89 us  [sketch_parts(): return [sketched, lax.ppermute(narrow, 'mp', [(0, 1), (1, 0)])]]
    ppermute x3, waiting for transfers between devices: 4.89 us -> 10.4 us  [to_plane(): lax.ppermute(block, 'dp', [(i, i ^ step * group) for i in range(owners)])]
    unnamed x37 -> x35, local copies, waits for them, and re-layouts: 8.64 us -> 8.64 us
where the time goes in v5:
time: 270 us; the launch traced here: 267 us
  waiting for transfers between devices  142 us (53%)
  starting transfers between devices  42.7 us (16%)
  Pallas kernels  38.6 us (14%)
  between operations  19.8 us (7%)
  other arithmetic  12 us (4%)
  local copies, waits for them, and re-layouts  11.2 us (4%)
    ppermute x3, waiting for transfers between devices, moved(): got.append(lax.ppermute(blocks[step], 'dp', pairs))  56.8 us
    pallas_call x9, Pallas kernels, call(): pl.pallas_call(body, out_shape=[out for out, _ in outs], in_specs=in_spec...  38.6 us
    ppermute x2, waiting for transfers between devices, local(): taken = lax.ppermute(give, 'dp', [(i, i ^ step) for i in range(owners)])  30.8 us
    ppermute x6, waiting for transfers between devices, add_over(): return value + sum((lax.ppermute(value, 'dp', p) for p in pairs))  23.4 us
    all_to_all x2, waiting for transfers between devices, exchange(): lax.all_to_all(blocks, 'dp', 0, 0, tiled=True)  15.7 us
    ppermute x6, starting transfers between devices, add_over(): return value + sum((lax.ppermute(value, 'dp', p) for p in pairs))  14.5 us
    all_to_all x2, starting transfers between devices, exchange(): lax.all_to_all(blocks, 'dp', 0, 0, tiled=True)  12.3 us
    ppermute x3, waiting for transfers between devices, to_plane(): lax.ppermute(block, 'dp', [(i, i ^ step * group) for i in range(owners)])  10.4 us
  transfers between devices with their start and end apart: 21, of which 9 were waited for; matrix products, arithmetic and copies ran while one was open for 5% of the time, Pallas kernels for 12%

profile of v5, /device:TPU:16, one launch (start us, length us, event | category | flops | bytes accessed | tf_op | source)
XLA Modules:
  0.0 267.4 jit_solution(12827475646440385690)
XLA Ops:
  6.5 0.8 select_reduce_fusion
  8.4 1.6 collective-permute-start.15
  11.2 5.8 %shard_map.55 = bf16[512,4096]{1,0:T(8,128)(2,1)} custom-call(s32[1,512]{1,0:T(1,128)} %get-tuple-element.326.target_ref, bf16[512,4096]{1,0:T(8,128)(2,1)} %hidden_ref.3), custom_call_target="tpu_custom_call" | custom-call | flops 1 | bytes 1 | tf_op jit(solution)/shard_map/pallas_call | solution.py:36
  17.1 6.3 %all-to-all-start = ((bf16[16,32,4096]{2,1,0:T(8,128)(2,1)}), bf16[16,32,4096]{2,1,0:T(8,128)(2,1)}, u32[]{:S(2)}, u32[]{:S(2)}) async-start(bf16[16,32,4096]{2,1,0:T(8,128)(2,1)} %bitcast.57), calls=%async_computation | async-start | bytes 8388608 | tf_op jit(solution)/shard_map/all_to_all | solution.py:360
  23.7 1.9 pad_maximum_fusion.weights_ref.refs_1_
  25.6 2.0 copy-done.13
  27.9 3.9 %shard_map.56 = bf16[64,4096]{1,0:T(8,128)(2,1)} custom-call(s32[1,512]{1,0:T(1,128)} %get-tuple-element.325.target_ref, bf16[512,4096]{1,0:T(8,128)(2,1)} %hidden_ref.3), custom_call_target="tpu_custom_call" | custom-call | flops 1 | bytes 1 | tf_op jit(solution)/shard_map/pallas_call | solution.py:36
  34.6 2.0 bitcast_select_fusion
  36.6 1.1 constant_dynamic-slice_fusion
  37.7 1.5 collective-permute-start.18
  39.1 0.7 fusion.17
  39.9 2.1 collective-permute-start.22
  42.0 2.6 shard_map.57.refs_4_
  44.6 1.6 collective-permute-start.23
  47.4 30.8 %collective-permute-done.18 = bf16[1,128,4096]{2,1,0:T(8,128)(2,1)} collective-permute-done((bf16[1,128,4096]{2,1,0:T(8,128)(2,1)}, bf16[1,128,4096]{2,1,0:T(8,128)(2,1)}, u32[]{:S(2)}, u32[]{:S(2)}) %collective-permute-start.18) | collective-permute-done | bytes 1048608 | tf_op jit(solution)/shard_map/ppermute | solution.py:390
  78.3 1.1 select_bitcast_fusion
  79.4 11.1 %collective-permute-start.19 = (s32[3,16]{1,0:T(4,128)S(1)}, s32[3,16]{1,0:T(4,128)S(1)}, u32[]{:S(2)}, u32[]{:S(2)}) collective-permute-start(s32[3,16]{1,0:T(4,128)S(1)} %pad_add_fusion), channel_id=1, source_target_pairs={{0,8},{2,10},{4,12},{6,14},{8,0},{10,2},{12,4},{14,6},{16,24},{18,... | collective-permute-start | bytes 584 | tf_op jit(solution)/shard_map/ppermute | solution.py:356
  90.5 1.5 collective-permute-start.21
  92.0 7.6 %collective-permute-done.19 = s32[3,16]{1,0:T(4,128)S(1)} collective-permute-done((s32[3,16]{1,0:T(4,128)S(1)}, s32[3,16]{1,0:T(4,128)S(1)}, u32[]{:S(2)}, u32[]{:S(2)}) %collective-permute-start.19) | collective-permute-done | bytes 224 | tf_op jit(solution)/shard_map/ppermute | solution.py:356
  99.6 14.9 %collective-permute-done.20 = s32[3,16]{1,0:T(4,128)S(1)} collective-permute-done((s32[3,16]{1,0:T(4,128)S(1)}, s32[3,16]{1,0:T(4,128)S(1)}, u32[]{:S(2)}, u32[]{:S(2)}) %collective-permute-start.20) | collective-permute-done | bytes 224 | tf_op jit(solution)/shard_map/ppermute | solution.py:356
  114.5 0.9 collective-permute-done.21
  115.4 0.8 all-to-all-done
  116.3 4.5 %shard_map.58 = (f32[512,640]{1,0:T(8,128)S(1)}, bf16[512,512]{1,0:T(8,128)(2,1)S(1)}) custom-call(bf16[512,4096]{1,0:T(8,128)(2,1)} %bitcast.15.rows_ref.refs_0_, bf16[512,4096]{1,0:T(8,128)(2,1)} %copy-done.13), custom_call_target="tpu_custom_call" | custom-call | flops 1 | bytes 1 | tf_op jit(solution)/shard_map/pallas_call | solution.py:36
  120.8 1.1 copy-done.11
  121.9 1.5 collective-permute-start.26
  123.4 1.7 collective-permute-start.24
  125.1 10.4 %collective-permute-done.24 = bf16[32,4096]{1,0:T(8,128)(2,1)S(1)} collective-permute-done((bf16[32,4096]{1,0:T(8,128)(2,1)S(1)}, bf16[32,4096]{1,0:T(8,128)(2,1)S(1)}, u32[]{:S(2)}, u32[]{:S(2)}) %collective-permute-start.24) | collective-permute-done | bytes 262176 | tf_op jit(solution)/shard_map/ppermute | solution.py:401
  135.5 2.5 collective-permute-start.25
  138.0 0.8 copy-done.23
  138.8 6.7 %shard_map.59 = bf16[512,4096]{1,0:T(8,128)(2,1)} custom-call(bf16[512,4096]{1,0:T(8,128)(2,1)} %bitcast.15.rows_ref.refs_0_, bf16[512,4096]{1,0:T(8,128)(2,1)} %copy-done.13, f32[512,640]{1,0:T(8,128)} %copy-done.11, bf16[512,512]{1,0:T(8,128)(2,1)} %copy-done.23, f32[256,512]{1,0:T(8,128)} %copy-done.9, f32[256,512]{1,0:T(8,128)} %copy-done.22), custom_call_target="tpu_custom_call" | custom-call | flops 1 | bytes 1 | tf_op jit(solution)/shard_map/pallas_call | solution.py:36
  145.4 5.9 %all-to-all-start.1 = ((bf16[16,32,4096]{2,1,0:T(8,128)(2,1)}), bf16[16,32,4096]{2,1,0:T(8,128)(2,1)}, u32[]{:S(2)}, u32[]{:S(2)}) async-start(bf16[16,32,4096]{2,1,0:T(8,128)(2,1)} %bitcast.58), calls=%async_computation.1 | async-start | bytes 8388608 | tf_op jit(solution)/shard_map/all_to_all | solution.py:360
  151.4 0.7 fusion.10
  152.8 2.2 copy-done.4
  155.0 2.6 shard_map.61.refs_4_
  158.2 1.0 constant_dynamic-update-slice_fusion.2
  159.9 2.8 %shard_map.60 = (f32[128,640]{1,0:T(8,128)S(1)}, bf16[128,512]{1,0:T(8,128)(2,1)S(1)}) custom-call(bf16[128,4096]{1,0:T(8,128)(2,1)S(1)} %constant_dynamic-update-slice_fusion.rows_ref.refs_0_, bf16[512,4096]{1,0:T(8,128)(2,1)S(1)} %copy-done.5), custom_call_target="tpu_custom_call" | custom-call | flops 1 | bytes 1 | tf_op jit(solution)/shard_map/pallas_call | solution.py:36
  162.7 0.7 copy-done.12
  163.5 1.5 collective-permute-start.27
  164.9 1.4 convert_reduce_fusion.2
  169.5 4.9 %collective-permute-done.27.refs_3_ = bf16[128,512]{1,0:T(8,128)(2,1)S(1)} collective-permute-done((bf16[128,512]{1,0:T(8,128)(2,1)S(1)}, bf16[128,512]{1,0:T(8,128)(2,1)S(1)}, u32[]{:S(2)}, u32[]{:S(2)}) %collective-permute-start.27) | collective-permute-done | bytes 131104 | tf_op jit(solution)/shard_map/ppermute | solution.py:227
  174.4 0.8 copy-done.21
  175.3 3.7 %shard_map.62 = bf16[128,4096]{1,0:T(8,128)(2,1)S(1)} custom-call(bf16[128,4096]{1,0:T(8,128)(2,1)} %copy-done.7, bf16[512,4096]{1,0:T(8,128)(2,1)} %all-gather.2.cloned.1.call-done.weights_ref.refs_1_, f32[128,640]{1,0:T(8,128)} %copy-done.12, bf16[128,512]{1,0:T(8,128)(2,1)} %copy-done.26, f32[256,512]{1,0:T(8,128)} %copy-done.8, f32[256,512]{1,0:T(8,128)} %copy-done.21), custom_call_target="tpu_custom_call" | custom-call | flops 1 | bytes 1 | tf_op jit(solution)/shard_map/pallas_call | solution.py:36
  179.0 59.6 %conditional.1 = (bf16[32,4096]{1,0:T(8,128)(2,1)S(1)}) conditional(s32[]{:T(128)} %clamp.3, (s32[]{:T(128)}, bf16[128,4096]{1,0:T(8,128)(2,1)S(1)}) %tuple.47, (s32[]{:T(128)}, bf16[128,4096]{1,0:T(8,128)(2,1)S(1)}) %tuple.47, (s32[]{:T(128)}, bf16[128,4096]{1,0:T(8,128)(2,1)S(1)}) %tuple.47, (s32[]{:T(128)}, ...), branch_computations={%region_8.9_spmd, %region_9.10_spmd, %region_10.11_spmd, %region_1... | conditional | flops 524289 | bytes 6029450 | solution.py:451
  180.5 1.3 collective-permute-start.9
  181.8 56.8 %collective-permute-done.9 = bf16[32,4096]{1,0:T(8,128)(2,1)S(1)} collective-permute-done((bf16[32,4096]{1,0:T(8,128)(2,1)S(1)}, bf16[32,4096]{1,0:T(8,128)(2,1)S(1)}, u32[]{:S(2)}, u32[]{:S(2)}) %collective-permute-start.9) | collective-permute-done | bytes 262176 | tf_op jit(solution)/shard_map/cond/branch_3_fun/ppermute | solution.py:445
  238.6 14.9 %all-to-all-done.1 = bf16[16,32,4096]{2,1,0:T(8,128)(2,1)} async-done(((bf16[16,32,4096]{2,1,0:T(8,128)(2,1)}), bf16[16,32,4096]{2,1,0:T(8,128)(2,1)}, u32[]{:S(2)}, u32[]{:S(2)}) %all-to-all-start.1) | async-done | bytes 4194336 | tf_op jit(solution)/shard_map/all_to_all | solution.py:360
  253.5 6.1 %shard_map.63 = bf16[512,4096]{1,0:T(8,128)(2,1)} custom-call(s32[512,1]{1,0:T(8,128)S(1)} %copy.18.refs_0_, s32[512,1]{1,0:T(8,128)S(1)} %copy.19.refs_1_, bf16[512,4096]{1,0:T(8,128)(2,1)} %bitcast.20.refs_2_, bf16[32,4096]{1,0:T(8,128)(2,1)S(1)} %get-tuple-element.450.refs_3_), custom_call_target="tpu_custom_call" | custom-call | flops 1 | bytes 1 | tf_op jit(solution)/shard_map/pallas_call | solution.py:36
  259.6 0.9 while.13
  (79 shorter events, 7.8 us)
Async XLA Ops:
  8.3 8.7 %collective-permute-start.14 = (s32[2,16]{1,0:T(2,128)S(1)}, s32[2,16]{1,0:T(2,128)S(1)}, u32[]{:S(2)}, u32[]{:S(2)}) collective-permute-start(s32[2,16]{1,0:T(2,128)S(1)} %pad_add_fusion.1), channel_id=1, source_target_pairs={{0,2},{2,0},{4,6},{6,4},{8,10},{10,8},{12,14},{14,12},{16,18},{18,... | collective-permute-start | bytes 392 | tf_op jit(solution)/shard_map/ppermute | solution.py:356
  8.4 8.7 %collective-permute-start.15 = (s32[2,16]{1,0:T(2,128)S(1)}, s32[2,16]{1,0:T(2,128)S(1)}, u32[]{:S(2)}, u32[]{:S(2)}) collective-permute-start(s32[2,16]{1,0:T(2,128)S(1)} %pad_add_fusion.1), channel_id=1, source_target_pairs={{0,4},{2,6},{4,0},{6,2},{8,12},{10,14},{12,8},{14,10},{16,20},{18,... | collective-permute-start | bytes 392 | tf_op jit(solution)/shard_map/ppermute | solution.py:356
  9.9 7.1 %collective-permute-start.16 = (s32[2,16]{1,0:T(2,128)S(1)}, s32[2,16]{1,0:T(2,128)S(1)}, u32[]{:S(2)}, u32[]{:S(2)}) collective-permute-start(s32[2,16]{1,0:T(2,128)S(1)} %pad_add_fusion.1), channel_id=1, source_target_pairs={{0,6},{2,4},{4,2},{6,0},{8,14},{10,12},{12,10},{14,8},{16,22},{18,... | collective-permute-start | bytes 392 | tf_op jit(solution)/shard_map/ppermute | solution.py:356
  17.1 6.6 %copy-start.19 = (bf16[1,4,64,4096]{3,2,1,0:T(8,128)(2,1)S(1)}, bf16[1,4,64,4096]{3,2,1,0:T(8,128)(2,1)}, u32[]{:S(2)}) copy-start(bf16[1,4,64,4096]{3,2,1,0:T(8,128)(2,1)} %param.15) | copy-start | bytes 6291460
  17.1 99.2 %all-to-all-start = ((bf16[16,32,4096]{2,1,0:T(8,128)(2,1)}), bf16[16,32,4096]{2,1,0:T(8,128)(2,1)}, u32[]{:S(2)}, u32[]{:S(2)}) async-start(bf16[16,32,4096]{2,1,0:T(8,128)(2,1)} %bitcast.57), calls=%async_computation | async-start | bytes 8388608 | tf_op jit(solution)/shard_map/all_to_all | solution.py:360
  23.4 129.4 %all-gather.2.cloned.1.call-start = ((), (), s32[]{:S(2)}) async-start(), calls=%async_computation.2 | async-start | bytes 5242880 | tf_op jit(solution)/shard_map/all_gather | solution.py:416
  25.6 2.0 copy-start.13
  27.7 6.9 %collective-permute-start.17 = (bf16[2,128,4096]{2,1,0:T(8,128)(2,1)S(1)}, bf16[2,128,4096]{2,1,0:T(8,128)(2,1)}, u32[]{:S(2)}, u32[]{:S(2)}) collective-permute-start(bf16[2,128,4096]{2,1,0:T(8,128)(2,1)S(1)} %dynamic-slice_bitcast_fusion), channel_id=1, source_target_pairs={{0,2},{2,0},{4,6},{6,4},{8,10},{10,8},{12,14},{14,12},{16,18},{18,... | collective-permute-start | bytes 6291464 | tf_op jit(solution)/shard_map/ppermute | solution.py:390
  34.6 4.5 %copy-start.18 = (bf16[64,4096]{1,0:T(8,128)(2,1)S(1)}, bf16[64,4096]{1,0:T(8,128)(2,1)}, u32[]{:S(2)}) copy-start(bf16[64,4096]{1,0:T(8,128)(2,1)} %shard_map.56) | copy-start | bytes 1572868
  34.6 7.4 %copy-start.14 = (bf16[512,4096]{1,0:T(8,128)(2,1)S(1)}, bf16[512,4096]{1,0:T(8,128)(2,1)}, u32[]{:S(2)}) copy-start(bf16[512,4096]{1,0:T(8,128)(2,1)} %copy-done.13) | copy-start | bytes 12582916
  37.7 40.6 %collective-permute-start.18 = (bf16[1,128,4096]{2,1,0:T(8,128)(2,1)}, bf16[1,128,4096]{2,1,0:T(8,128)(2,1)}, u32[]{:S(2)}, u32[]{:S(2)}) collective-permute-start(bf16[1,128,4096]{2,1,0:T(8,128)(2,1)} %constant_dynamic-slice_fusion), channel_id=1, source_target_pairs={{0,4},{2,6},{4,0},{6,2},{8,12},{10,14},{12,8},{14,10},{16,20},{18,... | collective-permute-start | bytes 3145736 | tf_op jit(solution)/shard_map/ppermute | solution.py:390
  39.9 75.5 %collective-permute-start.22 = (bf16[32,4096]{1,0:T(8,128)(2,1)S(1)}, bf16[32,4096]{1,0:T(8,128)(2,1)}, u32[]{:S(2)}, u32[]{:S(2)}) collective-permute-start(bf16[32,4096]{1,0:T(8,128)(2,1)S(1)} %get-tuple-element.244), channel_id=1, source_target_pairs={{0,8},{2,10},{4,12},{6,14},{8,0},{10,2},{12,4},{14,6},{16,24},{18,... | collective-permute-start | bytes 786440 | tf_op jit(solution)/shard_map/ppermute | solution.py:401
  44.6 76.2 %copy-start.9 = (f32[256,512]{1,0:T(8,128)}, f32[256,512]{1,0:T(8,128)S(1)}, u32[]{:S(2)}) copy-start(f32[256,512]{1,0:T(8,128)S(1)} %shard_map.57.refs_4_) | copy-start | bytes 1572868
  44.6 70.8 %collective-permute-start.23 = (f32[256,512]{1,0:T(8,128)S(1)}, f32[256,512]{1,0:T(8,128)S(1)}, u32[]{:S(2)}, u32[]{:S(2)}) collective-permute-start(f32[256,512]{1,0:T(8,128)S(1)} %shard_map.57.refs_4_), channel_id=1, source_target_pairs={{0,1},{1,0},{2,3},{3,2},{4,5},{5,4},{6,7},{7,6},{8,9},{9,8},{10,11... | collective-permute-start | bytes 1572872 | tf_op jit(solution)/shard_map/ppermute | solution.py:19
  79.4 20.2 %collective-permute-start.19 = (s32[3,16]{1,0:T(4,128)S(1)}, s32[3,16]{1,0:T(4,128)S(1)}, u32[]{:S(2)}, u32[]{:S(2)}) collective-permute-start(s32[3,16]{1,0:T(4,128)S(1)} %pad_add_fusion), channel_id=1, source_target_pairs={{0,8},{2,10},{4,12},{6,14},{8,0},{10,2},{12,4},{14,6},{16,24},{18,... | collective-permute-start | bytes 584 | tf_op jit(solution)/shard_map/ppermute | solution.py:356
  90.5 23.9 %collective-permute-start.20 = (s32[3,16]{1,0:T(4,128)S(1)}, s32[3,16]{1,0:T(4,128)S(1)}, u32[]{:S(2)}, u32[]{:S(2)}) collective-permute-start(s32[3,16]{1,0:T(4,128)S(1)} %pad_add_fusion), channel_id=1, source_target_pairs={{0,16},{2,18},{4,20},{6,22},{8,24},{10,26},{12,28},{14,30},{16,0},... | collective-permute-start | bytes 584 | tf_op jit(solution)/shard_map/ppermute | solution.py:356
  90.5 24.9 %collective-permute-start.21 = (s32[3,16]{1,0:T(4,128)S(1)}, s32[3,16]{1,0:T(4,128)S(1)}, u32[]{:S(2)}, u32[]{:S(2)}) collective-permute-start(s32[3,16]{1,0:T(4,128)S(1)} %pad_add_fusion), channel_id=1, source_target_pairs={{0,24},{2,26},{4,28},{6,30},{8,16},{10,18},{12,20},{14,22},{16,8},... | collective-permute-start | bytes 584 | tf_op jit(solution)/shard_map/ppermute | solution.py:356
  115.4 5.4 %copy-start.22 = (f32[256,512]{1,0:T(8,128)}, f32[256,512]{1,0:T(8,128)S(1)}, u32[]{:S(2)}) copy-start(f32[256,512]{1,0:T(8,128)S(1)} %collective-permute-done.23.refs_5_) | copy-start | bytes 1572868
  116.3 7.1 %copy-start.25 = (bf16[32,4096]{1,0:T(8,128)(2,1)S(1)}, bf16[32,4096]{1,0:T(8,128)(2,1)}, u32[]{:S(2)}) copy-start(bf16[32,4096]{1,0:T(8,128)(2,1)} %get-tuple-element.233) | copy-start | bytes 786436
  120.8 1.1 copy-start.11
  121.9 16.0 %collective-permute-start.26 = (bf16[512,512]{1,0:T(8,128)(2,1)S(1)}, bf16[512,512]{1,0:T(8,128)(2,1)S(1)}, u32[]{:S(2)}, u32[]{:S(2)}) collective-permute-start(bf16[512,512]{1,0:T(8,128)(2,1)S(1)} %get-tuple-element.238), channel_id=1, source_target_pairs={{0,1},{1,0},{2,3},{3,2},{4,5},{5,4},{6,7},{7,6},{8,9},{9,8},{10,11... | collective-permute-start | bytes 1572872 | tf_op jit(solution)/shard_map/ppermute | solution.py:227
  123.4 12.0 %collective-permute-start.24 = (bf16[32,4096]{1,0:T(8,128)(2,1)S(1)}, bf16[32,4096]{1,0:T(8,128)(2,1)S(1)}, u32[]{:S(2)}, u32[]{:S(2)}) collective-permute-start(bf16[32,4096]{1,0:T(8,128)(2,1)S(1)} %copy-done.25), channel_id=1, source_target_pairs={{0,16},{2,18},{4,20},{6,22},{8,24},{10,26},{12,28},{14,30},{16,0},... | collective-permute-start | bytes 786440 | tf_op jit(solution)/shard_map/ppermute | solution.py:401
  135.5 9.9 %collective-permute-start.25 = (bf16[32,4096]{1,0:T(8,128)(2,1)S(1)}, bf16[32,4096]{1,0:T(8,128)(2,1)S(1)}, u32[]{:S(2)}, u32[]{:S(2)}) collective-permute-start(bf16[32,4096]{1,0:T(8,128)(2,1)S(1)} %collective-permute-done.24), channel_id=1, source_target_pairs={{0,8},{2,10},{4,12},{6,14},{8,0},{10,2},{12,4},{14,6},{16,24},{18,... | collective-permute-start | bytes 786440 | tf_op jit(solution)/shard_map/ppermute | solution.py:401
  138.0 0.8 copy-start.23
  145.4 108.1 %all-to-all-start.1 = ((bf16[16,32,4096]{2,1,0:T(8,128)(2,1)}), bf16[16,32,4096]{2,1,0:T(8,128)(2,1)}, u32[]{:S(2)}, u32[]{:S(2)}) async-start(bf16[16,32,4096]{2,1,0:T(8,128)(2,1)} %bitcast.58), calls=%async_computation.1 | async-start | bytes 8388608 | tf_op jit(solution)/shard_map/all_to_all | solution.py:360
  152.8 2.2 copy-start.4
  155.0 4.9 %copy-start.5 = (bf16[512,4096]{1,0:T(8,128)(2,1)S(1)}, bf16[512,4096]{1,0:T(8,128)(2,1)}, u32[]{:S(2)}) copy-start(bf16[512,4096]{1,0:T(8,128)(2,1)} %all-gather.2.cloned.1.call-done.weights_ref.refs_1_) | copy-start | bytes 12582916
  157.6 17.7 %copy-start.8 = (f32[256,512]{1,0:T(8,128)}, f32[256,512]{1,0:T(8,128)S(1)}, u32[]{:S(2)}) copy-start(f32[256,512]{1,0:T(8,128)S(1)} %shard_map.61.refs_4_) | copy-start | bytes 1572868
  157.6 16.9 %collective-permute-start.28 = (f32[256,512]{1,0:T(8,128)S(1)}, f32[256,512]{1,0:T(8,128)S(1)}, u32[]{:S(2)}, u32[]{:S(2)}) collective-permute-start(f32[256,512]{1,0:T(8,128)S(1)} %shard_map.61.refs_4_), channel_id=1, source_target_pairs={{0,1},{1,0},{2,3},{3,2},{4,5},{5,4},{6,7},{7,6},{8,9},{9,8},{10,11... | collective-permute-start | bytes 1572872 | tf_op jit(solution)/shard_map/ppermute | solution.py:19
  159.2 16.0 %copy-start.7 = (bf16[128,4096]{1,0:T(8,128)(2,1)}, bf16[128,4096]{1,0:T(8,128)(2,1)S(1)}, u32[]{:S(2)}) copy-start(bf16[128,4096]{1,0:T(8,128)(2,1)S(1)} %constant_dynamic-update-slice_fusion.rows_ref.refs_0_) | copy-start | bytes 3145732
  162.7 0.7 copy-start.12
  163.5 11.0 %collective-permute-start.27 = (bf16[128,512]{1,0:T(8,128)(2,1)S(1)}, bf16[128,512]{1,0:T(8,128)(2,1)S(1)}, u32[]{:S(2)}, u32[]{:S(2)}) collective-permute-start(bf16[128,512]{1,0:T(8,128)(2,1)S(1)} %get-tuple-element.250), channel_id=1, source_target_pairs={{0,1},{1,0},{2,3},{3,2},{4,5},{5,4},{6,7},{7,6},{8,9},{9,8},{10,11... | collective-permute-start | bytes 393224 | tf_op jit(solution)/shard_map/ppermute | solution.py:227
  174.4 0.8 copy-start.26
  174.4 0.8 copy-start.21
  179.1 2.7 %collective-permute-start.10 = (bf16[32,4096]{1,0:T(8,128)(2,1)S(1)}, bf16[32,4096]{1,0:T(8,128)(2,1)S(1)}, u32[]{:S(2)}, u32[]{:S(2)}) collective-permute-start(bf16[32,4096]{1,0:T(8,128)(2,1)S(1)} %get-tuple-element.320), channel_id=1, source_target_pairs={{24,8},{26,10},{28,12},{30,14},{25,9},{27,11},{29,13},{31,15}} | collective-permute-start | bytes 786440 | tf_op jit(solution)/shard_map/cond/branch_3_fun/ppermute | solution.py:445
  179.8 2.0 collective-permute-start.11
  180.5 58.1 %collective-permute-start.9 = (bf16[32,4096]{1,0:T(8,128)(2,1)S(1)}, bf16[32,4096]{1,0:T(8,128)(2,1)S(1)}, u32[]{:S(2)}, u32[]{:S(2)}) collective-permute-start(bf16[32,4096]{1,0:T(8,128)(2,1)S(1)} %get-tuple-element.318), channel_id=1, source_target_pairs={{24,16},{26,18},{28,20},{30,22},{25,17},{27,19},{29,21},{31,23}} | collective-permute-start | bytes 786440 | tf_op jit(solution)/shard_map/cond/branch_3_fun/ppermute | solution.py:445
Sparse Core Ops, SparseCore 0:
  116.4 34.4 all-gather.1

commit v6 on v5

--- a/solution.py
+++ b/solution.py
@@ -269,14 +269,22 @@
     count, width = rows.shape
     half = weights.shape[0] // 2
     tiles = tiling(width)
+    far = [k for k, part in enumerate(sketched) if part.dtype == BF16]
 
     def body(*refs):
         rows_ref, weights_ref = refs[:2]
         sketch_refs = refs[2 : 2 + len(sketched)]
         table_refs = refs[2 + len(sketched) :][: len(tables)]
-        out_ref, rows_buf, up_buf, out_buf, in_sems, out_sems = refs[-6:]
+        out_ref, rows_buf, up_buf, out_buf, in_sems, out_sems = refs[-6 - 2 * len(far) :][:6]
+        landed = {}
+        for number, (buffer, sem) in zip(far, [refs[-2:]] if far else []):
+            landed[number] = (pltpu.make_async_copy(sketch_refs[number], buffer, sem), buffer)
+            landed[number][0].start()
         up_ref = weights_ref.at[pl.ds(half, half), :]
         copies = start_all([rows_ref, up_ref], [rows_buf, up_buf], in_sems, tiles)
+        for copy, _ in landed.values():
+            copy.wait()
+        sketch_refs = [landed[k][1] if k in landed else ref for k, ref in enumerate(sketch_refs)]
         whole_sketch = sum(widen(ref[...], 2 * half, half // layers) for ref in sketch_refs)
         whole_table = sum(ref[...] for ref in table_refs)
         low = low_rank(whole_sketch, whole_table, layers, model_width)
@@ -297,13 +305,15 @@
         body,
         [(jax.ShapeDtypeStruct((count, width), BF16), True)],
         (rows, weights, *sketched, *tables),
-        [0, 1],
+        [0, 1, *[2 + k for k in far]],
         [
             pltpu.VMEM((count, width), BF16),
             pltpu.VMEM((half, width), BF16),
             pltpu.VMEM((count, width), BF16),
             pltpu.SemaphoreType.DMA((2, len(tiles))),
             pltpu.SemaphoreType.DMA((1, len(tiles))),
+            *[pltpu.VMEM(sketched[k].shape, BF16) for k in far],
+            *[pltpu.SemaphoreType.DMA for _ in far],
         ],
         vmem=60,
     )[0]

time: 270 us -> 272 us (level)
  Pallas kernels: 38.6 us -> 42.9 us
    all_to_all x2, waiting for transfers between devices: 15.7 us -> 23.8 us  [exchange(): lax.all_to_all(blocks, 'dp', 0, 0, tiled=True)]
    ppermute x3, waiting for transfers between devices: 56.8 us -> 48.9 us  [moved(): got.append(lax.ppermute(blocks[step], 'dp', pairs))]
    pallas_call x9, Pallas kernels: 38.6 us -> 42.9 us  [call(): pl.pallas_call(body, out_shape=[out for out, _ in outs], in_specs=in_spec...]
  transfers between devices with their start and end apart: 21 -> 21, of which waited for: 9 -> 9; matrix products, arithmetic and copies ran while one was open for 5% -> 5% of each run, Pallas kernels for 12% -> 14%
where the time goes in v6:
time: 272 us; the launch traced here: 271 us
  waiting for transfers between devices  143 us (53%)
  Pallas kernels  42.9 us (16%)
  starting transfers between devices  41.4 us (15%)
  between operations  19.8 us (7%)
  other arithmetic  12 us (4%)
  local copies, waits for them, and re-layouts  11.2 us (4%)
    ppermute x3, waiting for transfers between devices, moved(): got.append(lax.ppermute(blocks[step], 'dp', pairs))  48.9 us
    pallas_call x9, Pallas kernels, call(): pl.pallas_call(body, out_shape=[out for out, _ in outs], in_specs=in_spec...  42.9 us
    ppermute x2, waiting for transfers between devices, local(): taken = lax.ppermute(give, 'dp', [(i, i ^ step) for i in range(owners)])  31.5 us
    all_to_all x2, waiting for transfers between devices, exchange(): lax.all_to_all(blocks, 'dp', 0, 0, tiled=True)  23.8 us
    ppermute x6, waiting for transfers between devices, add_over(): return value + sum((lax.ppermute(value, 'dp', p) for p in pairs))  23.4 us
    ppermute x6, starting transfers between devices, add_over(): return value + sum((lax.ppermute(value, 'dp', p) for p in pairs))  14.5 us
    all_to_all x2, starting transfers between devices, exchange(): lax.all_to_all(blocks, 'dp', 0, 0, tiled=True)  11.6 us
    ppermute x3, waiting for transfers between devices, to_plane(): lax.ppermute(block, 'dp', [(i, i ^ step * group) for i in range(owners)])  10.4 us
  transfers between devices with their start and end apart: 21, of which 9 were waited for; matrix products, arithmetic and copies ran while one was open for 5% of the time, Pallas kernels for 14%

profile of v6, /device:TPU:16, one launch (start us, length us, event | category | flops | bytes accessed | tf_op | source)
XLA Modules:
  0.0 271.1 jit_solution(12469415562999580997)
XLA Ops:
  6.5 0.8 select_reduce_fusion
  8.4 1.6 collective-permute-start.15
  11.2 5.8 %shard_map.55 = bf16[512,4096]{1,0:T(8,128)(2,1)} custom-call(s32[1,512]{1,0:T(1,128)} %get-tuple-element.326.target_ref, bf16[512,4096]{1,0:T(8,128)(2,1)} %hidden_ref.3), custom_call_target="tpu_custom_call" | custom-call | flops 1 | bytes 1 | tf_op jit(solution)/shard_map/pallas_call | solution.py:36
  17.1 6.3 %all-to-all-start = ((bf16[16,32,4096]{2,1,0:T(8,128)(2,1)}), bf16[16,32,4096]{2,1,0:T(8,128)(2,1)}, u32[]{:S(2)}, u32[]{:S(2)}) async-start(bf16[16,32,4096]{2,1,0:T(8,128)(2,1)} %bitcast.57), calls=%async_computation | async-start | bytes 8388608 | tf_op jit(solution)/shard_map/all_to_all | solution.py:370
  23.7 1.9 pad_maximum_fusion.weights_ref.refs_1_
  25.6 2.0 copy-done.13
  27.9 3.9 %shard_map.56 = bf16[64,4096]{1,0:T(8,128)(2,1)} custom-call(s32[1,512]{1,0:T(1,128)} %get-tuple-element.325.target_ref, bf16[512,4096]{1,0:T(8,128)(2,1)} %hidden_ref.3), custom_call_target="tpu_custom_call" | custom-call | flops 1 | bytes 1 | tf_op jit(solution)/shard_map/pallas_call | solution.py:36
  34.6 2.0 bitcast_select_fusion
  36.6 1.1 constant_dynamic-slice_fusion
  37.7 1.5 collective-permute-start.18
  39.1 0.7 fusion.17
  39.9 1.5 collective-permute-start.22
  41.4 2.6 shard_map.57.refs_4_
  44.0 1.6 collective-permute-start.23
  46.8 31.5 %collective-permute-done.18 = bf16[1,128,4096]{2,1,0:T(8,128)(2,1)} collective-permute-done((bf16[1,128,4096]{2,1,0:T(8,128)(2,1)}, bf16[1,128,4096]{2,1,0:T(8,128)(2,1)}, u32[]{:S(2)}, u32[]{:S(2)}) %collective-permute-start.18) | collective-permute-done | bytes 1048608 | tf_op jit(solution)/shard_map/ppermute | solution.py:400
  78.3 1.1 select_bitcast_fusion
  79.4 11.1 %collective-permute-start.19 = (s32[3,16]{1,0:T(4,128)S(1)}, s32[3,16]{1,0:T(4,128)S(1)}, u32[]{:S(2)}, u32[]{:S(2)}) collective-permute-start(s32[3,16]{1,0:T(4,128)S(1)} %pad_add_fusion), channel_id=1, source_target_pairs={{0,8},{2,10},{4,12},{6,14},{8,0},{10,2},{12,4},{14,6},{16,24},{18,... | collective-permute-start | bytes 584 | tf_op jit(solution)/shard_map/ppermute | solution.py:366
  90.5 1.5 collective-permute-start.21
  92.0 7.6 %collective-permute-done.19 = s32[3,16]{1,0:T(4,128)S(1)} collective-permute-done((s32[3,16]{1,0:T(4,128)S(1)}, s32[3,16]{1,0:T(4,128)S(1)}, u32[]{:S(2)}, u32[]{:S(2)}) %collective-permute-start.19) | collective-permute-done | bytes 224 | tf_op jit(solution)/shard_map/ppermute | solution.py:366
  99.6 14.9 %collective-permute-done.20 = s32[3,16]{1,0:T(4,128)S(1)} collective-permute-done((s32[3,16]{1,0:T(4,128)S(1)}, s32[3,16]{1,0:T(4,128)S(1)}, u32[]{:S(2)}, u32[]{:S(2)}) %collective-permute-start.20) | collective-permute-done | bytes 224 | tf_op jit(solution)/shard_map/ppermute | solution.py:366
  114.5 0.9 collective-permute-done.21
  115.4 0.8 all-to-all-done
  116.3 4.5 %shard_map.58 = (f32[512,640]{1,0:T(8,128)S(1)}, bf16[512,512]{1,0:T(8,128)(2,1)S(1)}) custom-call(bf16[512,4096]{1,0:T(8,128)(2,1)} %bitcast.15.rows_ref.refs_0_, bf16[512,4096]{1,0:T(8,128)(2,1)} %copy-done.13), custom_call_target="tpu_custom_call" | custom-call | flops 1 | bytes 1 | tf_op jit(solution)/shard_map/pallas_call | solution.py:36
  120.8 1.1 copy-done.11
  121.9 1.5 collective-permute-start.26
  123.4 1.7 collective-permute-start.24
  125.1 10.4 %collective-permute-done.24 = bf16[32,4096]{1,0:T(8,128)(2,1)S(1)} collective-permute-done((bf16[32,4096]{1,0:T(8,128)(2,1)S(1)}, bf16[32,4096]{1,0:T(8,128)(2,1)S(1)}, u32[]{:S(2)}, u32[]{:S(2)}) %collective-permute-start.24) | collective-permute-done | bytes 262176 | tf_op jit(solution)/shard_map/ppermute | solution.py:411
  135.5 2.5 collective-permute-start.25
  138.0 0.8 copy-done.23
  138.8 9.3 %shard_map.59 = bf16[512,4096]{1,0:T(8,128)(2,1)} custom-call(bf16[512,4096]{1,0:T(8,128)(2,1)} %bitcast.15.rows_ref.refs_0_, bf16[512,4096]{1,0:T(8,128)(2,1)} %copy-done.13, f32[512,640]{1,0:T(8,128)} %copy-done.11, bf16[512,512]{1,0:T(8,128)(2,1)} %copy-done.23, f32[256,512]{1,0:T(8,128)} %copy-done.9, f32[256,512]{1,0:T(8,128)} %copy-done.22), custom_call_target="tpu_custom_call" | custom-call | flops 1 | bytes 1 | tf_op jit(solution)/shard_map/pallas_call | solution.py:36
  148.1 5.2 %all-to-all-start.1 = ((bf16[16,32,4096]{2,1,0:T(8,128)(2,1)}), bf16[16,32,4096]{2,1,0:T(8,128)(2,1)}, u32[]{:S(2)}, u32[]{:S(2)}) async-start(bf16[16,32,4096]{2,1,0:T(8,128)(2,1)} %bitcast.58), calls=%async_computation.1 | async-start | bytes 8388608 | tf_op jit(solution)/shard_map/all_to_all | solution.py:370
  153.3 0.7 fusion.10
  154.8 2.2 copy-done.4
  157.0 2.6 shard_map.61.refs_4_
  160.2 1.0 constant_dynamic-update-slice_fusion.2
  161.9 2.8 %shard_map.60 = (f32[128,640]{1,0:T(8,128)S(1)}, bf16[128,512]{1,0:T(8,128)(2,1)S(1)}) custom-call(bf16[128,4096]{1,0:T(8,128)(2,1)S(1)} %constant_dynamic-update-slice_fusion.rows_ref.refs_0_, bf16[512,4096]{1,0:T(8,128)(2,1)S(1)} %copy-done.5), custom_call_target="tpu_custom_call" | custom-call | flops 1 | bytes 1 | tf_op jit(solution)/shard_map/pallas_call | solution.py:36
  164.7 0.7 copy-done.12
  165.4 1.4 collective-permute-start.27
  166.9 1.4 convert_reduce_fusion.2
  171.5 4.9 %collective-permute-done.27.refs_3_ = bf16[128,512]{1,0:T(8,128)(2,1)S(1)} collective-permute-done((bf16[128,512]{1,0:T(8,128)(2,1)S(1)}, bf16[128,512]{1,0:T(8,128)(2,1)S(1)}, u32[]{:S(2)}, u32[]{:S(2)}) %collective-permute-start.27) | collective-permute-done | bytes 131104 | tf_op jit(solution)/shard_map/ppermute | solution.py:227
  176.4 0.8 copy-done.21
  177.2 5.4 %shard_map.62 = bf16[128,4096]{1,0:T(8,128)(2,1)S(1)} custom-call(bf16[128,4096]{1,0:T(8,128)(2,1)} %copy-done.7, bf16[512,4096]{1,0:T(8,128)(2,1)} %all-gather.2.cloned.1.call-done.weights_ref.refs_1_, f32[128,640]{1,0:T(8,128)} %copy-done.12, bf16[128,512]{1,0:T(8,128)(2,1)} %copy-done.26, f32[256,512]{1,0:T(8,128)} %copy-done.8, f32[256,512]{1,0:T(8,128)} %copy-done.21), custom_call_target="tpu_custom_call" | custom-call | flops 1 | bytes 1 | tf_op jit(solution)/shard_map/pallas_call | solution.py:36
  182.6 51.7 %conditional.1 = (bf16[32,4096]{1,0:T(8,128)(2,1)S(1)}) conditional(s32[]{:T(128)} %clamp.3, (s32[]{:T(128)}, bf16[128,4096]{1,0:T(8,128)(2,1)S(1)}) %tuple.47, (s32[]{:T(128)}, bf16[128,4096]{1,0:T(8,128)(2,1)S(1)}) %tuple.47, (s32[]{:T(128)}, bf16[128,4096]{1,0:T(8,128)(2,1)S(1)}) %tuple.47, (s32[]{:T(128)}, ...), branch_computations={%region_8.9_spmd, %region_9.10_spmd, %region_10.11_spmd, %region_1... | conditional | flops 524289 | bytes 6029450 | solution.py:461
  183.4 1.3 collective-permute-start.1
  185.4 48.9 %collective-permute-done.1 = bf16[32,4096]{1,0:T(8,128)(2,1)S(1)} collective-permute-done((bf16[32,4096]{1,0:T(8,128)(2,1)S(1)}, bf16[32,4096]{1,0:T(8,128)(2,1)S(1)}, u32[]{:S(2)}, u32[]{:S(2)}) %collective-permute-start.1) | collective-permute-done | bytes 262176 | tf_op jit(solution)/shard_map/cond/branch_0_fun/ppermute | solution.py:455
  234.3 23.0 %all-to-all-done.1 = bf16[16,32,4096]{2,1,0:T(8,128)(2,1)} async-done(((bf16[16,32,4096]{2,1,0:T(8,128)(2,1)}), bf16[16,32,4096]{2,1,0:T(8,128)(2,1)}, u32[]{:S(2)}, u32[]{:S(2)}) %all-to-all-start.1) | async-done | bytes 4194336 | tf_op jit(solution)/shard_map/all_to_all | solution.py:370
  257.2 6.1 %shard_map.63 = bf16[512,4096]{1,0:T(8,128)(2,1)} custom-call(s32[512,1]{1,0:T(8,128)S(1)} %copy.18.refs_0_, s32[512,1]{1,0:T(8,128)S(1)} %copy.19.refs_1_, bf16[512,4096]{1,0:T(8,128)(2,1)} %bitcast.20.refs_2_, bf16[32,4096]{1,0:T(8,128)(2,1)S(1)} %get-tuple-element.450.refs_3_), custom_call_target="tpu_custom_call" | custom-call | flops 1 | bytes 1 | tf_op jit(solution)/shard_map/pallas_call | solution.py:36
  263.3 0.9 while.13
  (79 shorter events, 7.8 us)
Async XLA Ops:
  8.3 8.7 %collective-permute-start.14 = (s32[2,16]{1,0:T(2,128)S(1)}, s32[2,16]{1,0:T(2,128)S(1)}, u32[]{:S(2)}, u32[]{:S(2)}) collective-permute-start(s32[2,16]{1,0:T(2,128)S(1)} %pad_add_fusion.1), channel_id=1, source_target_pairs={{0,2},{2,0},{4,6},{6,4},{8,10},{10,8},{12,14},{14,12},{16,18},{18,... | collective-permute-start | bytes 392 | tf_op jit(solution)/shard_map/ppermute | solution.py:366
  8.4 8.7 %collective-permute-start.15 = (s32[2,16]{1,0:T(2,128)S(1)}, s32[2,16]{1,0:T(2,128)S(1)}, u32[]{:S(2)}, u32[]{:S(2)}) collective-permute-start(s32[2,16]{1,0:T(2,128)S(1)} %pad_add_fusion.1), channel_id=1, source_target_pairs={{0,4},{2,6},{4,0},{6,2},{8,12},{10,14},{12,8},{14,10},{16,20},{18,... | collective-permute-start | bytes 392 | tf_op jit(solution)/shard_map/ppermute | solution.py:366
  9.9 7.1 %collective-permute-start.16 = (s32[2,16]{1,0:T(2,128)S(1)}, s32[2,16]{1,0:T(2,128)S(1)}, u32[]{:S(2)}, u32[]{:S(2)}) collective-permute-start(s32[2,16]{1,0:T(2,128)S(1)} %pad_add_fusion.1), channel_id=1, source_target_pairs={{0,6},{2,4},{4,2},{6,0},{8,14},{10,12},{12,10},{14,8},{16,22},{18,... | collective-permute-start | bytes 392 | tf_op jit(solution)/shard_map/ppermute | solution.py:366
  17.1 6.6 %copy-start.19 = (bf16[1,4,64,4096]{3,2,1,0:T(8,128)(2,1)S(1)}, bf16[1,4,64,4096]{3,2,1,0:T(8,128)(2,1)}, u32[]{:S(2)}) copy-start(bf16[1,4,64,4096]{3,2,1,0:T(8,128)(2,1)} %param.15) | copy-start | bytes 6291460
  17.1 99.2 %all-to-all-start = ((bf16[16,32,4096]{2,1,0:T(8,128)(2,1)}), bf16[16,32,4096]{2,1,0:T(8,128)(2,1)}, u32[]{:S(2)}, u32[]{:S(2)}) async-start(bf16[16,32,4096]{2,1,0:T(8,128)(2,1)} %bitcast.57), calls=%async_computation | async-start | bytes 8388608 | tf_op jit(solution)/shard_map/all_to_all | solution.py:370
  23.4 131.4 %all-gather.2.cloned.1.call-start = ((), (), s32[]{:S(2)}) async-start(), calls=%async_computation.2 | async-start | bytes 5242880 | tf_op jit(solution)/shard_map/all_gather | solution.py:426
  25.6 2.0 copy-start.13
  27.7 6.9 %collective-permute-start.17 = (bf16[2,128,4096]{2,1,0:T(8,128)(2,1)S(1)}, bf16[2,128,4096]{2,1,0:T(8,128)(2,1)}, u32[]{:S(2)}, u32[]{:S(2)}) collective-permute-start(bf16[2,128,4096]{2,1,0:T(8,128)(2,1)S(1)} %dynamic-slice_bitcast_fusion), channel_id=1, source_target_pairs={{0,2},{2,0},{4,6},{6,4},{8,10},{10,8},{12,14},{14,12},{16,18},{18,... | collective-permute-start | bytes 6291464 | tf_op jit(solution)/shard_map/ppermute | solution.py:400
  34.6 4.5 %copy-start.18 = (bf16[64,4096]{1,0:T(8,128)(2,1)S(1)}, bf16[64,4096]{1,0:T(8,128)(2,1)}, u32[]{:S(2)}) copy-start(bf16[64,4096]{1,0:T(8,128)(2,1)} %shard_map.56) | copy-start | bytes 1572868
  34.6 6.7 %copy-start.14 = (bf16[512,4096]{1,0:T(8,128)(2,1)S(1)}, bf16[512,4096]{1,0:T(8,128)(2,1)}, u32[]{:S(2)}) copy-start(bf16[512,4096]{1,0:T(8,128)(2,1)} %copy-done.13) | copy-start | bytes 12582916
  37.7 40.6 %collective-permute-start.18 = (bf16[1,128,4096]{2,1,0:T(8,128)(2,1)}, bf16[1,128,4096]{2,1,0:T(8,128)(2,1)}, u32[]{:S(2)}, u32[]{:S(2)}) collective-permute-start(bf16[1,128,4096]{2,1,0:T(8,128)(2,1)} %constant_dynamic-slice_fusion), channel_id=1, source_target_pairs={{0,4},{2,6},{4,0},{6,2},{8,12},{10,14},{12,8},{14,10},{16,20},{18,... | collective-permute-start | bytes 3145736 | tf_op jit(solution)/shard_map/ppermute | solution.py:400
  39.9 75.5 %collective-permute-start.22 = (bf16[32,4096]{1,0:T(8,128)(2,1)S(1)}, bf16[32,4096]{1,0:T(8,128)(2,1)}, u32[]{:S(2)}, u32[]{:S(2)}) collective-permute-start(bf16[32,4096]{1,0:T(8,128)(2,1)S(1)} %get-tuple-element.244), channel_id=1, source_target_pairs={{0,8},{2,10},{4,12},{6,14},{8,0},{10,2},{12,4},{14,6},{16,24},{18,... | collective-permute-start | bytes 786440 | tf_op jit(solution)/shard_map/ppermute | solution.py:411
  43.9 76.9 %copy-start.9 = (f32[256,512]{1,0:T(8,128)}, f32[256,512]{1,0:T(8,128)S(1)}, u32[]{:S(2)}) copy-start(f32[256,512]{1,0:T(8,128)S(1)} %shard_map.57.refs_4_) | copy-start | bytes 1572868
  44.0 71.5 %collective-permute-start.23 = (f32[256,512]{1,0:T(8,128)S(1)}, f32[256,512]{1,0:T(8,128)S(1)}, u32[]{:S(2)}, u32[]{:S(2)}) collective-permute-start(f32[256,512]{1,0:T(8,128)S(1)} %shard_map.57.refs_4_), channel_id=1, source_target_pairs={{0,1},{1,0},{2,3},{3,2},{4,5},{5,4},{6,7},{7,6},{8,9},{9,8},{10,11... | collective-permute-start | bytes 1572872 | tf_op jit(solution)/shard_map/ppermute | solution.py:19
  79.4 20.2 %collective-permute-start.19 = (s32[3,16]{1,0:T(4,128)S(1)}, s32[3,16]{1,0:T(4,128)S(1)}, u32[]{:S(2)}, u32[]{:S(2)}) collective-permute-start(s32[3,16]{1,0:T(4,128)S(1)} %pad_add_fusion), channel_id=1, source_target_pairs={{0,8},{2,10},{4,12},{6,14},{8,0},{10,2},{12,4},{14,6},{16,24},{18,... | collective-permute-start | bytes 584 | tf_op jit(solution)/shard_map/ppermute | solution.py:366
  90.5 23.9 %collective-permute-start.20 = (s32[3,16]{1,0:T(4,128)S(1)}, s32[3,16]{1,0:T(4,128)S(1)}, u32[]{:S(2)}, u32[]{:S(2)}) collective-permute-start(s32[3,16]{1,0:T(4,128)S(1)} %pad_add_fusion), channel_id=1, source_target_pairs={{0,16},{2,18},{4,20},{6,22},{8,24},{10,26},{12,28},{14,30},{16,0},... | collective-permute-start | bytes 584 | tf_op jit(solution)/shard_map/ppermute | solution.py:366
  90.5 24.9 %collective-permute-start.21 = (s32[3,16]{1,0:T(4,128)S(1)}, s32[3,16]{1,0:T(4,128)S(1)}, u32[]{:S(2)}, u32[]{:S(2)}) collective-permute-start(s32[3,16]{1,0:T(4,128)S(1)} %pad_add_fusion), channel_id=1, source_target_pairs={{0,24},{2,26},{4,28},{6,30},{8,16},{10,18},{12,20},{14,22},{16,8},... | collective-permute-start | bytes 584 | tf_op jit(solution)/shard_map/ppermute | solution.py:366
  115.4 5.4 %copy-start.22 = (f32[256,512]{1,0:T(8,128)}, f32[256,512]{1,0:T(8,128)S(1)}, u32[]{:S(2)}) copy-start(f32[256,512]{1,0:T(8,128)S(1)} %collective-permute-done.23.refs_5_) | copy-start | bytes 1572868
  116.3 7.1 %copy-start.25 = (bf16[32,4096]{1,0:T(8,128)(2,1)S(1)}, bf16[32,4096]{1,0:T(8,128)(2,1)}, u32[]{:S(2)}) copy-start(bf16[32,4096]{1,0:T(8,128)(2,1)} %get-tuple-element.233) | copy-start | bytes 786436
  120.8 1.1 copy-start.11
  121.9 16.0 %collective-permute-start.26 = (bf16[512,512]{1,0:T(8,128)(2,1)S(1)}, bf16[512,512]{1,0:T(8,128)(2,1)S(1)}, u32[]{:S(2)}, u32[]{:S(2)}) collective-permute-start(bf16[512,512]{1,0:T(8,128)(2,1)S(1)} %get-tuple-element.238), channel_id=1, source_target_pairs={{0,1},{1,0},{2,3},{3,2},{4,5},{5,4},{6,7},{7,6},{8,9},{9,8},{10,11... | collective-permute-start | bytes 1572872 | tf_op jit(solution)/shard_map/ppermute | solution.py:227
  123.4 12.0 %collective-permute-start.24 = (bf16[32,4096]{1,0:T(8,128)(2,1)S(1)}, bf16[32,4096]{1,0:T(8,128)(2,1)S(1)}, u32[]{:S(2)}, u32[]{:S(2)}) collective-permute-start(bf16[32,4096]{1,0:T(8,128)(2,1)S(1)} %copy-done.25), channel_id=1, source_target_pairs={{0,16},{2,18},{4,20},{6,22},{8,24},{10,26},{12,28},{14,30},{16,0},... | collective-permute-start | bytes 786440 | tf_op jit(solution)/shard_map/ppermute | solution.py:411
  135.5 12.6 %collective-permute-start.25 = (bf16[32,4096]{1,0:T(8,128)(2,1)S(1)}, bf16[32,4096]{1,0:T(8,128)(2,1)S(1)}, u32[]{:S(2)}, u32[]{:S(2)}) collective-permute-start(bf16[32,4096]{1,0:T(8,128)(2,1)S(1)} %collective-permute-done.24), channel_id=1, source_target_pairs={{0,8},{2,10},{4,12},{6,14},{8,0},{10,2},{12,4},{14,6},{16,24},{18,... | collective-permute-start | bytes 786440 | tf_op jit(solution)/shard_map/ppermute | solution.py:411
  138.0 0.8 copy-start.23
  148.1 109.1 %all-to-all-start.1 = ((bf16[16,32,4096]{2,1,0:T(8,128)(2,1)}), bf16[16,32,4096]{2,1,0:T(8,128)(2,1)}, u32[]{:S(2)}, u32[]{:S(2)}) async-start(bf16[16,32,4096]{2,1,0:T(8,128)(2,1)} %bitcast.58), calls=%async_computation.1 | async-start | bytes 8388608 | tf_op jit(solution)/shard_map/all_to_all | solution.py:370
  154.8 2.2 copy-start.4
  157.0 5.0 %copy-start.5 = (bf16[512,4096]{1,0:T(8,128)(2,1)S(1)}, bf16[512,4096]{1,0:T(8,128)(2,1)}, u32[]{:S(2)}) copy-start(bf16[512,4096]{1,0:T(8,128)(2,1)} %all-gather.2.cloned.1.call-done.weights_ref.refs_1_) | copy-start | bytes 12582916
  159.5 17.7 %copy-start.8 = (f32[256,512]{1,0:T(8,128)}, f32[256,512]{1,0:T(8,128)S(1)}, u32[]{:S(2)}) copy-start(f32[256,512]{1,0:T(8,128)S(1)} %shard_map.61.refs_4_) | copy-start | bytes 1572868
  159.5 16.9 %collective-permute-start.28 = (f32[256,512]{1,0:T(8,128)S(1)}, f32[256,512]{1,0:T(8,128)S(1)}, u32[]{:S(2)}, u32[]{:S(2)}) collective-permute-start(f32[256,512]{1,0:T(8,128)S(1)} %shard_map.61.refs_4_), channel_id=1, source_target_pairs={{0,1},{1,0},{2,3},{3,2},{4,5},{5,4},{6,7},{7,6},{8,9},{9,8},{10,11... | collective-permute-start | bytes 1572872 | tf_op jit(solution)/shard_map/ppermute | solution.py:19
  161.2 16.0 %copy-start.7 = (bf16[128,4096]{1,0:T(8,128)(2,1)}, bf16[128,4096]{1,0:T(8,128)(2,1)S(1)}, u32[]{:S(2)}) copy-start(bf16[128,4096]{1,0:T(8,128)(2,1)S(1)} %constant_dynamic-update-slice_fusion.rows_ref.refs_0_) | copy-start | bytes 3145732
  164.7 0.7 copy-start.12
  165.4 10.9 %collective-permute-start.27 = (bf16[128,512]{1,0:T(8,128)(2,1)S(1)}, bf16[128,512]{1,0:T(8,128)(2,1)S(1)}, u32[]{:S(2)}, u32[]{:S(2)}) collective-permute-start(bf16[128,512]{1,0:T(8,128)(2,1)S(1)} %get-tuple-element.250), channel_id=1, source_target_pairs={{0,1},{1,0},{2,3},{3,2},{4,5},{5,4},{6,7},{7,6},{8,9},{9,8},{10,11... | collective-permute-start | bytes 393224 | tf_op jit(solution)/shard_map/ppermute | solution.py:227
  176.4 0.8 copy-start.26
  176.4 0.8 copy-start.21
  182.7 2.7 collective-permute-start
  183.4 50.9 %collective-permute-start.1 = (bf16[32,4096]{1,0:T(8,128)(2,1)S(1)}, bf16[32,4096]{1,0:T(8,128)(2,1)S(1)}, u32[]{:S(2)}, u32[]{:S(2)}) collective-permute-start(bf16[32,4096]{1,0:T(8,128)(2,1)S(1)} %get-tuple-element.311), channel_id=1, source_target_pairs={{0,16},{2,18},{4,20},{6,22},{1,17},{3,19},{5,21},{7,23}} | collective-permute-start | bytes 786440 | tf_op jit(solution)/shard_map/cond/branch_0_fun/ppermute | solution.py:455
  184.7 49.6 %collective-permute-start.2 = (bf16[32,4096]{1,0:T(8,128)(2,1)S(1)}, bf16[32,4096]{1,0:T(8,128)(2,1)S(1)}, u32[]{:S(2)}, u32[]{:S(2)}) collective-permute-start(bf16[32,4096]{1,0:T(8,128)(2,1)S(1)} %get-tuple-element.310), channel_id=1, source_target_pairs={{0,24},{2,26},{4,28},{6,30},{1,25},{3,27},{5,29},{7,31}} | collective-permute-start | bytes 786440 | tf_op jit(solution)/shard_map/cond/branch_0_fun/ppermute | solution.py:455
Sparse Core Ops, SparseCore 0:
  116.4 34.4 all-gather.1
